TPU v7x, 256 devices: a whole 4x4x8 slice. The times are simulated.
256 devices in a mesh: loop: 64 (over z, x_lo, y), tp: 4 (over x_hi, core).
Axes of the slice: x: 4 (x_hi: 2, x_lo: 2; x = x_hi * 2 + x_lo), y: 4, z: 8, core: 2. Of those that a mesh axis runs over, the one named last changes fastest.
Arguments:
- tokens: bfloat16 [32768, 5120], P('loop', 'tp'), may hold values from -6 to 6
- weights: float32 [64, 5120, 1024], P('loop', 'tp'), may hold values from -6 to 6
- gain: float32 [64, 128], P('loop'), may hold values from 0.5 to 1.5
- cotangent: bfloat16 [32768, 1024], P('loop'), may hold values from -6 to 6
- vectors: float32 [64, 4, 1024], P('loop'), may hold values from -6 to 6
Outputs:
- new_weights: float32 [64, 5120, 1024], P('loop', 'tp')
- input_grad: bfloat16 [32768, 5120], P('loop', 'tp')
- new_gain: float32 [64, 128], P('loop')
- new_vectors: float32 [64, 4, 1024], P('loop')
All inputs are finite; a program needn't handle non-finite values.
Results may differ from a plain program's by a relative error of at most 0.011.
Values may be sent and summed in bfloat16 or wider, within the bound.
No kernel may reach another device: no remote copies, remote signals or barrier semaphores. Data moves between devices by JAX's collectives and lax.ppermute only.
A program may use at most 128 MiB of HBM per device.

v0:
```python
import jax
import jax.numpy as jnp
from jax import lax
from jax.sharding import PartitionSpec as P

D = 5120


HIGH = lax.Precision.HIGHEST


def passed_along(x, axis, by):
    length = lax.axis_size(axis)
    return lax.ppermute(x, axis, [(i, (i + by) % length) for i in range(length)])


def lower_solve(lower, rhs):
    return lax.linalg.triangular_solve(lower, rhs, left_side=True, lower=True)


def norm_back(keys, gain, upstream):
    rows = keys.shape[0]
    split = keys.reshape(rows, -1, gain.shape[0])
    inv = lax.rsqrt(jnp.mean(split * split, axis=-1, keepdims=True) + 1e-06)
    unit = split * inv
    grad_up = upstream.astype(jnp.float32).reshape(split.shape)
    gain_grad = jnp.sum(grad_up * unit, axis=(0, 1))
    scaled = grad_up * gain
    key_grad = inv * (scaled - unit * jnp.mean(scaled * unit, axis=-1, keepdims=True))
    return (key_grad.reshape(rows, -1), gain_grad)


def contract_rank(left, right):
    return lax.dot_general(left, right, (((0,), (0,)), ((), ())), precision=HIGH)


def shards(tokens, weights, gain, cotangent, vectors):
    scale = D ** (-0.5)
    weight_now = weights[0]
    gain_now = gain[0]
    wb = weight_now.astype(jnp.bfloat16)
    partial_keys = jnp.dot(tokens, wb, preferred_element_type=jnp.float32) * scale
    keys = lax.psum(partial_keys, "tp")
    key_grad, gain_grad = norm_back(keys, gain_now, cotangent)
    kgb = key_grad.astype(jnp.bfloat16)
    input_sum = lax.dot_general(
        kgb, wb, (((1,), (1,)), ((), ())), preferred_element_type=jnp.float32
    )
    weight_sum = lax.dot_general(
        tokens, kgb, (((0,), (0,)), ((), ())), preferred_element_type=jnp.float32
    )
    input_grad = (input_sum * scale).astype(jnp.bfloat16)
    stepped = weight_now - 0.1 * (weight_sum * scale)
    new_gain = gain_now - 0.002 * gain_grad
    right_vec = vectors[0]
    left_vec = passed_along(vectors, "loop", 1)[0]
    proj_right = lax.dot_general(right_vec, stepped, (((1,), (1,)), ((), ())), precision=HIGH)
    proj_left = lax.dot_general(left_vec, stepped, (((1,), (1,)), ((), ())), precision=HIGH)
    recv_right = passed_along(proj_left, "loop", -1)
    recv_left = passed_along(proj_right, "loop", 1)
    rows_right = proj_right - recv_right
    rows_left = proj_left - recv_left
    gram_right = jnp.dot(rows_right, rows_right.T, precision=HIGH)
    gram_left = jnp.dot(rows_left, rows_left.T, precision=HIGH)
    gram_right, gram_left = lax.psum((gram_right, gram_left), "tp")
    lower_right = jnp.linalg.cholesky(gram_right)
    lower_left = jnp.linalg.cholesky(gram_left)
    unit_right = lower_solve(lower_right, rows_right)
    unit_left = lower_solve(lower_left, rows_left)
    source_right, source_left = (unit_right, unit_left)
    back_right_own = jnp.dot(source_right, stepped, precision=HIGH)
    back_left_own = jnp.dot(source_left, stepped, precision=HIGH)
    got_right = passed_along(back_left_own, "loop", -1)
    got_left = passed_along(back_right_own, "loop", 1)
    sum_right = back_right_own + got_right
    sum_left = back_left_own + got_left
    next_right, next_left = (
        lax.psum(sum_right.astype(jnp.bfloat16), "tp").astype(jnp.float32),
        lax.psum(sum_left.astype(jnp.bfloat16), "tp").astype(jnp.float32),
    )
    mixing = contract_rank(unit_right, next_right) + contract_rank(unit_left, next_left)
    new_weights = stepped - 1.0 / 3.0 * mixing
    return (new_weights[None], input_grad, new_gain[None], next_right[None])


def solution(mesh):
    return jax.shard_map(
        shards,
        mesh=mesh,
        in_specs=(
            P("loop", "tp"),
            P("loop", "tp", None),
            P("loop", None),
            P("loop", None),
            P("loop", None, None),
        ),
        out_specs=(P("loop", "tp", None), P("loop", "tp"), P("loop", None), P("loop", None, None)),
        check_vma=False,
    )
```

profile of v0, /device:TPU:1, one launch (start us, length us, event | category | flops | bytes accessed | tf_op | source)
XLA Modules:
  0.0 185.9 jit_solution(11871572251523952522)
XLA Ops:
  7.2 6.0 %copy.19 = f32[1,1280,1024]{1,2,0:T(8,128)} copy(f32[1,1280,1024]{2,1,0:T(8,128)} %param.9) | data formatting | bytes 10485760 | tf_op args[1]
  13.2 5.3 %convolution_multiply_fusion.1 = f32[512,1024]{1,0:T(8,128)} fusion(bf16[512,1280]{1,0:T(8,128)(2,1)S(1)} %copy-done, f32[1,1280,1024]{1,2,0:T(8,128)} %copy.19), kind=kOutput, calls=%fused_computation.19 | convolution fusion | flops 1342701568 | bytes 8650752 | tf_op jit(solution)/shard_map/dot_general | solution.py:42
  18.6 0.7 copy-done.6
  19.3 2.1 %collective-permute-start = (f32[1,4,1024]{2,1,0:T(4,128)S(1)}, f32[1,4,1024]{2,1,0:T(4,128)S(1)}, u32[]{:S(2)}, u32[]{:S(2)}) collective-permute-start(f32[1,4,1024]{2,1,0:T(4,128)S(1)} %copy-done.6), channel_id=1, source_target_pairs={{0,4},{4,8},{8,12},{12,16},{16,20},{20,24},{24,28},{28,32},{32,36}... | collective-permute-start | bytes 49160 | tf_op jit(solution)/shard_map/ppermute | solution.py:14
  21.4 0.2 convert_bitcast_fusion
  21.7 0.5 copy.35
  22.1 0.2 copy-done.7
  22.4 64.4 %all-reduce.4.cloned.1.call-done = f32[512,1024]{1,0:T(8,128)} async-done(((f32[512,1024]{1,0:T(8,128)}), f32[512,1024]{1,0:T(8,128)}) %all-reduce.4.cloned.1.call-update) | async-done | bytes 2097168 | tf_op jit(solution)/shard_map/psum | solution.py:43
  86.9 2.1 %copy.33 = f32[64,8,8,128]{3,2,1,0:T(8,128)S(1)} copy(f32[64,8,8,128]{3,1,2,0:T(8,128)} %bitcast.112) | data formatting | bytes 4194304
  88.9 0.6 multiply_reduce_fusion.1
  89.6 1.6 multiply_reduce_fusion
  91.3 0.6 mul.121
  91.9 0.6 mul.109
  92.5 0.4 copy-done.3
  92.9 0.3 copy-done.5
  93.1 1.5 fusion.4
  94.6 0.2 slice-done.1
  94.8 2.6 %fusion = bf16[512,1280]{1,0:T(8,128)(2,1)} fusion(bf16[512,1024]{1,0:T(8,128)(2,1)S(1)} %get-tuple-element.19, f32[1,1280,1024]{1,2,0:T(8,128)S(1)} %bitcast.109), kind=kOutput, calls=%fused_computation.7 | convolution fusion | flops 1343488000 | bytes 7602176 | tf_op jit(solution)/shard_map/dot_general | solution.py:46
  97.4 1.6 bitcast_subtract_fusion
  99.0 2.8 %convolution_bitcast_fusion.1 = f32[4,1280]{1,0:T(4,128)S(1)} fusion(f32[1280,1024]{0,1:T(8,128)S(1)} %bitcast_subtract_fusion, f32[1,4,1024]{2,1,0:T(4,128)S(1)} %copy-done.6), kind=kOutput, calls=%fused_computation.9 | convolution fusion | flops 62914560 | bytes 5279744 | tf_op jit(solution)/shard_map/dot_general | solution.py:57
  101.8 1.5 collective-permute-start.2
  103.3 5.6 %collective-permute-done.2 = f32[4,1280]{1,0:T(4,128)S(1)} collective-permute-done((f32[4,1280]{1,0:T(4,128)S(1)}, f32[4,1280]{1,0:T(4,128)S(1)}, u32[]{:S(2)}, u32[]{:S(2)}) %collective-permute-start.2) | collective-permute-done | bytes 20512 | tf_op jit(solution)/shard_map/ppermute | solution.py:14
  109.0 2.8 %fusion.17 = (f32[4,1280]{1,0:T(4,128)S(1)}, f32[4,1280]{1,0:T(4,128)S(1)}) fusion(f32[4,1280]{1,0:T(4,128)S(1)} %collective-permute-done.2, f32[1280,1024]{0,1:T(8,128)S(1)} %bitcast_subtract_fusion, f32[1,4,1024]{2,1,0:T(4,128)S(1)} %collective-permute-done), kind=kOutput, calls=%fused_computation.48 | convolution fusion | flops 62919680 | bytes 5320704 | tf_op jit(solution)/shard_map/dot_general | solution.py:58
  111.8 1.1 collective-permute-start.1
  113.0 1.5 collective-permute-done.1
  114.5 0.2 fusion.22
  114.6 9.2 %all-reduce = (f32[4,4]{0,1:T(4,128)S(1)}, f32[4,4]{0,1:T(4,128)S(1)}) all-reduce(f32[4,4]{0,1:T(4,128)S(1)} %fusion.24, f32[4,4]{0,1:T(4,128)S(1)} %fusion.22), channel_id=1, replica_groups=mesh['loop'=64,'tp'=4] {'tp'}, use_global_device_ids=true, to_apply=%region_6.9 | all-reduce | flops 32 | bytes 256 | tf_op jit(solution)/shard_map/psum | solution.py:65
  124.0 0.4 cholesky.55
  124.4 0.6 compare_reduce_fusion
  125.0 0.6 fusion.8
  125.7 0.3 custom-call.7
  126.0 0.4 cholesky.44
  126.4 0.6 compare_reduce_fusion.1
  127.1 0.6 fusion.7
  127.7 0.3 custom-call.6
  128.1 0.2 fusion.11
  128.3 6.9 %fusion.23 = f32[4,1024]{1,0:T(4,128)S(1)} fusion(f32[4,1280]{1,0:T(4,128)S(1)} %fusion.11, f32[1280,1024]{0,1:T(8,128)} %copy-done.1), kind=kOutput, calls=%fused_computation.52 | convolution fusion | flops 62914560 | bytes 5279744 | tf_op jit(solution)/shard_map/dot_general | solution.py:71
  135.3 0.3 fusion.9
  135.5 6.6 %collective-permute-done.4 = f32[4,1024]{1,0:T(4,128)S(1)} collective-permute-done((f32[4,1024]{1,0:T(4,128)S(1)}, f32[4,1024]{1,0:T(4,128)S(1)}, u32[]{:S(2)}, u32[]{:S(2)}) %collective-permute-start.4) | collective-permute-done | bytes 16416 | tf_op jit(solution)/shard_map/ppermute | solution.py:14
  142.1 4.4 %add_convert_fusion = (bf16[4,1024]{1,0:T(4,128)(2,1)S(1)}, f32[4,1024]{1,0:T(4,128)S(1)}) fusion(f32[4,1024]{1,0:T(4,128)S(1)} %collective-permute-done.4, f32[4,1280]{1,0:T(4,128)S(1)} %fusion.9, f32[1280,1024]{0,1:T(8,128)S(1)} %copy-done.2), kind=kOutput, calls=%fused_computation.24 | convolution fusion | flops 62922752 | bytes 5304320 | tf_op jit(solution)/shard_map/dot_general | solution.py:72
  146.5 1.2 collective-permute-start.3
  147.7 0.5 bitcast_subtract_fusion.1
  148.2 1.1 collective-permute-done.3
  149.3 13.2 %all-reduce.1 = (bf16[4,1024]{1,0:T(4,128)(2,1)S(1)}, bf16[4,1024]{1,0:T(4,128)(2,1)S(1)}) all-reduce(bf16[4,1024]{1,0:T(4,128)(2,1)S(1)} %get-tuple-element.22, bf16[4,1024]{1,0:T(4,128)(2,1)S(1)} %add_convert_fusion.1), channel_id=1, replica_groups=mesh['loop'=64,'tp'=4] {'tp'}, use_global_device_ids=true, to_apply=%region_8.11 | all-reduce | flops 8192 | bytes 32768 | tf_op jit(solution)/shard_map/psum | solution.py:79
  162.6 0.6 bitcast_convert_fusion.3
  163.2 2.3 %fusion.25 = f32[1280,1024]{0,1:T(8,128)S(1)} fusion(f32[4,1280]{1,0:T(4,128)S(1)} %fusion.9, bf16[4,1024]{1,0:T(4,128)(2,1)S(1)} %get-tuple-element.16), kind=kOutput, calls=%fused_computation.54 | convolution fusion | flops 62914560 | bytes 5271552 | tf_op jit(solution)/shard_map/dot_general | solution.py:34
  165.5 7.7 %subtract_bitcast_fusion = f32[1,1280,1024]{1,2,0:T(8,128)} fusion(f32[1280,1024]{0,1:T(8,128)} %copy-done.1, f32[1280,1024]{0,1:T(8,128)S(1)} %fusion.25, f32[4,1280]{1,0:T(4,128)S(1)} %fusion.11, bf16[4,1024]{1,0:T(4,128)(2,1)S(1)} %get-tuple-element.17), kind=kOutput, calls=%fused_computation.2 | convolution fusion | flops 66846720 | bytes 15757312 | tf_op jit(solution)/shard_map/dot_general | solution.py:34
  173.2 5.9 %copy.28 = f32[1,1280,1024]{2,1,0:T(8,128)} copy(f32[1,1280,1024]{1,2,0:T(8,128)} %subtract_bitcast_fusion) | data formatting | bytes 10485760
  (33 shorter events, 0.8 us)
Async XLA Ops:
  7.2 6.0 %copy-start = (bf16[512,1280]{1,0:T(8,128)(2,1)S(1)}, bf16[512,1280]{1,0:T(8,128)(2,1)}, u32[]{:S(2)}) copy-start(bf16[512,1280]{1,0:T(8,128)(2,1)} %param.8) | copy-start | bytes 3932164
  7.2 79.7 %all-reduce.4.cloned.1.call-start = ((), (), s32[]{:S(2)}) async-start(), calls=%async_computation | async-start | bytes 4194304 | tf_op jit(solution)/shard_map/psum | solution.py:43
  18.5 0.7 copy-start.6
  18.5 2.8 %copy-start.4 = (bf16[512,1024]{1,0:T(8,128)(2,1)S(1)}, bf16[512,1024]{1,0:T(8,128)(2,1)}, u32[]{:S(2)}) copy-start(bf16[512,1024]{1,0:T(8,128)(2,1)} %param.11) | copy-start | bytes 3145732
  19.3 84.1 %collective-permute-start = (f32[1,4,1024]{2,1,0:T(4,128)S(1)}, f32[1,4,1024]{2,1,0:T(4,128)S(1)}, u32[]{:S(2)}, u32[]{:S(2)}) collective-permute-start(f32[1,4,1024]{2,1,0:T(4,128)S(1)} %copy-done.6), channel_id=1, source_target_pairs={{0,4},{4,8},{8,12},{12,16},{16,20},{20,24},{24,28},{28,32},{32,36}... | collective-permute-start | bytes 49160 | tf_op jit(solution)/shard_map/ppermute | solution.py:14
  21.6 0.7 copy-start.7
  91.3 1.6 copy-start.3
  91.3 1.8 copy-start.5
  91.9 2.7 %slice-start = ((s8[5242880]{0:T(1024)(128)(4,1)}), s8[4194304]{0:T(1024)(128)(4,1)S(1)}, s32[]{:S(2)}) async-start(s8[5242880]{0:T(1024)(128)(4,1)} %bitcast.108), calls=%async_computation.1 | async-start | bytes 8388608
  93.1 1.7 slice-start.1
  99.0 9.9 %copy-start.1 = (f32[1280,1024]{0,1:T(8,128)}, f32[1280,1024]{0,1:T(8,128)S(1)}, u32[]{:S(2)}) copy-start(f32[1280,1024]{0,1:T(8,128)S(1)} %bitcast_subtract_fusion) | copy-start | bytes 15728644
  101.8 7.2 %collective-permute-start.2 = (f32[4,1280]{1,0:T(4,128)S(1)}, f32[4,1280]{1,0:T(4,128)S(1)}, u32[]{:S(2)}, u32[]{:S(2)}) collective-permute-start(f32[4,1280]{1,0:T(4,128)S(1)} %convolution_bitcast_fusion.1), channel_id=1, source_target_pairs={{0,4},{4,8},{8,12},{12,16},{16,20},{20,24},{24,28},{28,32},{32,36}... | collective-permute-start | bytes 61448 | tf_op jit(solution)/shard_map/ppermute | solution.py:14
  111.8 2.7 %collective-permute-start.1 = (f32[4,1280]{1,0:T(4,128)S(1)}, f32[4,1280]{1,0:T(4,128)S(1)}, u32[]{:S(2)}, u32[]{:S(2)}) collective-permute-start(f32[4,1280]{1,0:T(4,128)S(1)} %get-tuple-element.21), channel_id=1, source_target_pairs={{0,252},{4,0},{8,4},{12,8},{16,12},{20,16},{24,20},{28,24},{32,28}... | collective-permute-start | bytes 61448 | tf_op jit(solution)/shard_map/ppermute | solution.py:14
  128.3 13.8 %copy-start.2 = (f32[1280,1024]{0,1:T(8,128)S(1)}, f32[1280,1024]{0,1:T(8,128)}, u32[]{:S(2)}) copy-start(f32[1280,1024]{0,1:T(8,128)} %copy-done.1) | copy-start | bytes 15728644
  135.3 6.8 %collective-permute-start.4 = (f32[4,1024]{1,0:T(4,128)S(1)}, f32[4,1024]{1,0:T(4,128)S(1)}, u32[]{:S(2)}, u32[]{:S(2)}) collective-permute-start(f32[4,1024]{1,0:T(4,128)S(1)} %fusion.23), channel_id=1, source_target_pairs={{0,4},{4,8},{8,12},{12,16},{16,20},{20,24},{24,28},{28,32},{32,36}... | collective-permute-start | bytes 49160 | tf_op jit(solution)/shard_map/ppermute | solution.py:14
  146.5 2.8 %collective-permute-start.3 = (f32[4,1024]{1,0:T(4,128)S(1)}, f32[4,1024]{1,0:T(4,128)S(1)}, u32[]{:S(2)}, u32[]{:S(2)}) collective-permute-start(f32[4,1024]{1,0:T(4,128)S(1)} %get-tuple-element.23), channel_id=1, source_target_pairs={{0,252},{4,0},{8,4},{12,8},{16,12},{20,16},{24,20},{28,24},{32,28}... | collective-permute-start | bytes 49160 | tf_op jit(solution)/shard_map/ppermute | solution.py:14
Sparse Core Ops, SparseCore 0:
  18.7 68.1 all-reduce.3
where the time goes:
time: 187 us; the launch traced here: 186 us
  waiting for transfers between devices  79.2 us (42%)
  matrix products  37.2 us (20%)
  blocking collectives  22.4 us (12%)
  local copies, waits for them, and re-layouts  17.5 us (9%)
  between operations  14.3 us (8%)
  other arithmetic  9.35 us (5%)
  starting transfers between devices  5.97 us (3%)
    psum x1, waiting for transfers between devices, shards(): keys = lax.psum(partial_keys, 'tp')  64.4 us
    unnamed x24, local copies, waits for them, and re-layouts  16.1 us
    ppermute x5, waiting for transfers between devices, passed_along(): lax.ppermute(x, axis, [(i, (i + by) % length) for i in range(length)])  14.8 us
    psum x1, blocking collectives, shards(): lax.psum(sum_left.astype(jnp.bfloat16), 'tp').astype(jnp.float32)  13.2 us
    dot_general x2, matrix products, contract_rank(): lax.dot_general(left, right, (((0,), (0,)), ((), ())), precision=HIGH)  9.95 us
    psum x1, blocking collectives, shards(): gram_right, gram_left = lax.psum((gram_right, gram_left), 'tp')  9.16 us
    dot_general x1, matrix products, shards(): back_right_own = jnp.dot(source_right, stepped, precision=HIGH)  6.92 us
    ppermute x5, starting transfers between devices, passed_along(): lax.ppermute(x, axis, [(i, (i + by) % length) for i in range(length)])  5.93 us
  transfers between devices with their start and end apart: 6, of which 5 were waited for; matrix products, arithmetic and copies ran while one was open for 9% of the time, Pallas kernels for 0%

commit v1 on v0

v1 whole, which is shorter than its diff:
```python
import functools

import jax
import jax.numpy as jnp
from jax import lax
from jax.experimental import pallas as pl
from jax.experimental.pallas import tpu as pltpu
from jax.sharding import PartitionSpec as P

F32 = jnp.float32
BF16 = jnp.bfloat16
MIB = 1024 * 1024
VM = pl.BlockSpec(memory_space=pltpu.VMEM)
ANY = pl.BlockSpec(memory_space=pl.ANY)
NT = (((1,), (1,)), ((), ()))


def in_vmem(x):
    return pltpu.with_memory_space_constraint(x, pltpu.VMEM)


def call(body, args, outs, scratch=(), limit=24, flops=0, nbytes=0, spaces=None, out_spaces=None):
    spaces = spaces or (True,) * len(args)
    out_spaces = out_spaces or (True,) * len(outs)
    return pl.pallas_call(
        body,
        out_shape=[
            pltpu.VMEM(shape, dtype) if inside else jax.ShapeDtypeStruct(shape, dtype)
            for (shape, dtype), inside in zip(outs, out_spaces)
        ],
        in_specs=[VM if inside else ANY for inside in spaces],
        out_specs=[VM if inside else ANY for inside in out_spaces],
        scratch_shapes=list(scratch),
        compiler_params=pltpu.CompilerParams(vmem_limit_bytes=limit * MIB),
        cost_estimate=pl.CostEstimate(flops=flops, bytes_accessed=nbytes, transcendentals=0),
    )(*[in_vmem(a) if inside else a for a, inside in zip(args, spaces)])


def dot(a, b, dims=(((1,), (0,)), ((), ()))):
    return lax.dot_general(a, b, dims, preferred_element_type=F32)


def split(x):
    hi = x.astype(BF16)
    return hi, (x - hi.astype(F32)).astype(BF16)


def core_index():
    return lax.rem(lax.axis_index("tp"), 2)


def half_at(which, half):
    return pl.ds(pl.multiple_of(which * half, 128), half)


def sent_kernel(tok, w, tok_v, w_s, hi_s, part, tok_sem, w_sem):
    half = w_s.shape[1]
    depth = w_s.shape[0]
    steps = w_sem.shape[0]
    k = depth // steps
    cols = half_at(1 - core_index(), half)
    tok_copies, w_copies = [], []
    for j in range(steps):
        at = pl.ds(j * k, k)
        tok_copies.append(pltpu.make_async_copy(tok.at[:, at], tok_v.at[:, at], tok_sem.at[j]))
        w_copies.append(pltpu.make_async_copy(w.at[at, cols], w_s.at[at], w_sem.at[j]))
        tok_copies[j].start()
        w_copies[j].start()
    acc = None
    for j in range(steps):
        tok_copies[j].wait()
        w_copies[j].wait()
        hi = w_s[j * k : (j + 1) * k].astype(BF16)
        hi_s[j * k : (j + 1) * k] = hi
        term = dot(tok_v[:, j * k : (j + 1) * k], hi)
        acc = term if acc is None else acc + term
    part[...] = acc.astype(BF16)


def kept_kernel(tok_v, w, w_k, hi_k, part, w_sem):
    half = w_k.shape[1]
    depth = w_k.shape[0]
    steps = w_sem.shape[0]
    k = depth // steps
    cols = half_at(core_index(), half)
    w_copies = []
    for j in range(steps):
        at = pl.ds(j * k, k)
        w_copies.append(pltpu.make_async_copy(w.at[at, cols], w_k.at[at], w_sem.at[j]))
        w_copies[j].start()
    acc = None
    for j in range(steps):
        w_copies[j].wait()
        hi = w_k[j * k : (j + 1) * k].astype(BF16)
        hi_k[j * k : (j + 1) * k] = hi
        term = dot(tok_v[:, j * k : (j + 1) * k], hi)
        acc = term if acc is None else acc + term
    part[...] = acc


def chip_sum_kernel(part, got, out):
    out[...] = (part[...] + got[...].astype(F32)).astype(BF16)


def shadow_kernel(tok_v, w_s, w_k, vec, left_vec, proj, tok_t):
    half = w_s.shape[1]
    c = core_index()
    total = None
    for w_half, which in ((w_s, 1 - c), (w_k, c)):
        at = half_at(which, half)
        q = jnp.concatenate([vec[:, at], left_vec[:, at]], axis=0)
        q_hi, q_lo = split(q)
        w_hi, w_lo = split(w_half[...])
        term = dot(q_hi, w_hi, NT) + dot(q_lo, w_hi, NT) + dot(q_hi, w_lo, NT)
        total = term if total is None else total + term
    proj[...] = total
    tok_t[...] = tok_v[...].T


def norm_kernel(scale, own, got, cot, gain, kg, gain_grad):
    head = gain.shape[1]
    heads = own.shape[1] // head
    half = own.shape[1]
    at = half_at(core_index(), half)
    keys_all = (own[...].astype(F32) + got[...].astype(F32)) * scale
    up_all = cot[:, at].astype(F32)
    g = gain[...]
    total = None
    for h in range(heads):
        cols = slice(h * head, (h + 1) * head)
        keys = keys_all[:, cols]
        up = up_all[:, cols]
        gh = up * g
        inv = lax.rsqrt(jnp.mean(keys * keys, axis=-1, keepdims=True) + 1e-6)
        along = jnp.mean(gh * keys, axis=-1, keepdims=True)
        unit = keys * inv
        kg[:, cols] = (inv * (gh - unit * (inv * along))).astype(BF16)
        part = jnp.sum(up * unit, axis=0, keepdims=True)
        total = part if total is None else total + part
    gain_grad[...] = total


def project_kernel(rate, kg_k, kg_s, vec, left_vec, proj0, tok_v, right, left):
    half = kg_k.shape[1]
    c = core_index()
    g = None
    for kg, which in ((kg_k, c), (kg_s, 1 - c)):
        at = half_at(which, half)
        q_hi, q_lo = split(jnp.concatenate([vec[:, at], left_vec[:, at]], axis=0))
        term = dot(q_hi, kg[...], NT) + dot(q_lo, kg[...], NT)
        g = term if g is None else g + term
    g_hi, g_lo = split(g)
    proj = proj0[...] - rate * (dot(g_hi, tok_v[...]) + dot(g_lo, tok_v[...]))
    rank = right.shape[0]
    right[...] = proj[:rank]
    left[...] = proj[rank:]


def step_kernel(rate, tok_t, kg, w, out):
    out[...] = w[...] - rate * dot(tok_t[...], kg[...])


def input_kernel(scale, kg_k, kg_s, hi_k, hi_s, out):
    out[...] = ((dot(kg_k[...], hi_k[...], NT) + dot(kg_s[...], hi_s[...], NT)) * scale).astype(BF16)


def back_kernel(right, left, got_right, got_left, s_k, s_s, gain_grad, rows_out, payload):
    half = s_k.shape[1]
    c = core_index()
    rows = jnp.concatenate([right[...] - got_right[...], got_left[...] - left[...]], axis=0)
    rows_out[...] = rows
    r_hi, r_lo = split(rows)
    for s, which in ((s_k, c), (s_s, 1 - c)):
        s_hi, s_lo = split(s[...])
        payload[:, half_at(which, half)] = dot(r_hi, s_hi) + dot(r_lo, s_hi) + dot(r_hi, s_lo)
    n = rows.shape[0]
    gram = lax.dot_general(rows, rows, NT, precision=lax.Precision.HIGHEST, preferred_element_type=F32)
    payload[:, 2 * half : 2 * half + 128] = jnp.concatenate([gram, jnp.zeros((n, 128 - n), F32)], axis=1)
    payload[:, 2 * half + 128 :] = jnp.broadcast_to(gain_grad[...], (n, 128))


def pair_kernel(mine, other, gain, total, aside, new_gain):
    rank = aside.shape[0]
    width = aside.shape[1]
    both = mine[...] + other[...]
    total[...] = both[:, : width + 128]
    c = core_index()
    aside[...] = jnp.where(c == 0, both[:rank, :width], both[rank:, :width])
    new_gain[...] = gain[...] - 0.002 * both[0:1, width + 128 :]


def edge_kernel(total, other, got, got_far, mine, gram):
    rank, width = mine.shape
    whole = total[...] + other[...]
    c = core_index()
    near = jnp.where(c == 0, whole[rank:, :width], whole[:rank, :width])
    far = got[...] + got_far[...]
    mine[...] = jnp.where(c == 0, far - near, near - far)
    gram[...] = whole[:, width:]


def whiten_kernel(rank, gram, rows, inverse, unit):
    n = gram.shape[0]
    width = gram.shape[1]
    lane = lax.broadcasted_iota(jnp.int32, (rank, width), 1)
    row = lax.broadcasted_iota(jnp.int32, (rank, width), 0)
    parts = []
    for e in range(n // rank):
        a = gram[e * rank : (e + 1) * rank]
        a = jnp.where((lane >= e * rank) & (lane < (e + 1) * rank), a, 0.0)
        a = jnp.where(lane == n + e * rank + row, 1.0, a)
        for i in range(rank):
            col = a[:, e * rank + i : e * rank + i + 1]
            pivot = lax.rsqrt(col[i : i + 1])
            line = a[i : i + 1] * pivot
            a = jnp.where(row == i, line, jnp.where(row > i, a - (col * pivot) * line, a))
        parts.append(a)
    both = jnp.concatenate(parts, axis=0)
    inverse[...] = both
    unit[...] = apply_inverse(both, rows[...], n)


def apply_inverse(both, x, n):
    total = None
    for j in range(n):
        term = both[:, n + j : n + j + 1] * x[j : j + 1]
        total = term if total is None else total + term
    return total


def mix_kernel(s_k, s_s, unit, inverse, mine, other, out, new_vec, stage, sem):
    rank, width = mine.shape
    half = s_k.shape[1]
    depth = s_k.shape[0]
    steps = sem.shape[0]
    k = depth // steps
    n = 2 * rank
    c = core_index()
    a, b = mine[...], other[...]
    back = jnp.concatenate([jnp.where(c == 0, b, a), jnp.where(c == 0, a, b)], axis=0)
    nv = apply_inverse(inverse[...], back, n)
    new_vec[...] = nv[:rank]
    sign = jnp.where(lax.broadcasted_iota(jnp.int32, (n, width), 0) < rank, 1.0 / 3.0, -1.0 / 3.0)
    v_hi, v_lo = split(nv * sign)
    stacked = jnp.concatenate([v_hi, v_lo, v_hi], axis=0)
    u_hi, u_lo = split(unit[...])
    lhs = jnp.concatenate([u_hi, u_hi, u_lo], axis=0)
    stage_v = stage
    copies = []
    for j in range(steps):
        at = slice(j * k, (j + 1) * k)
        delta = lax.dot_general(lhs[:, at], stacked, (((0,), (0,)), ((), ())), preferred_element_type=F32)
        low = jnp.where(c == 0, s_k[at], s_s[at])
        high = jnp.where(c == 0, s_s[at], s_k[at])
        stage_v[at, :half] = low - delta[:, :half]
        stage_v[at, half:] = high - delta[:, half:]
        copies.append(pltpu.make_async_copy(stage_v.at[pl.ds(j * k, k)], out.at[pl.ds(j * k, k)], sem.at[j]))
        copies[j].start()
    for j in range(steps):
        copies[j].wait()


def shards(tokens, weights, gain, cotangent, vectors):
    rows, depth = tokens.shape
    width = weights.shape[2]
    half = width // 2
    rank = vectors.shape[1]
    tp = lax.axis_size("tp")
    loop = lax.axis_size("loop")
    scale = (depth * tp) ** -0.5
    rate = 0.1 * scale
    weight = weights[0]
    vec = vectors[0]
    core = [(i, i ^ 1) for i in range(tp)]
    chip = [(i, i ^ 2) for i in range(tp)]
    right = [(i, (i + 1) % loop) for i in range(loop)]
    left = [(i, (i - 1) % loop) for i in range(loop)]
    along, along_far = [], []
    for i in range(loop):
        for t in range(tp):
            to = (i + 1) % loop if t % 2 == 0 else (i - 1) % loop
            along.append((i * tp + t, to * tp + t))
            along_far.append((i * tp + t, to * tp + (t ^ 2)))
    everyone = ("loop", "tp")

    left_vec = lax.ppermute(vec, "loop", right)
    steps = 5
    dma = pltpu.SemaphoreType.DMA
    half_flops = 2 * rows * depth * half
    tok_v, w_s, hi_s, part_s = call(
        sent_kernel,
        (tokens, weight),
        [((rows, depth), BF16), ((depth, half), F32), ((depth, half), BF16), ((rows, half), BF16)],
        [dma((steps,)), dma((steps,))],
        spaces=(False, False),
        flops=half_flops,
        nbytes=4 * MIB,
    )
    from_core = lax.ppermute(part_s, "tp", core)
    w_k, hi_k, part_k = call(
        kept_kernel,
        (tok_v, weight),
        [((depth, half), F32), ((depth, half), BF16), ((rows, half), F32)],
        [dma((steps,))],
        spaces=(True, False),
        flops=half_flops,
        nbytes=3 * MIB,
    )
    (chip_part,) = call(chip_sum_kernel, (part_k, from_core), [((rows, half), BF16)], nbytes=2 * MIB)
    from_chip = lax.ppermute(chip_part, "tp", chip)
    proj0, tok_t = call(
        shadow_kernel,
        (tok_v, w_s, w_k, vec, left_vec),
        [((2 * rank, depth), F32), ((depth, rows), BF16)],
        flops=half_flops,
        nbytes=8 * MIB,
    )
    kg_k, gain_grad = call(
        functools.partial(norm_kernel, scale),
        (chip_part, from_chip, cotangent, gain),
        [((rows, half), BF16), (gain.shape, F32)],
        nbytes=2 * MIB,
    )
    kg_s = lax.ppermute(kg_k, "tp", core)
    (s_k,) = call(
        functools.partial(step_kernel, rate),
        (tok_t, kg_k, w_k),
        [((depth, half), F32)],
        flops=half_flops,
        nbytes=6 * MIB,
    )
    proj_right, proj_left = call(
        functools.partial(project_kernel, rate),
        (kg_k, kg_s, vec, left_vec, proj0, tok_v),
        [((rank, depth), F32), ((rank, depth), F32)],
        nbytes=2 * MIB,
    )
    got_left = lax.ppermute(proj_right, "loop", right)
    got_right = lax.ppermute(proj_left, "loop", left)
    (s_s,) = call(
        functools.partial(step_kernel, rate),
        (tok_t, kg_s, w_s),
        [((depth, half), F32)],
        flops=half_flops,
        nbytes=6 * MIB,
    )
    (input_grad,) = call(
        functools.partial(input_kernel, scale),
        (kg_k, kg_s, hi_k, hi_s),
        [((rows, depth), BF16)],
        flops=2 * half_flops,
        nbytes=5 * MIB,
    )
    edge_rows, payload = call(
        back_kernel,
        (proj_right, proj_left, got_right, got_left, s_k, s_s, gain_grad),
        [((2 * rank, depth), F32), ((2 * rank, width + 256), F32)],
        nbytes=6 * MIB,
    )
    other_core = lax.ppermute(payload, "tp", core)
    pair, aside, new_gain = call(
        pair_kernel,
        (payload, other_core, gain),
        [((2 * rank, width + 128), F32), ((rank, width), F32), (gain.shape, F32)],
    )
    got_near = lax.ppermute(aside, everyone, along)
    got_far = lax.ppermute(aside, everyone, along_far)
    other_chip = lax.ppermute(pair, "tp", chip)
    mine, gram = call(
        edge_kernel,
        (pair, other_chip, got_near, got_far),
        [((rank, width), F32), ((2 * rank, 128), F32)],
    )
    other = lax.ppermute(mine, "tp", core)
    inverse, unit = call(
        functools.partial(whiten_kernel, rank),
        (gram, edge_rows),
        [((2 * rank, 128), F32), ((2 * rank, depth), F32)],
    )
    new_weights, new_vec = call(
        mix_kernel,
        (s_k, s_s, unit, inverse, mine, other),
        [((depth, width), F32), ((rank, width), F32)],
        [pltpu.VMEM((depth, width), F32), dma((steps,))],
        out_spaces=(False, True),
        nbytes=10 * MIB,
    )
    return (new_weights[None], input_grad, new_gain, new_vec[None])


def solution(mesh):
    return jax.shard_map(
        shards,
        mesh=mesh,
        in_specs=(
            P("loop", "tp"),
            P("loop", "tp", None),
            P("loop", None),
            P("loop", None),
            P("loop", None, None),
        ),
        out_specs=(P("loop", "tp", None), P("loop", "tp"), P("loop", None), P("loop", None, None)),
        check_vma=False,
    )
```

time: 187 us -> 71.4 us (0.38)
  waiting for transfers between devices: 79.2 us -> 25.8 us
  matrix products: 37.2 us -> 0 us
  blocking collectives: 22.4 us -> 0 us
  starting transfers between devices: 5.97 us -> 23.8 us
  Pallas kernels: 0 us -> 14.8 us
  between operations: 14.3 us -> 0.77 us
  local copies, waits for them, and re-layouts: 17.5 us -> 5.99 us
  other arithmetic: 9.35 us -> 0 us
    psum x1 -> x0, waiting for transfers between devices: 64.4 us -> none  [shards(): keys = lax.psum(partial_keys, 'tp')]
    dot_general x11 -> x0, matrix products: 36.7 us -> none  [the longest x2 9.95 us: contract_rank(): lax.dot_general(left, right, (((0,), (0,)), ((), ())), precision=HIGH)]
    psum x2 -> x0, blocking collectives: 22.4 us -> none  [the longest x1 13.2 us: shards(): lax.psum(sum_left.astype(jnp.bfloat16), 'tp').astype(jnp.float32)]
    ppermute x5 -> x11, starting transfers between devices: 5.93 us -> 23.8 us  [the longest x1 5.9 us: shards(): got_far = lax.ppermute(aside, everyone, along_far)]
    pallas_call x0 -> x14, Pallas kernels: none -> 14.8 us  [call(): pl.pallas_call(body, out_shape=[pltpu.VMEM(shape, dtype) if inside else j...]
    ppermute x5 -> x11, waiting for transfers between devices: 14.8 us -> 25.8 us  [the longest x1 13.1 us: shards(): from_chip = lax.ppermute(chip_part, 'tp', chip)]
    unnamed x24 -> x15, local copies, waits for them, and re-layouts: 16.1 us -> 5.99 us
    another operation x10 -> x0, other arithmetic: 4.05 us -> none  [the longest x4 1.98 us: lower_solve(): return lax.linalg.triangular_solve(lower, rhs, left_side=True, lower=True)]
  transfers between devices with their start and end apart: 6 -> 11, of which waited for: 5 -> 7; matrix products, arithmetic and copies ran while one was open for 9% -> 2% of each run, Pallas kernels for 0% -> 10%
where the time goes in v1:
time: 71.4 us; the launch traced here: 71.2 us
  waiting for transfers between devices  25.8 us (36%)
  starting transfers between devices  23.8 us (33%)
  Pallas kernels  14.8 us (21%)
  local copies, waits for them, and re-layouts  5.99 us (8%)
  between operations  0.77 us (1%)
    pallas_call x14, Pallas kernels, call(): pl.pallas_call(body, out_shape=[pltpu.VMEM(shape, dtype) if inside else j...  14.8 us
    ppermute x1, waiting for transfers between devices, shards(): from_chip = lax.ppermute(chip_part, 'tp', chip)  13.1 us
    ppermute x1, waiting for transfers between devices, shards(): left_vec = lax.ppermute(vec, 'loop', right)  8.42 us
    unnamed x15, local copies, waits for them, and re-layouts  5.99 us
    ppermute x1, starting transfers between devices, shards(): got_far = lax.ppermute(aside, everyone, along_far)  5.9 us
    ppermute x1, starting transfers between devices, shards(): got_right = lax.ppermute(proj_left, 'loop', left)  5.7 us
    ppermute x1, starting transfers between devices, shards(): from_core = lax.ppermute(part_s, 'tp', core)  3.33 us
    ppermute x1, starting transfers between devices, shards(): other_chip = lax.ppermute(pair, 'tp', chip)  2.72 us
  transfers between devices with their start and end apart: 11, of which 7 were waited for; matrix products, arithmetic and copies ran while one was open for 2% of the time, Pallas kernels for 10%

profile of v1, /device:TPU:1, one launch (start us, length us, event | category | flops | bytes accessed | tf_op | source)
XLA Modules:
  0.0 71.2 jit_solution(11914215594168494959)
XLA Ops:
  0.6 0.0 copy-start
  0.6 2.5 %copy-done = f32[1,1280,1024]{2,1,0:T(8,128)S(1)} copy-done((f32[1,1280,1024]{2,1,0:T(8,128)S(1)}, f32[1,1280,1024]{2,1,0:T(8,128)}, u32[]{:S(2)}) %copy-start) | copy-done | bytes 5242904
  3.1 0.0 copy-start.2
  3.1 1.3 %copy-done.2 = bf16[512,1280]{1,0:T(8,128)(2,1)S(1)} copy-done((bf16[512,1280]{1,0:T(8,128)(2,1)S(1)}, bf16[512,1280]{1,0:T(8,128)(2,1)}, u32[]{:S(2)}) %copy-start.2) | copy-done | bytes 1310744
  4.4 1.5 %shard_map.84 = (bf16[512,1280]{1,0:T(8,128)(2,1)S(1)}, f32[1280,512]{1,0:T(8,128)S(1)}, bf16[1280,512]{1,0:T(8,128)(2,1)S(1)}, bf16[512,512]{1,0:T(8,128)(2,1)S(1)}) custom-call(bf16[512,1280]{1,0:T(8,128)(2,1)S(1)} %copy-done.2, f32[1280,1024]{1,0:T(8,128)S(1)} %bitcast.5), custom_call_target="tpu_custom_call" | custom-call | flops 671088640 | bytes 4194304 | tf_op jit(solution)/shard_map/pallas_call | solution.py:25
  5.9 3.3 %collective-permute-start.1 = (bf16[512,512]{1,0:T(8,128)(2,1)S(1)}, bf16[512,512]{1,0:T(8,128)(2,1)S(1)}, u32[]{:S(2)}, u32[]{:S(2)}) collective-permute-start(bf16[512,512]{1,0:T(8,128)(2,1)S(1)} %get-tuple-element.33), channel_id=1, source_target_pairs={{0,1},{1,0},{2,3},{3,2},{4,5},{5,4},{6,7},{7,6},{8,9},{9,8},{10,11... | collective-permute-start | bytes 1572872 | tf_op jit(solution)/shard_map/ppermute | solution.py:299
  9.3 0.0 copy-done.1
  9.3 1.3 %shard_map.85 = (f32[1280,512]{1,0:T(8,128)S(1)}, bf16[1280,512]{1,0:T(8,128)(2,1)S(1)}, f32[512,512]{1,0:T(8,128)S(1)}) custom-call(bf16[512,1280]{1,0:T(8,128)(2,1)S(1)} %get-tuple-element.28.tok_v, f32[1280,1024]{1,0:T(8,128)S(1)} %bitcast.6), custom_call_target="tpu_custom_call" | custom-call | flops 671088640 | bytes 3145728 | tf_op jit(solution)/shard_map/pallas_call | solution.py:25
  10.6 0.0 copy-start.3
  10.6 0.0 copy-start.5
  10.6 0.2 collective-permute-done.1.got
  10.8 0.1 shard_map.87.own
  10.9 0.0 copy-start.4
  10.9 1.2 %collective-permute-start.2 = (bf16[512,512]{1,0:T(8,128)(2,1)S(1)}, bf16[512,512]{1,0:T(8,128)(2,1)S(1)}, u32[]{:S(2)}, u32[]{:S(2)}) collective-permute-start(bf16[512,512]{1,0:T(8,128)(2,1)S(1)} %shard_map.87.own), channel_id=1, source_target_pairs={{0,2},{1,3},{2,0},{3,1},{4,6},{5,7},{6,4},{7,5},{8,10},{9,11},{10,... | collective-permute-start | bytes 1572872 | tf_op jit(solution)/shard_map/ppermute | solution.py:310
  12.1 13.1 %collective-permute-done.2.got = bf16[512,512]{1,0:T(8,128)(2,1)S(1)} collective-permute-done((bf16[512,512]{1,0:T(8,128)(2,1)S(1)}, bf16[512,512]{1,0:T(8,128)(2,1)S(1)}, u32[]{:S(2)}, u32[]{:S(2)}) %collective-permute-start.2) | collective-permute-done | bytes 524320 | tf_op jit(solution)/shard_map/ppermute | solution.py:310
  25.2 0.0 copy-done.3
  25.2 0.0 copy-done.5
  25.2 0.8 %shard_map.88 = (bf16[512,512]{1,0:T(8,128)(2,1)S(1)}, f32[1,128]{1,0:T(1,128)S(1)}) custom-call(bf16[512,512]{1,0:T(8,128)(2,1)S(1)} %shard_map.87.own, bf16[512,512]{1,0:T(8,128)(2,1)S(1)} %collective-permute-done.2.got, bf16[512,1024]{1,0:T(8,128)(2,1)S(1)} %copy-done.3, f32[1,128]{1,0:T(1,128)S(1)} %copy-done.5), custom_call_target="tpu_custom_call" | custom-call | bytes 2097152 | tf_op jit(solution)/shard_map/pallas_call | solution.py:25
  26.0 1.7 %collective-permute-start.3 = (bf16[512,512]{1,0:T(8,128)(2,1)S(1)}, bf16[512,512]{1,0:T(8,128)(2,1)S(1)}, u32[]{:S(2)}, u32[]{:S(2)}) collective-permute-start(bf16[512,512]{1,0:T(8,128)(2,1)S(1)} %get-tuple-element.34.kg.kg_k), channel_id=1, source_target_pairs={{0,1},{1,0},{2,3},{3,2},{4,5},{5,4},{6,7},{7,6},{8,9},{9,8},{10,11... | collective-permute-start | bytes 1572872 | tf_op jit(solution)/shard_map/ppermute | solution.py:324
  27.8 0.0 copy-done.4
  27.8 0.0 collective-permute-start
  27.8 8.4 %collective-permute-done.left_vec = f32[4,1024]{1,0:T(4,128)S(1)} collective-permute-done((f32[4,1024]{1,0:T(4,128)S(1)}, f32[4,1024]{1,0:T(4,128)S(1)}, u32[]{:S(2)}, u32[]{:S(2)}) %collective-permute-start) | collective-permute-done | bytes 16416 | tf_op jit(solution)/shard_map/ppermute | solution.py:286
  36.2 2.1 %shard_map.86 = (f32[8,1280]{1,0:T(8,128)S(1)}, bf16[1280,512]{1,0:T(8,128)(2,1)S(1)}) custom-call(bf16[512,1280]{1,0:T(8,128)(2,1)S(1)} %get-tuple-element.28.tok_v, f32[1280,512]{1,0:T(8,128)S(1)} %get-tuple-element.29.w_s.w, f32[1280,512]{1,0:T(8,128)S(1)} %get-tuple-element.30.w_k.w, f32[4,1024]{1,0:T(4,128)S(1)} %bitcast.8, ...), custom_call_target="tpu_custom_call" | custom-call | flops 671088640 | bytes 8388608 | tf_op jit(solution)/shard_map/pallas_call | solution.py:25
  38.3 0.9 %shard_map.89.s_k = f32[1280,512]{1,0:T(8,128)S(1)} custom-call(bf16[1280,512]{1,0:T(8,128)(2,1)S(1)} %get-tuple-element.31.tok_t, bf16[512,512]{1,0:T(8,128)(2,1)S(1)} %get-tuple-element.34.kg.kg_k, f32[1280,512]{1,0:T(8,128)S(1)} %get-tuple-element.30.w_k.w), custom_call_target="tpu_custom_call" | custom-call | flops 671088640 | bytes 6291456 | tf_op jit(solution)/shard_map/pallas_call | solution.py:25
  39.2 0.0 collective-permute-done.3.kg.kg_s
  39.2 1.2 %shard_map.91 = (f32[4,1280]{1,0:T(4,128)S(1)}, f32[4,1280]{1,0:T(4,128)S(1)}) custom-call(bf16[512,512]{1,0:T(8,128)(2,1)S(1)} %get-tuple-element.34.kg.kg_k, bf16[512,512]{1,0:T(8,128)(2,1)S(1)} %collective-permute-done.3.kg.kg_s, f32[4,1024]{1,0:T(4,128)S(1)} %bitcast.9, f32[4,1024]{1,0:T(4,128)S(1)} %collective-permute-done.left_vec, ...), custom_call_target="tpu_custom_call" | custom-call | bytes 2097152 | tf_op jit(solution)/shard_map/pallas_call | solution.py:25
  40.4 0.0 collective-permute-start.5
  40.4 5.7 %collective-permute-start.4 = (f32[4,1280]{1,0:T(4,128)S(1)}, f32[4,1280]{1,0:T(4,128)S(1)}, u32[]{:S(2)}, u32[]{:S(2)}) collective-permute-start(f32[4,1280]{1,0:T(4,128)S(1)} %get-tuple-element.37.left), channel_id=1, source_target_pairs={{0,252},{4,0},{8,4},{12,8},{16,12},{20,16},{24,20},{28,24},{32,28}... | collective-permute-start | bytes 61448 | tf_op jit(solution)/shard_map/ppermute | solution.py:339
  46.1 0.8 %shard_map.90.s_s = f32[1280,512]{1,0:T(8,128)S(1)} custom-call(bf16[1280,512]{1,0:T(8,128)(2,1)S(1)} %get-tuple-element.31.tok_t, bf16[512,512]{1,0:T(8,128)(2,1)S(1)} %collective-permute-done.3.kg.kg_s, f32[1280,512]{1,0:T(8,128)S(1)} %get-tuple-element.29.w_s.w), custom_call_target="tpu_custom_call" | custom-call | flops 671088640 | bytes 6291456 | tf_op jit(solution)/shard_map/pallas_call | solution.py:25
  46.9 0.3 collective-permute-done.5.got_left
  47.3 0.0 collective-permute-done.4.got_right
  47.3 1.3 %shard_map.92 = (f32[8,1280]{1,0:T(8,128)S(1)}, f32[8,1280]{1,0:T(8,128)S(1)}) custom-call(f32[4,1280]{1,0:T(4,128)S(1)} %get-tuple-element.36.right, f32[4,1280]{1,0:T(4,128)S(1)} %get-tuple-element.37.left, f32[4,1280]{1,0:T(4,128)S(1)} %collective-permute-done.4.got_right, f32[4,1280]{1,0:T(4,128)S(1)} %collective-permute-done.5.got_left, ...), custom_call_target="tpu_custom_call" | custom-call | bytes 6291456 | tf_op jit(solution)/shard_map/pallas_call | solution.py:25
  48.6 2.1 %collective-permute-start.6 = (f32[8,1280]{1,0:T(8,128)S(1)}, f32[8,1280]{1,0:T(8,128)S(1)}, u32[]{:S(2)}, u32[]{:S(2)}) collective-permute-start(f32[8,1280]{1,0:T(8,128)S(1)} %get-tuple-element.39.mine), channel_id=1, source_target_pairs={{0,1},{1,0},{2,3},{3,2},{4,5},{5,4},{6,7},{7,6},{8,9},{9,8},{10,11... | collective-permute-start | bytes 122888 | tf_op jit(solution)/shard_map/ppermute | solution.py:360
  50.7 0.9 %collective-permute-done.6.other = f32[8,1280]{1,0:T(8,128)S(1)} collective-permute-done((f32[8,1280]{1,0:T(8,128)S(1)}, f32[8,1280]{1,0:T(8,128)S(1)}, u32[]{:S(2)}, u32[]{:S(2)}) %collective-permute-start.6) | collective-permute-done | bytes 40992 | tf_op jit(solution)/shard_map/ppermute | solution.py:360
  51.6 2.7 %collective-permute-start.7 = (f32[8,1152]{1,0:T(8,128)S(1)}, f32[8,1152]{1,0:T(8,128)S(1)}, u32[]{:S(2)}, u32[]{:S(2)}) collective-permute-start(f32[8,1152]{1,0:T(8,128)S(1)} %get-tuple-element.40.total), channel_id=1, source_target_pairs={{0,2},{1,3},{2,0},{3,1},{4,6},{5,7},{6,4},{7,5},{8,10},{9,11},{10,... | collective-permute-start | bytes 110600 | tf_op jit(solution)/shard_map/ppermute | solution.py:368
  54.3 5.9 %collective-permute-start.9 = (f32[4,1024]{1,0:T(4,128)S(1)}, f32[4,1024]{1,0:T(4,128)S(1)}, u32[]{:S(2)}, u32[]{:S(2)}) collective-permute-start(f32[4,1024]{1,0:T(4,128)S(1)} %get-tuple-element.41), channel_id=1, source_target_pairs={{0,6},{1,255},{2,4},{3,253},{4,10},{5,3},{6,8},{7,1},{8,14},{9,7},... | collective-permute-start | bytes 49160 | tf_op jit(solution)/shard_map/ppermute | solution.py:367
  60.2 0.0 collective-permute-start.8
  60.2 0.9 %collective-permute-done.9.got_far = f32[4,1024]{1,0:T(4,128)S(1)} collective-permute-done((f32[4,1024]{1,0:T(4,128)S(1)}, f32[4,1024]{1,0:T(4,128)S(1)}, u32[]{:S(2)}, u32[]{:S(2)}) %collective-permute-start.9) | collective-permute-done | bytes 16416 | tf_op jit(solution)/shard_map/ppermute | solution.py:367
  61.1 2.0 %collective-permute-done.8.got = f32[4,1024]{1,0:T(4,128)S(1)} collective-permute-done((f32[4,1024]{1,0:T(4,128)S(1)}, f32[4,1024]{1,0:T(4,128)S(1)}, u32[]{:S(2)}, u32[]{:S(2)}) %collective-permute-start.8) | collective-permute-done | bytes 16416 | tf_op jit(solution)/shard_map/ppermute | solution.py:366
  63.1 0.0 collective-permute-done.7.other
  63.1 1.1 %collective-permute-start.10 = (f32[4,1024]{1,0:T(4,128)S(1)}, f32[4,1024]{1,0:T(4,128)S(1)}, u32[]{:S(2)}, u32[]{:S(2)}) collective-permute-start(f32[4,1024]{1,0:T(4,128)S(1)} %get-tuple-element.46.mine), channel_id=1, source_target_pairs={{0,1},{1,0},{2,3},{3,2},{4,5},{5,4},{6,7},{7,6},{8,9},{9,8},{10,11... | collective-permute-start | bytes 49160 | tf_op jit(solution)/shard_map/ppermute | solution.py:374
  64.2 1.6 %shard_map.97 = bf16[512,1280]{1,0:T(8,128)(2,1)S(1)} custom-call(bf16[512,512]{1,0:T(8,128)(2,1)S(1)} %get-tuple-element.34.kg.kg_k, bf16[512,512]{1,0:T(8,128)(2,1)S(1)} %collective-permute-done.3.kg.kg_s, bf16[1280,512]{1,0:T(8,128)(2,1)S(1)} %get-tuple-element.48.hi_k, bf16[1280,512]{1,0:T(8,128)(2,1)S(1)} %get-tuple-element.49.hi_s), custom_call_target="tpu_custom_call" | custom-call | flops 1342177280 | bytes 5242880 | tf_op jit(solution)/shard_map/pallas_call | solution.py:25
  65.8 1.1 %copy.9 = bf16[512,1280]{1,0:T(8,128)(2,1)} copy(bf16[512,1280]{1,0:T(8,128)(2,1)S(1)} %shard_map.97) | data formatting | bytes 2621440
  66.9 0.5 copy.10
  67.4 0.4 shard_map.95
  67.8 0.0 collective-permute-done.10.other
  67.8 2.8 %shard_map.96 = (f32[1280,1024]{1,0:T(8,128)}, f32[4,1024]{1,0:T(4,128)S(1)}) custom-call(f32[1280,512]{1,0:T(8,128)S(1)} %shard_map.89.s_k, f32[1280,512]{1,0:T(8,128)S(1)} %shard_map.90.s_s, f32[8,1280]{1,0:T(8,128)S(1)} %get-tuple-element.44.unit, f32[8,128]{1,0:T(8,128)S(1)} %get-tuple-element.45.inverse, f32[4,1024]{1,0:T(4,128)S(1)} %get-tuple-element.46.mine, ...), custom_call_target="tpu_custom_call" | custom-call | bytes 10485760 | tf_op jit(solution)/shard_map/pallas_call | solution.py:25
  70.6 0.6 copy.11
  (3 shorter events, 0.0 us)
Async XLA Ops:
  0.6 2.5 %copy-start = (f32[1,1280,1024]{2,1,0:T(8,128)S(1)}, f32[1,1280,1024]{2,1,0:T(8,128)}, u32[]{:S(2)}) copy-start(f32[1,1280,1024]{2,1,0:T(8,128)} %param.6) | copy-start | bytes 15728644
  3.1 1.3 %copy-start.2 = (bf16[512,1280]{1,0:T(8,128)(2,1)S(1)}, bf16[512,1280]{1,0:T(8,128)(2,1)}, u32[]{:S(2)}) copy-start(bf16[512,1280]{1,0:T(8,128)(2,1)} %tok.1) | copy-start | bytes 3932164
  4.4 4.8 %copy-start.1 = (f32[1,1280,1024]{2,1,0:T(8,128)S(1)}, f32[1,1280,1024]{2,1,0:T(8,128)}, u32[]{:S(2)}) copy-start(f32[1,1280,1024]{2,1,0:T(8,128)} %param.6) | copy-start | bytes 15728644
  5.9 4.9 %collective-permute-start.1 = (bf16[512,512]{1,0:T(8,128)(2,1)S(1)}, bf16[512,512]{1,0:T(8,128)(2,1)S(1)}, u32[]{:S(2)}, u32[]{:S(2)}) collective-permute-start(bf16[512,512]{1,0:T(8,128)(2,1)S(1)} %get-tuple-element.33), channel_id=1, source_target_pairs={{0,1},{1,0},{2,3},{3,2},{4,5},{5,4},{6,7},{7,6},{8,9},{9,8},{10,11... | collective-permute-start | bytes 1572872 | tf_op jit(solution)/shard_map/ppermute | solution.py:299
  10.6 14.6 %copy-start.3 = (bf16[512,1024]{1,0:T(8,128)(2,1)S(1)}, bf16[512,1024]{1,0:T(8,128)(2,1)}, u32[]{:S(2)}) copy-start(bf16[512,1024]{1,0:T(8,128)(2,1)} %cot.1) | copy-start | bytes 3145732
  10.6 14.6 %copy-start.5 = (f32[1,128]{1,0:T(1,128)S(1)}, f32[1,128]{1,0:T(1,128)}, u32[]{:S(2)}) copy-start(f32[1,128]{1,0:T(1,128)} %gain.3) | copy-start | bytes 1540
  10.9 16.9 %copy-start.4 = (f32[1,4,1024]{2,1,0:T(4,128)S(1)}, f32[1,4,1024]{2,1,0:T(4,128)}, u32[]{:S(2)}) copy-start(f32[1,4,1024]{2,1,0:T(4,128)} %param.9) | copy-start | bytes 49156
  10.9 14.3 %collective-permute-start.2 = (bf16[512,512]{1,0:T(8,128)(2,1)S(1)}, bf16[512,512]{1,0:T(8,128)(2,1)S(1)}, u32[]{:S(2)}, u32[]{:S(2)}) collective-permute-start(bf16[512,512]{1,0:T(8,128)(2,1)S(1)} %shard_map.87.own), channel_id=1, source_target_pairs={{0,2},{1,3},{2,0},{3,1},{4,6},{5,7},{6,4},{7,5},{8,10},{9,11},{10,... | collective-permute-start | bytes 1572872 | tf_op jit(solution)/shard_map/ppermute | solution.py:310
  26.0 13.2 %collective-permute-start.3 = (bf16[512,512]{1,0:T(8,128)(2,1)S(1)}, bf16[512,512]{1,0:T(8,128)(2,1)S(1)}, u32[]{:S(2)}, u32[]{:S(2)}) collective-permute-start(bf16[512,512]{1,0:T(8,128)(2,1)S(1)} %get-tuple-element.34.kg.kg_k), channel_id=1, source_target_pairs={{0,1},{1,0},{2,3},{3,2},{4,5},{5,4},{6,7},{7,6},{8,9},{9,8},{10,11... | collective-permute-start | bytes 1572872 | tf_op jit(solution)/shard_map/ppermute | solution.py:324
  27.8 8.4 %collective-permute-start = (f32[4,1024]{1,0:T(4,128)S(1)}, f32[4,1024]{1,0:T(4,128)S(1)}, u32[]{:S(2)}, u32[]{:S(2)}) collective-permute-start(f32[4,1024]{1,0:T(4,128)S(1)} %bitcast.7), channel_id=1, source_target_pairs={{0,4},{4,8},{8,12},{12,16},{16,20},{20,24},{24,28},{28,32},{32,36}... | collective-permute-start | bytes 49160 | tf_op jit(solution)/shard_map/ppermute | solution.py:286
  40.4 6.9 %collective-permute-start.5 = (f32[4,1280]{1,0:T(4,128)S(1)}, f32[4,1280]{1,0:T(4,128)S(1)}, u32[]{:S(2)}, u32[]{:S(2)}) collective-permute-start(f32[4,1280]{1,0:T(4,128)S(1)} %get-tuple-element.36.right), channel_id=1, source_target_pairs={{0,4},{4,8},{8,12},{12,16},{16,20},{20,24},{24,28},{28,32},{32,36}... | collective-permute-start | bytes 61448 | tf_op jit(solution)/shard_map/ppermute | solution.py:338
  40.4 6.9 %collective-permute-start.4 = (f32[4,1280]{1,0:T(4,128)S(1)}, f32[4,1280]{1,0:T(4,128)S(1)}, u32[]{:S(2)}, u32[]{:S(2)}) collective-permute-start(f32[4,1280]{1,0:T(4,128)S(1)} %get-tuple-element.37.left), channel_id=1, source_target_pairs={{0,252},{4,0},{8,4},{12,8},{16,12},{20,16},{24,20},{28,24},{32,28}... | collective-permute-start | bytes 61448 | tf_op jit(solution)/shard_map/ppermute | solution.py:339
  48.6 3.0 %collective-permute-start.6 = (f32[8,1280]{1,0:T(8,128)S(1)}, f32[8,1280]{1,0:T(8,128)S(1)}, u32[]{:S(2)}, u32[]{:S(2)}) collective-permute-start(f32[8,1280]{1,0:T(8,128)S(1)} %get-tuple-element.39.mine), channel_id=1, source_target_pairs={{0,1},{1,0},{2,3},{3,2},{4,5},{5,4},{6,7},{7,6},{8,9},{9,8},{10,11... | collective-permute-start | bytes 122888 | tf_op jit(solution)/shard_map/ppermute | solution.py:360
  51.6 11.5 %collective-permute-start.7 = (f32[8,1152]{1,0:T(8,128)S(1)}, f32[8,1152]{1,0:T(8,128)S(1)}, u32[]{:S(2)}, u32[]{:S(2)}) collective-permute-start(f32[8,1152]{1,0:T(8,128)S(1)} %get-tuple-element.40.total), channel_id=1, source_target_pairs={{0,2},{1,3},{2,0},{3,1},{4,6},{5,7},{6,4},{7,5},{8,10},{9,11},{10,... | collective-permute-start | bytes 110600 | tf_op jit(solution)/shard_map/ppermute | solution.py:368
  54.3 6.8 %collective-permute-start.9 = (f32[4,1024]{1,0:T(4,128)S(1)}, f32[4,1024]{1,0:T(4,128)S(1)}, u32[]{:S(2)}, u32[]{:S(2)}) collective-permute-start(f32[4,1024]{1,0:T(4,128)S(1)} %get-tuple-element.41), channel_id=1, source_target_pairs={{0,6},{1,255},{2,4},{3,253},{4,10},{5,3},{6,8},{7,1},{8,14},{9,7},... | collective-permute-start | bytes 49160 | tf_op jit(solution)/shard_map/ppermute | solution.py:367
  60.2 2.9 %collective-permute-start.8 = (f32[4,1024]{1,0:T(4,128)S(1)}, f32[4,1024]{1,0:T(4,128)S(1)}, u32[]{:S(2)}, u32[]{:S(2)}) collective-permute-start(f32[4,1024]{1,0:T(4,128)S(1)} %get-tuple-element.41), channel_id=1, source_target_pairs={{0,4},{1,253},{2,6},{3,255},{4,8},{5,1},{6,10},{7,3},{8,12},{9,5},... | collective-permute-start | bytes 49160 | tf_op jit(solution)/shard_map/ppermute | solution.py:366
  63.1 4.7 %collective-permute-start.10 = (f32[4,1024]{1,0:T(4,128)S(1)}, f32[4,1024]{1,0:T(4,128)S(1)}, u32[]{:S(2)}, u32[]{:S(2)}) collective-permute-start(f32[4,1024]{1,0:T(4,128)S(1)} %get-tuple-element.46.mine), channel_id=1, source_target_pairs={{0,1},{1,0},{2,3},{3,2},{4,5},{5,4},{6,7},{7,6},{8,9},{9,8},{10,11... | collective-permute-start | bytes 49160 | tf_op jit(solution)/shard_map/ppermute | solution.py:374

commit v2 on v0

v2 whole, which is shorter than its diff:
```python
import functools

import jax
import jax.numpy as jnp
from jax import lax
from jax.experimental import pallas as pl
from jax.experimental.pallas import tpu as pltpu
from jax.sharding import PartitionSpec as P

F32 = jnp.float32
BF16 = jnp.bfloat16
MIB = 1024 * 1024
VM = pl.BlockSpec(memory_space=pltpu.VMEM)
ANY = pl.BlockSpec(memory_space=pl.ANY)
NT = (((1,), (1,)), ((), ()))


def in_vmem(x):
    return pltpu.with_memory_space_constraint(x, pltpu.VMEM)


def in_hbm(x):
    return pltpu.with_memory_space_constraint(x, pltpu.HBM)


def call(body, args, outs, scratch=(), limit=24, nbytes=1, spaces=None, out_spaces=None, aliases=None):
    spaces = spaces or (True,) * len(args)
    out_spaces = out_spaces or (True,) * len(outs)
    return pl.pallas_call(
        body,
        out_shape=[
            pltpu.VMEM(shape, dtype) if inside else pltpu.HBM(shape, dtype)
            for (shape, dtype), inside in zip(outs, out_spaces)
        ],
        in_specs=[VM if inside else ANY for inside in spaces],
        out_specs=[VM if inside else ANY for inside in out_spaces],
        scratch_shapes=list(scratch),
        input_output_aliases=aliases or {},
        compiler_params=pltpu.CompilerParams(vmem_limit_bytes=limit * MIB),
        cost_estimate=pl.CostEstimate(flops=400 * nbytes, bytes_accessed=nbytes, transcendentals=0),
    )(*[in_vmem(a) if inside else in_hbm(a) for a, inside in zip(args, spaces)])


def dot(a, b, dims=(((1,), (0,)), ((), ()))):
    return lax.dot_general(a, b, dims, preferred_element_type=F32)


def split(x):
    hi = x.astype(BF16)
    return hi, (x - hi.astype(F32)).astype(BF16)


def core_index():
    return lax.rem(lax.axis_index("tp"), 2)


def chunk_at(kept, i, wide):
    c = core_index()
    which = c if kept else 1 - c
    return pl.ds(pl.multiple_of(which * (2 * wide) + i * wide, 128), wide)


def half_in(w, to, kept, sems):
    half = to.shape[1]
    steps = sems.shape[0]
    k = to.shape[0] // steps
    c = core_index()
    cols = pl.ds(pl.multiple_of((c if kept else 1 - c) * half, 128), half)
    copies = []
    for j in range(steps):
        at = pl.ds(j * k, k)
        copies.append(pltpu.make_async_copy(w.at[at, cols], to.at[at], sems.at[j]))
        copies[j].start()
    return copies


def partial(tok_v, w_v, hi_v, copies):
    steps = len(copies)
    k = w_v.shape[0] // steps
    acc = None
    for j in range(steps):
        copies[j].wait()
        at = slice(j * k, (j + 1) * k)
        hi = w_v[at].astype(BF16)
        hi_v[at] = hi
        term = dot(tok_v[:, at], hi)
        acc = term if acc is None else acc + term
    return acc


def first_kernel(tok, w, tok_v, w_s, hi_s, part, tok_sem, w_sem):
    tok_copy = pltpu.make_async_copy(tok, tok_v, tok_sem)
    tok_copy.start()
    copies = half_in(w, w_s, False, w_sem)
    tok_copy.wait()
    part[...] = partial(tok_v, w_s, hi_s, copies).astype(BF16)


def own_kernel(tok_v, w, w_k, hi_k, own, w_sem):
    own[...] = partial(tok_v, w_k, hi_k, half_in(w, w_k, True, w_sem))


def chip_sum_kernel(own, got, out0, out1):
    wide = out0.shape[1]
    out0[...] = (own[:, :wide] + got[:, :wide].astype(F32)).astype(BF16)
    out1[...] = (own[:, wide:] + got[:, wide:].astype(F32)).astype(BF16)


def halves_of(vec, left_vec, at):
    hi, lo = split(jnp.concatenate([vec[:, at], left_vec[:, at]], axis=0))
    return jnp.concatenate([hi, lo], axis=0)


def shadow_kernel(tok_v, w_k, w_s, vec, left_vec, _, proj, tok_t):
    wide = w_k.shape[1] // 2
    n = proj.shape[0]
    total = None
    for w, kept, i in ((w_k, True, 0), (w_k, True, 1), (w_s, False, 0), (w_s, False, 1)):
        q = halves_of(vec, left_vec, chunk_at(kept, i, wide))
        w_hi, w_lo = split(w[:, i * wide : (i + 1) * wide])
        both = dot(q, w_hi, NT)
        term = both[:n] + both[n:] + dot(q[:n], w_lo, NT)
        total = term if total is None else total + term
    proj[...] = total
    tok_t[...] = tok_v[...].T


def norm_kernel(scale, i, own, got, cot, gain, vec, left_vec, on_keys_in, gain_in, _, kg, on_keys, gain_grad, passed):
    head = gain.shape[1]
    wide = own.shape[1]
    n = on_keys.shape[0]
    g = gain[...]
    start = chunk_at(True, i, wide).start
    total = gain_in[...]
    for h in range(wide // head):
        cols = slice(h * head, (h + 1) * head)
        keys = (own[:, cols].astype(F32) + got[:, cols].astype(F32)) * scale
        up = cot[:, pl.ds(pl.multiple_of(start + h * head, head), head)].astype(F32)
        gh = up * g
        inv = lax.rsqrt(jnp.mean(keys * keys, axis=-1, keepdims=True) + 1e-6)
        along = jnp.mean(gh * keys, axis=-1, keepdims=True)
        unit = keys * inv
        kg[:, cols] = (inv * (gh - unit * (inv * along))).astype(BF16)
        total = total + jnp.sum(up * unit, axis=0, keepdims=True)
    gain_grad[...] = total
    both = dot(halves_of(vec, left_vec, chunk_at(True, i, wide)), kg[...], NT)
    on_keys[...] = on_keys_in[...] + both[:n] + both[n:]


def odd_replica():
    return lax.rem(lax.axis_index("loop"), 2) == 1


def project_kernel(rate, mine, other, proj0, tok_v, kg_0, kg_1, first, second, out, *passed):
    hi, lo = split(mine[...] + other[...])
    rank = first.shape[0]
    n = 2 * rank
    both = dot(jnp.concatenate([hi, lo], axis=0), tok_v[...])
    proj = proj0[...] - rate * (both[:n] + both[n:])
    out[...] = proj
    odd = odd_replica()
    first[...] = jnp.where(odd, proj[:rank], proj[rank:])
    second[...] = jnp.where(odd, proj[rank:], proj[:rank])


def step_kernel(rate, i, tok_t, kg, w, out, out_hi, out_lo, kg_out):
    wide = kg.shape[1]
    stepped = w[:, i * wide : (i + 1) * wide] - rate * dot(tok_t[...], kg[...])
    out[...] = stepped
    hi, lo = split(stepped)
    out_hi[...] = hi
    out_lo[...] = lo


def input_kernel(scale, kg_k0, kg_k1, kg_s0, kg_s1, hi_k, hi_s, _, out, stage, sem):
    wide = kg_k0.shape[1]
    steps = sem.shape[0]
    k = stage.shape[1] // steps
    copies = []
    for j in range(steps):
        at = slice(j * k, (j + 1) * k)
        total = None
        for kg, hi, i in ((kg_k0, hi_k, 0), (kg_k1, hi_k, 1), (kg_s0, hi_s, 0), (kg_s1, hi_s, 1)):
            term = dot(kg[...], hi[at, i * wide : (i + 1) * wide], NT)
            total = term if total is None else total + term
        stage[:, at] = (total * scale).astype(BF16)
        copies.append(pltpu.make_async_copy(stage.at[:, pl.ds(j * k, k)], out.at[:, pl.ds(j * k, k)], sem.at[j]))
        copies[j].start()
    for j in range(steps):
        copies[j].wait()


def rows_kernel(proj, got_first, got_second, _0, _1, rows_out, gram_out):
    n = proj.shape[0]
    rank = n // 2
    odd = odd_replica()
    got_right = jnp.where(odd, got_first[...], got_second[...])
    got_left = jnp.where(odd, got_second[...], got_first[...])
    rows = jnp.concatenate([proj[:rank] - got_right, got_left - proj[rank:]], axis=0)
    rows_out[...] = rows
    gram = lax.dot_general(rows, rows, NT, precision=lax.Precision.HIGHEST, preferred_element_type=F32)
    gram_out[...] = jnp.concatenate([gram, jnp.zeros((n, 128 - n), F32)], axis=1)


def back_kernel(rows, gram, gain_grad, *refs):
    *blocks, out = refs
    wide = blocks[0].shape[1]
    width = 4 * wide
    n = rows.shape[0]
    r_hi, r_lo = split(rows[...])
    r = jnp.concatenate([r_hi, r_lo], axis=0)
    for j, (kept, i) in enumerate(((True, 0), (True, 1), (False, 0), (False, 1))):
        s_hi, s_lo = blocks[2 * j], blocks[2 * j + 1]
        both = dot(r, s_hi[...])
        out[:, chunk_at(kept, i, wide)] = both[:n] + both[n:] + dot(r_hi, s_lo[...])
    out[:, width : width + 128] = gram[...]
    out[:, width + 128 :] = jnp.broadcast_to(gain_grad[...], (n, 128))


def pair_kernel(mine, other, pair, gain_grad):
    both = mine[...] + other[...]
    width = pair.shape[1]
    pair[...] = both[:, :width]
    gain_grad[...] = both[0:1, width:]


def sum_kernel(mine, other, aside, keep, gram):
    rank, width = aside.shape
    whole = mine[...] + other[...]
    first = core_index() == 0
    aside[...] = jnp.where(first, whole[:rank, :width], whole[rank:, :width])
    keep[...] = jnp.where(first, whole[rank:, :width], whole[:rank, :width])
    gram[...] = whole[:, width:]


def edge_kernel(keep, got, _0, _1, out):
    out[...] = jnp.where(core_index() == 0, got[...] - keep[...], keep[...] - got[...])


def inverse_factor(gram, rank):
    n = gram.shape[0]
    width = gram.shape[1]
    lane = lax.broadcasted_iota(jnp.int32, (rank, width), 1)
    row = lax.broadcasted_iota(jnp.int32, (rank, width), 0)
    parts = []
    for e in range(n // rank):
        a = gram[e * rank : (e + 1) * rank]
        a = jnp.where((lane >= e * rank) & (lane < (e + 1) * rank), a, 0.0)
        a = jnp.where(lane == n + e * rank + row, 1.0, a)
        for i in range(rank):
            col = a[:, e * rank + i : e * rank + i + 1]
            pivot = lax.rsqrt(col[i : i + 1])
            line = a[i : i + 1] * pivot
            a = jnp.where(row == i, line, jnp.where(row > i, a - (col * pivot) * line, a))
        parts.append(a)
    return jnp.concatenate(parts, axis=0)


def apply_inverse(both, x, n):
    total = None
    for j in range(n):
        term = both[:, n + j : n + j + 1] * x[j : j + 1]
        total = term if total is None else total + term
    return total


def whiten_kernel(rank, gram, rows, gain, gain_grad, inverse, lhs, new_gain, stage, sem):
    stage[...] = gain[...] - 0.002 * gain_grad[...]
    copy = pltpu.make_async_copy(stage, new_gain, sem)
    copy.start()
    both = inverse_factor(gram[...], rank)
    inverse[...] = both
    u_hi, u_lo = split(apply_inverse(both, rows[...], 2 * rank))
    lhs[...] = jnp.concatenate([u_hi, u_hi, u_lo, jnp.zeros_like(u_hi)], axis=0).T
    copy.wait()


def mix_kernel(s_k0, s_k1, s_s0, s_s1, inverse, lhs, mine, other, out, new_vec, stage, vec_stage, right_side, sem, vec_sem):
    rank, width = vec_stage.shape
    depth, wide = s_k0.shape
    n = 2 * rank
    first = core_index() == 0
    a, b = mine[...], other[...]
    back = jnp.concatenate([jnp.where(first, b, a), jnp.where(first, a, b)], axis=0)
    nv = apply_inverse(inverse[...], back, n)
    sign = jnp.where(lax.broadcasted_iota(jnp.int32, (n, width), 0) < rank, 1.0 / 3.0, -1.0 / 3.0)
    v_hi, v_lo = split(nv * sign)
    right_side[...] = jnp.concatenate([v_hi, v_lo, v_hi, jnp.zeros_like(v_hi)], axis=0)
    vec_stage[...] = nv[:rank]
    vec_copy = pltpu.make_async_copy(vec_stage, new_vec, vec_sem)
    vec_copy.start()
    parts = sem.shape[0]
    k = depth // parts
    copies = []
    for p in range(parts):
        at = slice(p * k, (p + 1) * k)
        for s, kept, i in ((s_k0, True, 0), (s_k1, True, 1), (s_s0, False, 0), (s_s1, False, 1)):
            cols = chunk_at(kept, i, wide)
            stage[at, cols] = s[at] - dot(lhs[at], right_side[:, cols])
        copies.append(pltpu.make_async_copy(stage.at[pl.ds(p * k, k)], out.at[pl.ds(p * k, k)], sem.at[p]))
        copies[p].start()
    for copy in copies:
        copy.wait()
    vec_copy.wait()


def shards(tokens, weights, gain, cotangent, vectors):
    rows, depth = tokens.shape
    width = weights.shape[2]
    half = width // 2
    wide = half // 2
    rank = vectors.shape[1]
    n = 2 * rank
    tp = lax.axis_size("tp")
    loop = lax.axis_size("loop")
    scale = (depth * tp) ** -0.5
    rate = 0.1 * scale
    weight = weights[0]
    vec = vectors[0]
    core = [(i, i ^ 1) for i in range(tp)]
    chip = [(i, i ^ 2) for i in range(tp)]
    right = [(i, (i + 1) % loop) for i in range(loop)]
    odd_edges = [(i, (i + 1 if i % 2 else i - 1) % loop) for i in range(loop)]
    even_edges = [(i, i ^ 1) for i in range(loop)]
    along = [
        (i * tp + t, ((i + 1) % loop if t % 2 == 0 else (i - 1) % loop) * tp + t) for i in range(loop) for t in range(tp)
    ]
    dma = pltpu.SemaphoreType.DMA
    block, block16, keys16 = ((depth, wide), F32), ((depth, wide), BF16), ((rows, wide), BF16)
    steps = 5

    tok_v, w_s, hi_s, part = call(
        first_kernel,
        (tokens, weight),
        [((rows, depth), BF16), ((depth, half), F32), ((depth, half), BF16), ((rows, half), BF16)],
        [dma, dma((steps,))],
        spaces=(False, False),
    )
    from_core = lax.ppermute(part, "tp", core)
    w_k, hi_k, own = call(
        own_kernel,
        (tok_v, weight),
        [((depth, half), F32), ((depth, half), BF16), ((rows, half), F32)],
        [dma((steps,))],
        spaces=(True, False),
    )
    chip0, chip1 = call(chip_sum_kernel, (own, from_core), [keys16, keys16])
    from_chip0 = lax.ppermute(chip0, "tp", chip)
    from_chip1 = lax.ppermute(chip1, "tp", chip)
    left_vec = lax.ppermute(vec, "loop", right)
    proj0, tok_t = call(
        shadow_kernel,
        (tok_v, w_k, w_s, vec, left_vec, chip1),
        [((n, depth), F32), ((depth, rows), BF16)],
    )

    def norm(i, chip_part, from_chip, on_keys, gain_part, after):
        return call(
            functools.partial(norm_kernel, scale, i),
            (chip_part, from_chip, cotangent, gain, vec, left_vec, on_keys, gain_part, after),
            [keys16, ((n, rows), F32), (gain.shape, F32), (after.shape, after.dtype)],
            aliases={8: 3},
            nbytes=40 * MIB,
        )

    def step(i, kg, w):
        return call(
            functools.partial(step_kernel, rate, i),
            (tok_t, kg, w),
            [block, block16, block16, keys16],
            aliases={1: 3},
        )

    kg_k0, on_keys, gain_part, proj0 = norm(
        0, chip0, from_chip0, jnp.zeros((n, rows), F32), jnp.zeros(gain.shape, F32), proj0
    )
    kg_k1, on_keys, gain_part, kg_k0 = norm(1, chip1, from_chip1, on_keys, gain_part, kg_k0)
    on_keys_s = lax.ppermute(on_keys, "tp", core)
    s_k0, s_hi_k0, s_lo_k0, kg_k0 = step(0, kg_k0, w_k)
    s_k1, s_hi_k1, s_lo_k1, kg_k1 = step(1, kg_k1, w_k)
    first, second, proj, kg_k0, kg_k1 = call(
        functools.partial(project_kernel, rate),
        (on_keys, on_keys_s, proj0, tok_v, kg_k0, kg_k1),
        [((rank, depth), F32), ((rank, depth), F32), ((n, depth), F32), keys16, keys16],
        aliases={4: 3, 5: 4},
    )
    kg_s0 = lax.ppermute(kg_k0, "tp", core)
    kg_s1 = lax.ppermute(kg_k1, "tp", core)
    got_first = lax.ppermute(first, "loop", odd_edges)
    got_second = lax.ppermute(second, "loop", even_edges)
    s_s0, s_hi_s0, s_lo_s0, kg_s0 = step(0, kg_s0, w_s)
    s_s1, s_hi_s1, s_lo_s1, kg_s1 = step(1, kg_s1, w_s)
    edge_rows, gram = call(
        rows_kernel, (proj, got_first, got_second, s_lo_s0, s_lo_s1), [((n, depth), F32), ((n, 128), F32)]
    )
    (payload,) = call(
        back_kernel,
        (edge_rows, gram, gain_part, s_hi_k0, s_lo_k0, s_hi_k1, s_lo_k1, s_hi_s0, s_lo_s0, s_hi_s1, s_lo_s1),
        [((n, width + 256), F32)],
    )
    other_core = lax.ppermute(payload, "tp", core)
    pair, gain_grad = call(pair_kernel, (payload, other_core), [((n, width + 128), F32), (gain.shape, F32)])
    other_chip = lax.ppermute(pair, "tp", chip)
    aside, keep, gram = call(
        sum_kernel, (pair, other_chip), [((rank, width), F32), ((rank, width), F32), ((n, 128), F32)]
    )
    got = lax.ppermute(aside, ("loop", "tp"), along)
    inverse, lhs, new_gain = call(
        functools.partial(whiten_kernel, rank),
        (gram, edge_rows, gain, gain_grad),
        [((n, 128), F32), ((depth, 4 * n), BF16), (gain.shape, F32)],
        [pltpu.VMEM(gain.shape, F32), dma],
        out_spaces=(True, True, False),
    )
    (input_grad,) = call(
        functools.partial(input_kernel, scale),
        (kg_k0, kg_k1, kg_s0, kg_s1, hi_k, hi_s, keep),
        [((rows, depth), BF16)],
        [pltpu.VMEM((rows, depth), BF16), dma((steps,))],
        out_spaces=(False,),
    )
    (mine,) = call(
        edge_kernel, (keep, got, inverse, input_grad), [((rank, width), F32)], spaces=(True, True, True, False)
    )
    other = lax.ppermute(mine, "tp", core)
    parts = 5
    new_weights, new_vec = call(
        mix_kernel,
        (s_k0, s_k1, s_s0, s_s1, inverse, lhs, mine, other),
        [((depth, width), F32), ((rank, width), F32)],
        [
            pltpu.VMEM((depth, width), F32),
            pltpu.VMEM((rank, width), F32),
            pltpu.VMEM((4 * n, width), BF16),
            dma((parts,)),
            dma,
        ],
        out_spaces=(False, False),
    )
    return (new_weights[None], input_grad, new_gain, new_vec[None])


def solution(mesh):
    return jax.shard_map(
        shards,
        mesh=mesh,
        in_specs=(
            P("loop", "tp"),
            P("loop", "tp", None),
            P("loop", None),
            P("loop", None),
            P("loop", None, None),
        ),
        out_specs=(P("loop", "tp", None), P("loop", "tp"), P("loop", None), P("loop", None, None)),
        check_vma=False,
    )
```

time: 187 us -> 59.2 us (0.32)
  waiting for transfers between devices: 79.2 us -> 15 us
  matrix products: 37.2 us -> 0 us
  blocking collectives: 22.4 us -> 0 us
  starting transfers between devices: 5.97 us -> 25.7 us
  local copies, waits for them, and re-layouts: 17.5 us -> 0.03 us
  Pallas kernels: 0 us -> 17.3 us
  between operations: 14.3 us -> 0.94 us
  other arithmetic: 9.35 us -> 0 us
    psum x1 -> x0, waiting for transfers between devices: 64.4 us -> none  [shards(): keys = lax.psum(partial_keys, 'tp')]
    dot_general x11 -> x0, matrix products: 36.7 us -> none  [the longest x2 9.95 us: contract_rank(): lax.dot_general(left, right, (((0,), (0,)), ((), ())), precision=HIGH)]
    psum x2 -> x0, blocking collectives: 22.4 us -> none  [the longest x1 13.2 us: shards(): lax.psum(sum_left.astype(jnp.bfloat16), 'tp').astype(jnp.float32)]
    ppermute x5 -> x13, starting transfers between devices: 5.93 us -> 25.7 us  [the longest x1 7.58 us: shards(): got_first = lax.ppermute(first, 'loop', odd_edges)]
    pallas_call x0 -> x19, Pallas kernels: none -> 17.3 us  [call(): pl.pallas_call(body, out_shape=[pltpu.VMEM(shape, dtype) if inside else p...]
    unnamed x24 -> x6, local copies, waits for them, and re-layouts: 16.1 us -> 0.01 us
    another operation x10 -> x0, other arithmetic: 4.05 us -> none  [the longest x4 1.98 us: lower_solve(): return lax.linalg.triangular_solve(lower, rhs, left_side=True, lower=True)]
    reduce_sum x4 -> x0, other arithmetic: 3.71 us -> none  [the longest x1 1.61 us: norm_back(): jnp.mean(scaled * unit, axis=-1, keepdims=True)]
  transfers between devices with their start and end apart: 6 -> 13, of which waited for: 5 -> 7; matrix products, arithmetic and copies ran while one was open for 9% -> 0% of each run, Pallas kernels for 0% -> 17%
where the time goes in v2:
time: 59.2 us; the launch traced here: 59 us
  starting transfers between devices  25.7 us (43%)
  Pallas kernels  17.3 us (29%)
  waiting for transfers between devices  15 us (25%)
  between operations  0.94 us (2%)
    pallas_call x19, Pallas kernels, call(): pl.pallas_call(body, out_shape=[pltpu.VMEM(shape, dtype) if inside else p...  17.3 us
    ppermute x1, starting transfers between devices, shards(): got_first = lax.ppermute(first, 'loop', odd_edges)  7.58 us
    ppermute x1, waiting for transfers between devices, shards(): left_vec = lax.ppermute(vec, 'loop', right)  7.33 us
    ppermute x1, starting transfers between devices, shards(): got = lax.ppermute(aside, ('loop', 'tp'), along)  4.02 us
    ppermute x1, starting transfers between devices, shards(): from_core = lax.ppermute(part, 'tp', core)  3.33 us
    ppermute x1, waiting for transfers between devices, shards(): from_chip1 = lax.ppermute(chip1, 'tp', chip)  2.53 us
    ppermute x1, starting transfers between devices, shards(): other_chip = lax.ppermute(pair, 'tp', chip)  2.45 us
    ppermute x1, starting transfers between devices, shards(): other = lax.ppermute(mine, 'tp', core)  2.08 us
  transfers between devices with their start and end apart: 13, of which 7 were waited for; matrix products, arithmetic and copies ran while one was open for 0% of the time, Pallas kernels for 17%

profile of v2, /device:TPU:1, one launch (start us, length us, event | category | flops | bytes accessed | tf_op | source)
XLA Modules:
  0.0 59.0 jit_solution(6608047409548904903)
XLA Ops:
  0.6 2.7 %shard_map.84 = (bf16[512,1280]{1,0:T(8,128)(2,1)S(1)}, f32[1280,512]{1,0:T(8,128)S(1)}, bf16[1280,512]{1,0:T(8,128)(2,1)S(1)}, bf16[512,512]{1,0:T(8,128)(2,1)S(1)}) custom-call(bf16[512,1280]{1,0:T(8,128)(2,1)} %tok.1, f32[1280,1024]{1,0:T(8,128)} %bitcast.8), custom_call_target="tpu_custom_call" | custom-call | flops 400 | bytes 1 | tf_op jit(solution)/shard_map/pallas_call | solution.py:29
  3.3 3.3 %collective-permute-start.1 = (bf16[512,512]{1,0:T(8,128)(2,1)S(1)}, bf16[512,512]{1,0:T(8,128)(2,1)S(1)}, u32[]{:S(2)}, u32[]{:S(2)}) collective-permute-start(bf16[512,512]{1,0:T(8,128)(2,1)S(1)} %get-tuple-element.60), channel_id=1, source_target_pairs={{0,1},{1,0},{2,3},{3,2},{4,5},{5,4},{6,7},{7,6},{8,9},{9,8},{10,11... | collective-permute-start | bytes 1572872 | tf_op jit(solution)/shard_map/ppermute | solution.py:339
  6.6 2.2 %shard_map.85 = (f32[1280,512]{1,0:T(8,128)S(1)}, bf16[1280,512]{1,0:T(8,128)(2,1)S(1)}, f32[512,512]{1,0:T(8,128)S(1)}) custom-call(bf16[512,1280]{1,0:T(8,128)(2,1)S(1)} %get-tuple-element.56.tok_v, f32[1280,1024]{1,0:T(8,128)} %bitcast.9), custom_call_target="tpu_custom_call" | custom-call | flops 400 | bytes 1 | tf_op jit(solution)/shard_map/pallas_call | solution.py:29
  8.9 0.0 copy-start
  8.9 0.0 collective-permute-done.1.got
  8.9 0.1 shard_map.86
  9.0 1.1 %collective-permute-start.3 = (bf16[512,256]{1,0:T(8,128)(2,1)S(1)}, bf16[512,256]{1,0:T(8,128)(2,1)S(1)}, u32[]{:S(2)}, u32[]{:S(2)}) collective-permute-start(bf16[512,256]{1,0:T(8,128)(2,1)S(1)} %get-tuple-element.63.own), channel_id=1, source_target_pairs={{0,2},{1,3},{2,0},{3,1},{4,6},{5,7},{6,4},{7,5},{8,10},{9,11},{10,... | collective-permute-start | bytes 786440 | tf_op jit(solution)/shard_map/ppermute | solution.py:348
  10.1 0.0 copy-done
  10.1 1.3 %collective-permute-start = (f32[4,1024]{1,0:T(4,128)S(1)}, f32[4,1024]{1,0:T(4,128)S(1)}, u32[]{:S(2)}, u32[]{:S(2)}) collective-permute-start(f32[4,1024]{1,0:T(4,128)S(1)} %bitcast.4), channel_id=1, source_target_pairs={{0,4},{4,8},{8,12},{12,16},{16,20},{20,24},{24,28},{28,32},{32,36}... | collective-permute-start | bytes 49160 | tf_op jit(solution)/shard_map/ppermute | solution.py:350
  11.4 0.7 %collective-permute-start.2 = (bf16[512,256]{1,0:T(8,128)(2,1)S(1)}, bf16[512,256]{1,0:T(8,128)(2,1)S(1)}, u32[]{:S(2)}, u32[]{:S(2)}) collective-permute-start(bf16[512,256]{1,0:T(8,128)(2,1)S(1)} %get-tuple-element.61._.own), channel_id=1, source_target_pairs={{0,2},{1,3},{2,0},{3,1},{4,6},{5,7},{6,4},{7,5},{8,10},{9,11},{10,... | collective-permute-start | bytes 786440 | tf_op jit(solution)/shard_map/ppermute | solution.py:349
  12.1 7.3 %collective-permute-done.left_vec = f32[4,1024]{1,0:T(4,128)S(1)} collective-permute-done((f32[4,1024]{1,0:T(4,128)S(1)}, f32[4,1024]{1,0:T(4,128)S(1)}, u32[]{:S(2)}, u32[]{:S(2)}) %collective-permute-start) | collective-permute-done | bytes 16416 | tf_op jit(solution)/shard_map/ppermute | solution.py:350
  19.4 0.0 copy-start.1
  19.4 0.0 copy-start.2
  19.4 1.6 %shard_map.87 = (f32[8,1280]{1,0:T(8,128)S(1)}, bf16[1280,512]{1,0:T(8,128)(2,1)S(1)}) custom-call(bf16[512,1280]{1,0:T(8,128)(2,1)S(1)} %get-tuple-element.56.tok_v, f32[1280,512]{1,0:T(8,128)S(1)} %get-tuple-element.57.w_k.w, f32[1280,512]{1,0:T(8,128)S(1)} %get-tuple-element.58.w_s.w, f32[4,1024]{1,0:T(4,128)S(1)} %bitcast.5, ...), custom_call_target="tpu_custom_call" | custom-call | flops 400 | bytes 1 | tf_op jit(solution)/shard_map/pallas_call | solution.py:29
  21.0 0.0 collective-permute-done.3.got
  21.0 0.0 copy-done.1
  21.0 0.0 copy-done.2
  21.0 0.6 shard_map.88
  21.6 2.5 %collective-permute-done.2.got = bf16[512,256]{1,0:T(8,128)(2,1)S(1)} collective-permute-done((bf16[512,256]{1,0:T(8,128)(2,1)S(1)}, bf16[512,256]{1,0:T(8,128)(2,1)S(1)}, u32[]{:S(2)}, u32[]{:S(2)}) %collective-permute-start.2) | collective-permute-done | bytes 262176 | tf_op jit(solution)/shard_map/ppermute | solution.py:349
  24.1 0.6 shard_map.89
  24.7 0.8 %collective-permute-start.4 = (f32[8,512]{1,0:T(8,128)S(1)}, f32[8,512]{1,0:T(8,128)S(1)}, u32[]{:S(2)}, u32[]{:S(2)}) collective-permute-start(f32[8,512]{1,0:T(8,128)S(1)} %get-tuple-element.72.mine), channel_id=1, source_target_pairs={{0,1},{1,0},{2,3},{3,2},{4,5},{5,4},{6,7},{7,6},{8,9},{9,8},{10,11... | collective-permute-start | bytes 49160 | tf_op jit(solution)/shard_map/ppermute | solution.py:378
  25.5 0.5 shard_map.90
  26.0 0.5 shard_map.91
  26.5 0.0 collective-permute-done.4.other
  26.6 0.3 shard_map.92
  26.8 0.2 collective-permute-start.6
  27.1 0.4 collective-permute-start.5
  27.4 7.6 %collective-permute-start.7 = (f32[4,1280]{1,0:T(4,128)S(1)}, f32[4,1280]{1,0:T(4,128)S(1)}, u32[]{:S(2)}, u32[]{:S(2)}) collective-permute-start(f32[4,1280]{1,0:T(4,128)S(1)} %get-tuple-element.81), channel_id=1, source_target_pairs={{0,252},{4,8},{8,4},{12,16},{16,12},{20,24},{24,20},{28,32},{32,28... | collective-permute-start | bytes 61448 | tf_op jit(solution)/shard_map/ppermute | solution.py:389
  35.0 0.0 collective-permute-start.8
  35.0 0.0 collective-permute-done.6.kg
  35.0 0.5 shard_map.94
  35.5 0.0 collective-permute-done.5.kg
  35.5 0.5 shard_map.93
  36.1 0.1 collective-permute-done.7.got_first
  36.2 1.5 %collective-permute-done.8.got_second = f32[4,1280]{1,0:T(4,128)S(1)} collective-permute-done((f32[4,1280]{1,0:T(4,128)S(1)}, f32[4,1280]{1,0:T(4,128)S(1)}, u32[]{:S(2)}, u32[]{:S(2)}) %collective-permute-start.8) | collective-permute-done | bytes 20512 | tf_op jit(solution)/shard_map/ppermute | solution.py:390
  37.6 0.2 shard_map.95
  37.8 0.8 %shard_map.96.mine = f32[8,1280]{1,0:T(8,128)S(1)} custom-call(f32[8,1280]{1,0:T(8,128)S(1)} %get-tuple-element.85.rows, f32[8,128]{1,0:T(8,128)S(1)} %get-tuple-element.86.gram, f32[1,128]{1,0:T(1,128)S(1)} %get-tuple-element.87.gain_grad, bf16[1280,256]{1,0:T(8,128)(2,1)S(1)} %get-tuple-element.88.refs_0_, ...), custom_call_target="tpu_custom_call" | custom-call | flops 400 | bytes 1 | tf_op jit(solution)/shard_map/pallas_call | solution.py:29
  38.6 1.8 %collective-permute-start.9 = (f32[8,1280]{1,0:T(8,128)S(1)}, f32[8,1280]{1,0:T(8,128)S(1)}, u32[]{:S(2)}, u32[]{:S(2)}) collective-permute-start(f32[8,1280]{1,0:T(8,128)S(1)} %shard_map.96.mine), channel_id=1, source_target_pairs={{0,1},{1,0},{2,3},{3,2},{4,5},{5,4},{6,7},{7,6},{8,9},{9,8},{10,11... | collective-permute-start | bytes 122888 | tf_op jit(solution)/shard_map/ppermute | solution.py:401
  40.4 0.9 %collective-permute-done.9.other = f32[8,1280]{1,0:T(8,128)S(1)} collective-permute-done((f32[8,1280]{1,0:T(8,128)S(1)}, f32[8,1280]{1,0:T(8,128)S(1)}, u32[]{:S(2)}, u32[]{:S(2)}) %collective-permute-start.9) | collective-permute-done | bytes 40992 | tf_op jit(solution)/shard_map/ppermute | solution.py:401
  41.3 2.5 %collective-permute-start.10 = (f32[8,1152]{1,0:T(8,128)S(1)}, f32[8,1152]{1,0:T(8,128)S(1)}, u32[]{:S(2)}, u32[]{:S(2)}) collective-permute-start(f32[8,1152]{1,0:T(8,128)S(1)} %get-tuple-element.94.mine), channel_id=1, source_target_pairs={{0,2},{1,3},{2,0},{3,1},{4,6},{5,7},{6,4},{7,5},{8,10},{9,11},{10,... | collective-permute-start | bytes 110600 | tf_op jit(solution)/shard_map/ppermute | solution.py:403
  43.8 1.9 %collective-permute-done.10.other = f32[8,1152]{1,0:T(8,128)S(1)} collective-permute-done((f32[8,1152]{1,0:T(8,128)S(1)}, f32[8,1152]{1,0:T(8,128)S(1)}, u32[]{:S(2)}, u32[]{:S(2)}) %collective-permute-start.10) | collective-permute-done | bytes 36896 | tf_op jit(solution)/shard_map/ppermute | solution.py:403
  45.6 4.0 %collective-permute-start.11 = (f32[4,1024]{1,0:T(4,128)S(1)}, f32[4,1024]{1,0:T(4,128)S(1)}, u32[]{:S(2)}, u32[]{:S(2)}) collective-permute-start(f32[4,1024]{1,0:T(4,128)S(1)} %get-tuple-element.100), channel_id=1, source_target_pairs={{0,4},{1,253},{2,6},{3,255},{4,8},{5,1},{6,10},{7,3},{8,12},{9,5},... | collective-permute-start | bytes 49160 | tf_op jit(solution)/shard_map/ppermute | solution.py:407
  49.7 1.0 %shard_map.99 = (f32[8,128]{1,0:T(8,128)S(1)}, bf16[1280,32]{1,0:T(8,128)(2,1)S(1)}, f32[1,128]{1,0:T(1,128)}) custom-call(f32[8,128]{1,0:T(8,128)S(1)} %get-tuple-element.95.gram, f32[8,1280]{1,0:T(8,128)S(1)} %get-tuple-element.85.rows, f32[1,128]{1,0:T(1,128)S(1)} %copy-done.1, f32[1,128]{1,0:T(1,128)S(1)} %get-tuple-element.96.gain_grad), custom_call_target="tpu_custom_call" | custom-call | flops 400 | bytes 1 | tf_op jit(solution)/shard_map/pallas_call | solution.py:29
  50.7 2.4 %shard_map.100._1 = bf16[512,1280]{1,0:T(8,128)(2,1)} custom-call(bf16[512,256]{1,0:T(8,128)(2,1)S(1)} %get-tuple-element.76.kg_k0, bf16[512,256]{1,0:T(8,128)(2,1)S(1)} %get-tuple-element.78.kg_k1, bf16[512,256]{1,0:T(8,128)(2,1)S(1)} %get-tuple-element.101.kg_s0, bf16[512,256]{1,0:T(8,128)(2,1)S(1)} %get-tuple-element.102.kg_s1, ...), custom_call_target="tpu_custom_call" | custom-call | flops 400 | bytes 1 | tf_op jit(solution)/shard_map/pallas_call | solution.py:29
  53.1 0.0 collective-permute-done.11.got
  53.1 2.1 %collective-permute-start.12 = (f32[4,1024]{1,0:T(4,128)S(1)}, f32[4,1024]{1,0:T(4,128)S(1)}, u32[]{:S(2)}, u32[]{:S(2)}) collective-permute-start(f32[4,1024]{1,0:T(4,128)S(1)} %shard_map.101.mine), channel_id=1, source_target_pairs={{0,1},{1,0},{2,3},{3,2},{4,5},{5,4},{6,7},{7,6},{8,9},{9,8},{10,11... | collective-permute-start | bytes 49160 | tf_op jit(solution)/shard_map/ppermute | solution.py:425
  55.2 0.8 %collective-permute-done.12.other = f32[4,1024]{1,0:T(4,128)S(1)} collective-permute-done((f32[4,1024]{1,0:T(4,128)S(1)}, f32[4,1024]{1,0:T(4,128)S(1)}, u32[]{:S(2)}, u32[]{:S(2)}) %collective-permute-start.12) | collective-permute-done | bytes 16416 | tf_op jit(solution)/shard_map/ppermute | solution.py:425
  56.0 2.8 %shard_map.102 = (f32[1280,1024]{1,0:T(8,128)}, f32[4,1024]{1,0:T(4,128)}) custom-call(f32[1280,256]{1,0:T(8,128)S(1)} %get-tuple-element.69.s_k0, f32[1280,256]{1,0:T(8,128)S(1)} %get-tuple-element.71.s_k1, f32[1280,256]{1,0:T(8,128)S(1)} %get-tuple-element.77.s_s0, f32[1280,256]{1,0:T(8,128)S(1)} %get-tuple-element.79.s_s1, ...), custom_call_target="tpu_custom_call" | custom-call | flops 400 | bytes 1 | tf_op jit(solution)/shard_map/pallas_call | solution.py:29
  (5 shorter events, 0.0 us)
Async XLA Ops:
  3.3 5.6 %collective-permute-start.1 = (bf16[512,512]{1,0:T(8,128)(2,1)S(1)}, bf16[512,512]{1,0:T(8,128)(2,1)S(1)}, u32[]{:S(2)}, u32[]{:S(2)}) collective-permute-start(bf16[512,512]{1,0:T(8,128)(2,1)S(1)} %get-tuple-element.60), channel_id=1, source_target_pairs={{0,1},{1,0},{2,3},{3,2},{4,5},{5,4},{6,7},{7,6},{8,9},{9,8},{10,11... | collective-permute-start | bytes 1572872 | tf_op jit(solution)/shard_map/ppermute | solution.py:339
  8.9 1.2 %copy-start = (f32[1,4,1024]{2,1,0:T(4,128)S(1)}, f32[1,4,1024]{2,1,0:T(4,128)}, u32[]{:S(2)}) copy-start(f32[1,4,1024]{2,1,0:T(4,128)} %param.9) | copy-start | bytes 49156
  9.0 12.0 %collective-permute-start.3 = (bf16[512,256]{1,0:T(8,128)(2,1)S(1)}, bf16[512,256]{1,0:T(8,128)(2,1)S(1)}, u32[]{:S(2)}, u32[]{:S(2)}) collective-permute-start(bf16[512,256]{1,0:T(8,128)(2,1)S(1)} %get-tuple-element.63.own), channel_id=1, source_target_pairs={{0,2},{1,3},{2,0},{3,1},{4,6},{5,7},{6,4},{7,5},{8,10},{9,11},{10,... | collective-permute-start | bytes 786440 | tf_op jit(solution)/shard_map/ppermute | solution.py:348
  10.1 9.3 %collective-permute-start = (f32[4,1024]{1,0:T(4,128)S(1)}, f32[4,1024]{1,0:T(4,128)S(1)}, u32[]{:S(2)}, u32[]{:S(2)}) collective-permute-start(f32[4,1024]{1,0:T(4,128)S(1)} %bitcast.4), channel_id=1, source_target_pairs={{0,4},{4,8},{8,12},{12,16},{16,20},{20,24},{24,28},{28,32},{32,36}... | collective-permute-start | bytes 49160 | tf_op jit(solution)/shard_map/ppermute | solution.py:350
  11.4 12.7 %collective-permute-start.2 = (bf16[512,256]{1,0:T(8,128)(2,1)S(1)}, bf16[512,256]{1,0:T(8,128)(2,1)S(1)}, u32[]{:S(2)}, u32[]{:S(2)}) collective-permute-start(bf16[512,256]{1,0:T(8,128)(2,1)S(1)} %get-tuple-element.61._.own), channel_id=1, source_target_pairs={{0,2},{1,3},{2,0},{3,1},{4,6},{5,7},{6,4},{7,5},{8,10},{9,11},{10,... | collective-permute-start | bytes 786440 | tf_op jit(solution)/shard_map/ppermute | solution.py:349
  19.4 1.6 %copy-start.1 = (f32[1,128]{1,0:T(1,128)S(1)}, f32[1,128]{1,0:T(1,128)}, u32[]{:S(2)}) copy-start(f32[1,128]{1,0:T(1,128)} %gain.5) | copy-start | bytes 1540
  19.4 1.6 %copy-start.2 = (bf16[512,1024]{1,0:T(8,128)(2,1)S(1)}, bf16[512,1024]{1,0:T(8,128)(2,1)}, u32[]{:S(2)}) copy-start(bf16[512,1024]{1,0:T(8,128)(2,1)} %cot.3) | copy-start | bytes 3145732
  24.7 1.8 %collective-permute-start.4 = (f32[8,512]{1,0:T(8,128)S(1)}, f32[8,512]{1,0:T(8,128)S(1)}, u32[]{:S(2)}, u32[]{:S(2)}) collective-permute-start(f32[8,512]{1,0:T(8,128)S(1)} %get-tuple-element.72.mine), channel_id=1, source_target_pairs={{0,1},{1,0},{2,3},{3,2},{4,5},{5,4},{6,7},{7,6},{8,9},{9,8},{10,11... | collective-permute-start | bytes 49160 | tf_op jit(solution)/shard_map/ppermute | solution.py:378
  26.8 8.2 %collective-permute-start.6 = (bf16[512,256]{1,0:T(8,128)(2,1)S(1)}, bf16[512,256]{1,0:T(8,128)(2,1)S(1)}, u32[]{:S(2)}, u32[]{:S(2)}) collective-permute-start(bf16[512,256]{1,0:T(8,128)(2,1)S(1)} %get-tuple-element.78.kg_k1), channel_id=1, source_target_pairs={{0,1},{1,0},{2,3},{3,2},{4,5},{5,4},{6,7},{7,6},{8,9},{9,8},{10,11... | collective-permute-start | bytes 786440 | tf_op jit(solution)/shard_map/ppermute | solution.py:388
  27.1 8.5 %collective-permute-start.5 = (bf16[512,256]{1,0:T(8,128)(2,1)S(1)}, bf16[512,256]{1,0:T(8,128)(2,1)S(1)}, u32[]{:S(2)}, u32[]{:S(2)}) collective-permute-start(bf16[512,256]{1,0:T(8,128)(2,1)S(1)} %get-tuple-element.76.kg_k0), channel_id=1, source_target_pairs={{0,1},{1,0},{2,3},{3,2},{4,5},{5,4},{6,7},{7,6},{8,9},{9,8},{10,11... | collective-permute-start | bytes 786440 | tf_op jit(solution)/shard_map/ppermute | solution.py:387
  27.4 8.7 %collective-permute-start.7 = (f32[4,1280]{1,0:T(4,128)S(1)}, f32[4,1280]{1,0:T(4,128)S(1)}, u32[]{:S(2)}, u32[]{:S(2)}) collective-permute-start(f32[4,1280]{1,0:T(4,128)S(1)} %get-tuple-element.81), channel_id=1, source_target_pairs={{0,252},{4,8},{8,4},{12,16},{16,12},{20,24},{24,20},{28,32},{32,28... | collective-permute-start | bytes 61448 | tf_op jit(solution)/shard_map/ppermute | solution.py:389
  35.0 2.6 %collective-permute-start.8 = (f32[4,1280]{1,0:T(4,128)S(1)}, f32[4,1280]{1,0:T(4,128)S(1)}, u32[]{:S(2)}, u32[]{:S(2)}) collective-permute-start(f32[4,1280]{1,0:T(4,128)S(1)} %get-tuple-element.82), channel_id=1, source_target_pairs={{0,4},{4,0},{8,12},{12,8},{16,20},{20,16},{24,28},{28,24},{32,36},... | collective-permute-start | bytes 61448 | tf_op jit(solution)/shard_map/ppermute | solution.py:390
  38.6 2.7 %collective-permute-start.9 = (f32[8,1280]{1,0:T(8,128)S(1)}, f32[8,1280]{1,0:T(8,128)S(1)}, u32[]{:S(2)}, u32[]{:S(2)}) collective-permute-start(f32[8,1280]{1,0:T(8,128)S(1)} %shard_map.96.mine), channel_id=1, source_target_pairs={{0,1},{1,0},{2,3},{3,2},{4,5},{5,4},{6,7},{7,6},{8,9},{9,8},{10,11... | collective-permute-start | bytes 122888 | tf_op jit(solution)/shard_map/ppermute | solution.py:401
  41.3 4.3 %collective-permute-start.10 = (f32[8,1152]{1,0:T(8,128)S(1)}, f32[8,1152]{1,0:T(8,128)S(1)}, u32[]{:S(2)}, u32[]{:S(2)}) collective-permute-start(f32[8,1152]{1,0:T(8,128)S(1)} %get-tuple-element.94.mine), channel_id=1, source_target_pairs={{0,2},{1,3},{2,0},{3,1},{4,6},{5,7},{6,4},{7,5},{8,10},{9,11},{10,... | collective-permute-start | bytes 110600 | tf_op jit(solution)/shard_map/ppermute | solution.py:403
  45.6 7.4 %collective-permute-start.11 = (f32[4,1024]{1,0:T(4,128)S(1)}, f32[4,1024]{1,0:T(4,128)S(1)}, u32[]{:S(2)}, u32[]{:S(2)}) collective-permute-start(f32[4,1024]{1,0:T(4,128)S(1)} %get-tuple-element.100), channel_id=1, source_target_pairs={{0,4},{1,253},{2,6},{3,255},{4,8},{5,1},{6,10},{7,3},{8,12},{9,5},... | collective-permute-start | bytes 49160 | tf_op jit(solution)/shard_map/ppermute | solution.py:407
  53.1 2.9 %collective-permute-start.12 = (f32[4,1024]{1,0:T(4,128)S(1)}, f32[4,1024]{1,0:T(4,128)S(1)}, u32[]{:S(2)}, u32[]{:S(2)}) collective-permute-start(f32[4,1024]{1,0:T(4,128)S(1)} %shard_map.101.mine), channel_id=1, source_target_pairs={{0,1},{1,0},{2,3},{3,2},{4,5},{5,4},{6,7},{7,6},{8,9},{9,8},{10,11... | collective-permute-start | bytes 49160 | tf_op jit(solution)/shard_map/ppermute | solution.py:425

commit v3 on v2

--- a/solution.py
+++ b/solution.py
@@ -151,7 +151,7 @@
     return lax.rem(lax.axis_index("loop"), 2) == 1
 
 
-def project_kernel(rate, mine, other, proj0, tok_v, kg_0, kg_1, first, second, out, *passed):
+def project_kernel(rate, mine, other, proj0, tok_v, first, second, out):
     hi, lo = split(mine[...] + other[...])
     rank = first.shape[0]
     n = 2 * rank
@@ -163,7 +163,7 @@
     second[...] = jnp.where(odd, proj[rank:], proj[:rank])
 
 
-def step_kernel(rate, i, tok_t, kg, w, out, out_hi, out_lo, kg_out):
+def step_kernel(rate, i, tok_t, kg, w, out, out_hi, out_lo):
     wide = kg.shape[1]
     stepped = w[:, i * wide : (i + 1) * wide] - rate * dot(tok_t[...], kg[...])
     out[...] = stepped
@@ -190,7 +190,7 @@
         copies[j].wait()
 
 
-def rows_kernel(proj, got_first, got_second, _0, _1, rows_out, gram_out):
+def rows_kernel(proj, got_first, got_second, _0, _1, _2, _3, rows_out, gram_out):
     n = proj.shape[0]
     rank = n // 2
     odd = odd_replica()
@@ -217,24 +217,20 @@
     out[:, width + 128 :] = jnp.broadcast_to(gain_grad[...], (n, 128))
 
 
-def pair_kernel(mine, other, pair, gain_grad):
+def pair_kernel(mine, other, pair, aside, gain_grad):
+    rank, width = aside.shape
     both = mine[...] + other[...]
-    width = pair.shape[1]
-    pair[...] = both[:, :width]
-    gain_grad[...] = both[0:1, width:]
-
-
-def sum_kernel(mine, other, aside, keep, gram):
-    rank, width = aside.shape
-    whole = mine[...] + other[...]
-    first = core_index() == 0
-    aside[...] = jnp.where(first, whole[:rank, :width], whole[rank:, :width])
-    keep[...] = jnp.where(first, whole[rank:, :width], whole[:rank, :width])
+    pair[...] = both[:, : width + 128]
+    aside[...] = jnp.where(core_index() == 0, both[:rank, :width], both[rank:, :width])
+    gain_grad[...] = both[0:1, width + 128 :]
+
+
+def edge_kernel(pair, other, near, far, _, out, gram):
+    rank, width = out.shape
+    whole = pair[...] + other[...]
+    beyond = near[...] + far[...]
+    out[...] = jnp.where(core_index() == 0, beyond - whole[rank:, :width], whole[:rank, :width] - beyond)
     gram[...] = whole[:, width:]
-
-
-def edge_kernel(keep, got, _0, _1, out):
-    out[...] = jnp.where(core_index() == 0, got[...] - keep[...], keep[...] - got[...])
 
 
 def inverse_factor(gram, rank):
@@ -325,6 +321,7 @@
     along = [
         (i * tp + t, ((i + 1) % loop if t % 2 == 0 else (i - 1) % loop) * tp + t) for i in range(loop) for t in range(tp)
     ]
+    along_far = [(i, j ^ 2) for i, j in along]
     dma = pltpu.SemaphoreType.DMA
     block, block16, keys16 = ((depth, wide), F32), ((depth, wide), BF16), ((rows, wide), BF16)
     steps = 5
@@ -360,15 +357,14 @@
             (chip_part, from_chip, cotangent, gain, vec, left_vec, on_keys, gain_part, after),
             [keys16, ((n, rows), F32), (gain.shape, F32), (after.shape, after.dtype)],
             aliases={8: 3},
-            nbytes=40 * MIB,
+            nbytes=40 * MIB if i == 0 else 1,
         )
 
     def step(i, kg, w):
         return call(
             functools.partial(step_kernel, rate, i),
             (tok_t, kg, w),
-            [block, block16, block16, keys16],
-            aliases={1: 3},
+            [block, block16, block16],
         )
 
     kg_k0, on_keys, gain_part, proj0 = norm(
@@ -376,22 +372,24 @@
     )
     kg_k1, on_keys, gain_part, kg_k0 = norm(1, chip1, from_chip1, on_keys, gain_part, kg_k0)
     on_keys_s = lax.ppermute(on_keys, "tp", core)
-    s_k0, s_hi_k0, s_lo_k0, kg_k0 = step(0, kg_k0, w_k)
-    s_k1, s_hi_k1, s_lo_k1, kg_k1 = step(1, kg_k1, w_k)
-    first, second, proj, kg_k0, kg_k1 = call(
-        functools.partial(project_kernel, rate),
-        (on_keys, on_keys_s, proj0, tok_v, kg_k0, kg_k1),
-        [((rank, depth), F32), ((rank, depth), F32), ((n, depth), F32), keys16, keys16],
-        aliases={4: 3, 5: 4},
-    )
+    s_k0, s_hi_k0, s_lo_k0 = step(0, kg_k0, w_k)
+    s_k1, s_hi_k1, s_lo_k1 = step(1, kg_k1, w_k)
     kg_s0 = lax.ppermute(kg_k0, "tp", core)
     kg_s1 = lax.ppermute(kg_k1, "tp", core)
+    first, second, proj = call(
+        functools.partial(project_kernel, rate),
+        (on_keys, on_keys_s, proj0, tok_v),
+        [((rank, depth), F32), ((rank, depth), F32), ((n, depth), F32)],
+        nbytes=40 * MIB,
+    )
     got_first = lax.ppermute(first, "loop", odd_edges)
     got_second = lax.ppermute(second, "loop", even_edges)
-    s_s0, s_hi_s0, s_lo_s0, kg_s0 = step(0, kg_s0, w_s)
-    s_s1, s_hi_s1, s_lo_s1, kg_s1 = step(1, kg_s1, w_s)
+    s_s0, s_hi_s0, s_lo_s0 = step(0, kg_s0, w_s)
+    s_s1, s_hi_s1, s_lo_s1 = step(1, kg_s1, w_s)
     edge_rows, gram = call(
-        rows_kernel, (proj, got_first, got_second, s_lo_s0, s_lo_s1), [((n, depth), F32), ((n, 128), F32)]
+        rows_kernel,
+        (proj, got_first, got_second, s_lo_k0, s_lo_k1, s_lo_s0, s_lo_s1),
+        [((n, depth), F32), ((n, 128), F32)],
     )
     (payload,) = call(
         back_kernel,
@@ -399,12 +397,29 @@
         [((n, width + 256), F32)],
     )
     other_core = lax.ppermute(payload, "tp", core)
-    pair, gain_grad = call(pair_kernel, (payload, other_core), [((n, width + 128), F32), (gain.shape, F32)])
+    pair, aside, gain_grad = call(
+        pair_kernel,
+        (payload, other_core),
+        [((n, width + 128), F32), ((rank, width), F32), (gain.shape, F32)],
+    )
+    everyone = ("loop", "tp")
+    near = lax.ppermute(aside, everyone, along)
+    far = lax.ppermute(aside, everyone, along_far)
     other_chip = lax.ppermute(pair, "tp", chip)
-    aside, keep, gram = call(
-        sum_kernel, (pair, other_chip), [((rank, width), F32), ((rank, width), F32), ((n, 128), F32)]
-    )
-    got = lax.ppermute(aside, ("loop", "tp"), along)
+    (input_grad,) = call(
+        functools.partial(input_kernel, scale),
+        (kg_k0, kg_k1, kg_s0, kg_s1, hi_k, hi_s, aside),
+        [((rows, depth), BF16)],
+        [pltpu.VMEM((rows, depth), BF16), dma((steps,))],
+        out_spaces=(False,),
+    )
+    mine, gram = call(
+        edge_kernel,
+        (pair, other_chip, near, far, input_grad),
+        [((rank, width), F32), ((n, 128), F32)],
+        spaces=(True, True, True, True, False),
+    )
+    other = lax.ppermute(mine, "tp", core)
     inverse, lhs, new_gain = call(
         functools.partial(whiten_kernel, rank),
         (gram, edge_rows, gain, gain_grad),
@@ -412,18 +427,7 @@
         [pltpu.VMEM(gain.shape, F32), dma],
         out_spaces=(True, True, False),
     )
-    (input_grad,) = call(
-        functools.partial(input_kernel, scale),
-        (kg_k0, kg_k1, kg_s0, kg_s1, hi_k, hi_s, keep),
-        [((rows, depth), BF16)],
-        [pltpu.VMEM((rows, depth), BF16), dma((steps,))],
-        out_spaces=(False,),
-    )
-    (mine,) = call(
-        edge_kernel, (keep, got, inverse, input_grad), [((rank, width), F32)], spaces=(True, True, True, False)
-    )
-    other = lax.ppermute(mine, "tp", core)
-    parts = 5
+    parts = 10
     new_weights, new_vec = call(
         mix_kernel,
         (s_k0, s_k1, s_s0, s_s1, inverse, lhs, mine, other),

time: 59.2 us -> 57.3 us (0.968)
  waiting for transfers between devices: 15 us -> 12.1 us
  starting transfers between devices: 25.7 us -> 26.9 us
    ppermute x1, waiting for transfers between devices: 1.86 us -> 0.01 us  [shards(): other_chip = lax.ppermute(pair, 'tp', chip)]
    ppermute x1, starting transfers between devices: 2.08 us -> 3.12 us  [shards(): other = lax.ppermute(mine, 'tp', core)]
    ppermute x1, waiting for transfers between devices: 1.46 us -> 0.55 us  [shards(): got_second = lax.ppermute(second, 'loop', even_edges)]
    ppermute x1, waiting for transfers between devices: 0.84 us -> 0.01 us  [shards(): other = lax.ppermute(mine, 'tp', core)]
    ppermute x1 -> x2, starting transfers between devices: 4.02 us -> 3.89 us  [the longest x1 3.88 us: shards(): far = lax.ppermute(aside, everyone, along_far)]
    pallas_call x19 -> x18, Pallas kernels: 17.3 us -> 17.2 us  [call(): pl.pallas_call(body, out_shape=[pltpu.VMEM(shape, dtype) if inside else p...]
  transfers between devices with their start and end apart: 13 -> 14, of which waited for: 7 -> 6; matrix products, arithmetic and copies ran while one was open for 0% -> 0% of each run, Pallas kernels for 17% -> 18%
where the time goes in v3:
time: 57.3 us; the launch traced here: 57.2 us
  starting transfers between devices  26.9 us (47%)
  Pallas kernels  17.2 us (30%)
  waiting for transfers between devices  12.1 us (21%)
  between operations  0.96 us (2%)
    pallas_call x18, Pallas kernels, call(): pl.pallas_call(body, out_shape=[pltpu.VMEM(shape, dtype) if inside else p...  17.2 us
    ppermute x1, starting transfers between devices, shards(): got_first = lax.ppermute(first, 'loop', odd_edges)  7.65 us
    ppermute x1, waiting for transfers between devices, shards(): left_vec = lax.ppermute(vec, 'loop', right)  7.33 us
    ppermute x1, starting transfers between devices, shards(): far = lax.ppermute(aside, everyone, along_far)  3.88 us
    ppermute x1, starting transfers between devices, shards(): from_core = lax.ppermute(part, 'tp', core)  3.33 us
    ppermute x1, starting transfers between devices, shards(): other = lax.ppermute(mine, 'tp', core)  3.12 us
    ppermute x1, waiting for transfers between devices, shards(): from_chip1 = lax.ppermute(chip1, 'tp', chip)  2.55 us
    ppermute x1, starting transfers between devices, shards(): other_chip = lax.ppermute(pair, 'tp', chip)  2.54 us
  transfers between devices with their start and end apart: 14, of which 6 were waited for; matrix products, arithmetic and copies ran while one was open for 0% of the time, Pallas kernels for 18%

profile of v3, /device:TPU:1, one launch (start us, length us, event | category | flops | bytes accessed | tf_op | source)
XLA Modules:
  0.0 57.2 jit_solution(8766014890475669467)
XLA Ops:
  0.6 2.7 %shard_map.84 = (bf16[512,1280]{1,0:T(8,128)(2,1)S(1)}, f32[1280,512]{1,0:T(8,128)S(1)}, bf16[1280,512]{1,0:T(8,128)(2,1)S(1)}, bf16[512,512]{1,0:T(8,128)(2,1)S(1)}) custom-call(bf16[512,1280]{1,0:T(8,128)(2,1)} %tok.1, f32[1280,1024]{1,0:T(8,128)} %bitcast.8), custom_call_target="tpu_custom_call" | custom-call | flops 400 | bytes 1 | tf_op jit(solution)/shard_map/pallas_call | solution.py:29
  3.3 3.3 %collective-permute-start.1 = (bf16[512,512]{1,0:T(8,128)(2,1)S(1)}, bf16[512,512]{1,0:T(8,128)(2,1)S(1)}, u32[]{:S(2)}, u32[]{:S(2)}) collective-permute-start(bf16[512,512]{1,0:T(8,128)(2,1)S(1)} %get-tuple-element.54), channel_id=1, source_target_pairs={{0,1},{1,0},{2,3},{3,2},{4,5},{5,4},{6,7},{7,6},{8,9},{9,8},{10,11... | collective-permute-start | bytes 1572872 | tf_op jit(solution)/shard_map/ppermute | solution.py:336
  6.6 2.2 %shard_map.85 = (f32[1280,512]{1,0:T(8,128)S(1)}, bf16[1280,512]{1,0:T(8,128)(2,1)S(1)}, f32[512,512]{1,0:T(8,128)S(1)}) custom-call(bf16[512,1280]{1,0:T(8,128)(2,1)S(1)} %get-tuple-element.50.tok_v, f32[1280,1024]{1,0:T(8,128)} %bitcast.9), custom_call_target="tpu_custom_call" | custom-call | flops 400 | bytes 1 | tf_op jit(solution)/shard_map/pallas_call | solution.py:29
  8.9 0.0 copy-start.1
  8.9 0.0 collective-permute-done.1.got
  8.9 0.1 shard_map.86
  9.0 1.1 %collective-permute-start.3 = (bf16[512,256]{1,0:T(8,128)(2,1)S(1)}, bf16[512,256]{1,0:T(8,128)(2,1)S(1)}, u32[]{:S(2)}, u32[]{:S(2)}) collective-permute-start(bf16[512,256]{1,0:T(8,128)(2,1)S(1)} %get-tuple-element.57.own), channel_id=1, source_target_pairs={{0,2},{1,3},{2,0},{3,1},{4,6},{5,7},{6,4},{7,5},{8,10},{9,11},{10,... | collective-permute-start | bytes 786440 | tf_op jit(solution)/shard_map/ppermute | solution.py:345
  10.1 0.0 copy-done.1
  10.1 1.3 %collective-permute-start = (f32[4,1024]{1,0:T(4,128)S(1)}, f32[4,1024]{1,0:T(4,128)S(1)}, u32[]{:S(2)}, u32[]{:S(2)}) collective-permute-start(f32[4,1024]{1,0:T(4,128)S(1)} %bitcast.4), channel_id=1, source_target_pairs={{0,4},{4,8},{8,12},{12,16},{16,20},{20,24},{24,28},{28,32},{32,36}... | collective-permute-start | bytes 49160 | tf_op jit(solution)/shard_map/ppermute | solution.py:347
  11.4 0.7 %collective-permute-start.2 = (bf16[512,256]{1,0:T(8,128)(2,1)S(1)}, bf16[512,256]{1,0:T(8,128)(2,1)S(1)}, u32[]{:S(2)}, u32[]{:S(2)}) collective-permute-start(bf16[512,256]{1,0:T(8,128)(2,1)S(1)} %get-tuple-element.55._.own), channel_id=1, source_target_pairs={{0,2},{1,3},{2,0},{3,1},{4,6},{5,7},{6,4},{7,5},{8,10},{9,11},{10,... | collective-permute-start | bytes 786440 | tf_op jit(solution)/shard_map/ppermute | solution.py:346
  12.1 7.3 %collective-permute-done.left_vec = f32[4,1024]{1,0:T(4,128)S(1)} collective-permute-done((f32[4,1024]{1,0:T(4,128)S(1)}, f32[4,1024]{1,0:T(4,128)S(1)}, u32[]{:S(2)}, u32[]{:S(2)}) %collective-permute-start) | collective-permute-done | bytes 16416 | tf_op jit(solution)/shard_map/ppermute | solution.py:347
  19.4 1.6 %shard_map.87 = (f32[8,1280]{1,0:T(8,128)S(1)}, bf16[1280,512]{1,0:T(8,128)(2,1)S(1)}) custom-call(bf16[512,1280]{1,0:T(8,128)(2,1)S(1)} %get-tuple-element.50.tok_v, f32[1280,512]{1,0:T(8,128)S(1)} %get-tuple-element.51.w_k.w, f32[1280,512]{1,0:T(8,128)S(1)} %get-tuple-element.52.w_s.w, f32[4,1024]{1,0:T(4,128)S(1)} %bitcast.5, ...), custom_call_target="tpu_custom_call" | custom-call | flops 400 | bytes 1 | tf_op jit(solution)/shard_map/pallas_call | solution.py:29
  21.0 0.0 collective-permute-done.3.got
  21.0 0.0 copy-done
  21.0 0.0 copy-done.2
  21.0 0.6 shard_map.88
  21.6 2.5 %collective-permute-done.2.got = bf16[512,256]{1,0:T(8,128)(2,1)S(1)} collective-permute-done((bf16[512,256]{1,0:T(8,128)(2,1)S(1)}, bf16[512,256]{1,0:T(8,128)(2,1)S(1)}, u32[]{:S(2)}, u32[]{:S(2)}) %collective-permute-start.2) | collective-permute-done | bytes 262176 | tf_op jit(solution)/shard_map/ppermute | solution.py:346
  24.1 0.6 shard_map.89
  24.7 0.8 %collective-permute-start.6 = (f32[8,512]{1,0:T(8,128)S(1)}, f32[8,512]{1,0:T(8,128)S(1)}, u32[]{:S(2)}, u32[]{:S(2)}) collective-permute-start(f32[8,512]{1,0:T(8,128)S(1)} %get-tuple-element.68.mine), channel_id=1, source_target_pairs={{0,1},{1,0},{2,3},{3,2},{4,5},{5,4},{6,7},{7,6},{8,9},{9,8},{10,11... | collective-permute-start | bytes 49160 | tf_op jit(solution)/shard_map/ppermute | solution.py:374
  25.5 0.1 collective-permute-start.4
  25.6 0.4 collective-permute-start.5
  26.0 0.3 collective-permute-done.6.other
  26.4 0.3 shard_map.94
  26.6 7.7 %collective-permute-start.7 = (f32[4,1280]{1,0:T(4,128)S(1)}, f32[4,1280]{1,0:T(4,128)S(1)}, u32[]{:S(2)}, u32[]{:S(2)}) collective-permute-start(f32[4,1280]{1,0:T(4,128)S(1)} %get-tuple-element.71), channel_id=1, source_target_pairs={{0,252},{4,8},{8,4},{12,16},{16,12},{20,24},{24,20},{28,32},{32,28... | collective-permute-start | bytes 61448 | tf_op jit(solution)/shard_map/ppermute | solution.py:385
  34.3 0.0 collective-permute-start.8
  34.3 0.5 shard_map.90
  34.8 0.5 shard_map.91
  35.3 0.0 collective-permute-done.5.kg.kg_s1
  35.3 0.5 shard_map.93
  35.8 0.0 collective-permute-done.4.kg.kg_s0
  35.9 0.5 shard_map.92
  36.4 0.0 collective-permute-done.7.got_first
  36.4 0.5 collective-permute-done.8.got_second
  36.9 0.2 shard_map.95
  37.1 0.8 %shard_map.96.mine = f32[8,1280]{1,0:T(8,128)S(1)} custom-call(f32[8,1280]{1,0:T(8,128)S(1)} %get-tuple-element.77.rows, f32[8,128]{1,0:T(8,128)S(1)} %get-tuple-element.78.gram, f32[1,128]{1,0:T(1,128)S(1)} %get-tuple-element.79.gain_grad, bf16[1280,256]{1,0:T(8,128)(2,1)S(1)} %get-tuple-element.80.refs_0_, ...), custom_call_target="tpu_custom_call" | custom-call | flops 400 | bytes 1 | tf_op jit(solution)/shard_map/pallas_call | solution.py:29
  37.9 2.0 %collective-permute-start.9 = (f32[8,1280]{1,0:T(8,128)S(1)}, f32[8,1280]{1,0:T(8,128)S(1)}, u32[]{:S(2)}, u32[]{:S(2)}) collective-permute-start(f32[8,1280]{1,0:T(8,128)S(1)} %shard_map.96.mine), channel_id=1, source_target_pairs={{0,1},{1,0},{2,3},{3,2},{4,5},{5,4},{6,7},{7,6},{8,9},{9,8},{10,11... | collective-permute-start | bytes 122888 | tf_op jit(solution)/shard_map/ppermute | solution.py:399
  39.9 0.9 %collective-permute-done.9.other = f32[8,1280]{1,0:T(8,128)S(1)} collective-permute-done((f32[8,1280]{1,0:T(8,128)S(1)}, f32[8,1280]{1,0:T(8,128)S(1)}, u32[]{:S(2)}, u32[]{:S(2)}) %collective-permute-start.9) | collective-permute-done | bytes 40992 | tf_op jit(solution)/shard_map/ppermute | solution.py:399
  40.8 2.5 %collective-permute-start.10 = (f32[8,1152]{1,0:T(8,128)S(1)}, f32[8,1152]{1,0:T(8,128)S(1)}, u32[]{:S(2)}, u32[]{:S(2)}) collective-permute-start(f32[8,1152]{1,0:T(8,128)S(1)} %get-tuple-element.84.pair), channel_id=1, source_target_pairs={{0,2},{1,3},{2,0},{3,1},{4,6},{5,7},{6,4},{7,5},{8,10},{9,11},{10,... | collective-permute-start | bytes 110600 | tf_op jit(solution)/shard_map/ppermute | solution.py:408
  43.3 3.9 %collective-permute-start.12 = (f32[4,1024]{1,0:T(4,128)S(1)}, f32[4,1024]{1,0:T(4,128)S(1)}, u32[]{:S(2)}, u32[]{:S(2)}) collective-permute-start(f32[4,1024]{1,0:T(4,128)S(1)} %get-tuple-element.85._), channel_id=1, source_target_pairs={{0,6},{1,255},{2,4},{3,253},{4,10},{5,3},{6,8},{7,1},{8,14},{9,7},... | collective-permute-start | bytes 49160 | tf_op jit(solution)/shard_map/ppermute | solution.py:407
  47.2 0.0 collective-permute-start.11
  47.2 2.4 %shard_map.98._ = bf16[512,1280]{1,0:T(8,128)(2,1)} custom-call(bf16[512,256]{1,0:T(8,128)(2,1)S(1)} %get-tuple-element.62.kg.kg_k0, bf16[512,256]{1,0:T(8,128)(2,1)S(1)} %get-tuple-element.64.kg.kg_k1, bf16[512,256]{1,0:T(8,128)(2,1)S(1)} %collective-permute-done.4.kg.kg_s0, bf16[512,256]{1,0:T(8,128)(2,1)S(1)} %collective-permute-done.5.kg.kg_s1, ...), custom_call_target="tpu_custom_call" | custom-call | flops 400 | bytes 1 | tf_op jit(solution)/shard_map/pallas_call | solution.py:29
  49.6 0.0 collective-permute-done.12.far
  49.7 0.5 collective-permute-done.11.near
  50.1 0.0 collective-permute-done.10.other
  50.1 3.1 %collective-permute-start.13 = (f32[4,1024]{1,0:T(4,128)S(1)}, f32[4,1024]{1,0:T(4,128)S(1)}, u32[]{:S(2)}, u32[]{:S(2)}) collective-permute-start(f32[4,1024]{1,0:T(4,128)S(1)} %get-tuple-element.92.mine), channel_id=1, source_target_pairs={{0,1},{1,0},{2,3},{3,2},{4,5},{5,4},{6,7},{7,6},{8,9},{9,8},{10,11... | collective-permute-start | bytes 49160 | tf_op jit(solution)/shard_map/ppermute | solution.py:422
  53.3 1.0 %shard_map.100 = (f32[8,128]{1,0:T(8,128)S(1)}, bf16[1280,32]{1,0:T(8,128)(2,1)S(1)}, f32[1,128]{1,0:T(1,128)}) custom-call(f32[8,128]{1,0:T(8,128)S(1)} %get-tuple-element.88.gram, f32[8,1280]{1,0:T(8,128)S(1)} %get-tuple-element.77.rows, f32[1,128]{1,0:T(1,128)S(1)} %copy-done.2, f32[1,128]{1,0:T(1,128)S(1)} %get-tuple-element.89.gain_grad), custom_call_target="tpu_custom_call" | custom-call | flops 400 | bytes 1 | tf_op jit(solution)/shard_map/pallas_call | solution.py:29
  54.2 0.0 collective-permute-done.13.other
  54.3 2.7 %shard_map.101 = (f32[1280,1024]{1,0:T(8,128)}, f32[4,1024]{1,0:T(4,128)}) custom-call(f32[1280,256]{1,0:T(8,128)S(1)} %get-tuple-element.63.s_k0, f32[1280,256]{1,0:T(8,128)S(1)} %get-tuple-element.65.s_k1, f32[1280,256]{1,0:T(8,128)S(1)} %get-tuple-element.66.s_s0, f32[1280,256]{1,0:T(8,128)S(1)} %get-tuple-element.67.s_s1, ...), custom_call_target="tpu_custom_call" | custom-call | flops 400 | bytes 1 | tf_op jit(solution)/shard_map/pallas_call | solution.py:29
  (6 shorter events, 0.0 us)
Async XLA Ops:
  3.3 5.6 %collective-permute-start.1 = (bf16[512,512]{1,0:T(8,128)(2,1)S(1)}, bf16[512,512]{1,0:T(8,128)(2,1)S(1)}, u32[]{:S(2)}, u32[]{:S(2)}) collective-permute-start(bf16[512,512]{1,0:T(8,128)(2,1)S(1)} %get-tuple-element.54), channel_id=1, source_target_pairs={{0,1},{1,0},{2,3},{3,2},{4,5},{5,4},{6,7},{7,6},{8,9},{9,8},{10,11... | collective-permute-start | bytes 1572872 | tf_op jit(solution)/shard_map/ppermute | solution.py:336
  8.9 1.2 %copy-start.1 = (f32[1,4,1024]{2,1,0:T(4,128)S(1)}, f32[1,4,1024]{2,1,0:T(4,128)}, u32[]{:S(2)}) copy-start(f32[1,4,1024]{2,1,0:T(4,128)} %param.9) | copy-start | bytes 49156
  9.0 12.0 %collective-permute-start.3 = (bf16[512,256]{1,0:T(8,128)(2,1)S(1)}, bf16[512,256]{1,0:T(8,128)(2,1)S(1)}, u32[]{:S(2)}, u32[]{:S(2)}) collective-permute-start(bf16[512,256]{1,0:T(8,128)(2,1)S(1)} %get-tuple-element.57.own), channel_id=1, source_target_pairs={{0,2},{1,3},{2,0},{3,1},{4,6},{5,7},{6,4},{7,5},{8,10},{9,11},{10,... | collective-permute-start | bytes 786440 | tf_op jit(solution)/shard_map/ppermute | solution.py:345
  10.1 9.3 %collective-permute-start = (f32[4,1024]{1,0:T(4,128)S(1)}, f32[4,1024]{1,0:T(4,128)S(1)}, u32[]{:S(2)}, u32[]{:S(2)}) collective-permute-start(f32[4,1024]{1,0:T(4,128)S(1)} %bitcast.4), channel_id=1, source_target_pairs={{0,4},{4,8},{8,12},{12,16},{16,20},{20,24},{24,28},{28,32},{32,36}... | collective-permute-start | bytes 49160 | tf_op jit(solution)/shard_map/ppermute | solution.py:347
  11.4 12.7 %collective-permute-start.2 = (bf16[512,256]{1,0:T(8,128)(2,1)S(1)}, bf16[512,256]{1,0:T(8,128)(2,1)S(1)}, u32[]{:S(2)}, u32[]{:S(2)}) collective-permute-start(bf16[512,256]{1,0:T(8,128)(2,1)S(1)} %get-tuple-element.55._.own), channel_id=1, source_target_pairs={{0,2},{1,3},{2,0},{3,1},{4,6},{5,7},{6,4},{7,5},{8,10},{9,11},{10,... | collective-permute-start | bytes 786440 | tf_op jit(solution)/shard_map/ppermute | solution.py:346
  19.4 1.6 %copy-start = (bf16[512,1024]{1,0:T(8,128)(2,1)S(1)}, bf16[512,1024]{1,0:T(8,128)(2,1)}, u32[]{:S(2)}) copy-start(bf16[512,1024]{1,0:T(8,128)(2,1)} %cot.3) | copy-start | bytes 3145732
  19.4 1.6 %copy-start.2 = (f32[1,128]{1,0:T(1,128)S(1)}, f32[1,128]{1,0:T(1,128)}, u32[]{:S(2)}) copy-start(f32[1,128]{1,0:T(1,128)} %gain.5) | copy-start | bytes 1540
  24.7 1.7 %collective-permute-start.6 = (f32[8,512]{1,0:T(8,128)S(1)}, f32[8,512]{1,0:T(8,128)S(1)}, u32[]{:S(2)}, u32[]{:S(2)}) collective-permute-start(f32[8,512]{1,0:T(8,128)S(1)} %get-tuple-element.68.mine), channel_id=1, source_target_pairs={{0,1},{1,0},{2,3},{3,2},{4,5},{5,4},{6,7},{7,6},{8,9},{9,8},{10,11... | collective-permute-start | bytes 49160 | tf_op jit(solution)/shard_map/ppermute | solution.py:374
  25.5 10.3 %collective-permute-start.4 = (bf16[512,256]{1,0:T(8,128)(2,1)S(1)}, bf16[512,256]{1,0:T(8,128)(2,1)S(1)}, u32[]{:S(2)}, u32[]{:S(2)}) collective-permute-start(bf16[512,256]{1,0:T(8,128)(2,1)S(1)} %get-tuple-element.62.kg.kg_k0), channel_id=1, source_target_pairs={{0,1},{1,0},{2,3},{3,2},{4,5},{5,4},{6,7},{7,6},{8,9},{9,8},{10,11... | collective-permute-start | bytes 786440 | tf_op jit(solution)/shard_map/ppermute | solution.py:377
  25.6 9.7 %collective-permute-start.5 = (bf16[512,256]{1,0:T(8,128)(2,1)S(1)}, bf16[512,256]{1,0:T(8,128)(2,1)S(1)}, u32[]{:S(2)}, u32[]{:S(2)}) collective-permute-start(bf16[512,256]{1,0:T(8,128)(2,1)S(1)} %get-tuple-element.64.kg.kg_k1), channel_id=1, source_target_pairs={{0,1},{1,0},{2,3},{3,2},{4,5},{5,4},{6,7},{7,6},{8,9},{9,8},{10,11... | collective-permute-start | bytes 786440 | tf_op jit(solution)/shard_map/ppermute | solution.py:378
  26.6 9.7 %collective-permute-start.7 = (f32[4,1280]{1,0:T(4,128)S(1)}, f32[4,1280]{1,0:T(4,128)S(1)}, u32[]{:S(2)}, u32[]{:S(2)}) collective-permute-start(f32[4,1280]{1,0:T(4,128)S(1)} %get-tuple-element.71), channel_id=1, source_target_pairs={{0,252},{4,8},{8,4},{12,16},{16,12},{20,24},{24,20},{28,32},{32,28... | collective-permute-start | bytes 61448 | tf_op jit(solution)/shard_map/ppermute | solution.py:385
  34.3 2.6 %collective-permute-start.8 = (f32[4,1280]{1,0:T(4,128)S(1)}, f32[4,1280]{1,0:T(4,128)S(1)}, u32[]{:S(2)}, u32[]{:S(2)}) collective-permute-start(f32[4,1280]{1,0:T(4,128)S(1)} %get-tuple-element.72), channel_id=1, source_target_pairs={{0,4},{4,0},{8,12},{12,8},{16,20},{20,16},{24,28},{28,24},{32,36},... | collective-permute-start | bytes 61448 | tf_op jit(solution)/shard_map/ppermute | solution.py:386
  37.9 2.8 %collective-permute-start.9 = (f32[8,1280]{1,0:T(8,128)S(1)}, f32[8,1280]{1,0:T(8,128)S(1)}, u32[]{:S(2)}, u32[]{:S(2)}) collective-permute-start(f32[8,1280]{1,0:T(8,128)S(1)} %shard_map.96.mine), channel_id=1, source_target_pairs={{0,1},{1,0},{2,3},{3,2},{4,5},{5,4},{6,7},{7,6},{8,9},{9,8},{10,11... | collective-permute-start | bytes 122888 | tf_op jit(solution)/shard_map/ppermute | solution.py:399
  40.8 9.3 %collective-permute-start.10 = (f32[8,1152]{1,0:T(8,128)S(1)}, f32[8,1152]{1,0:T(8,128)S(1)}, u32[]{:S(2)}, u32[]{:S(2)}) collective-permute-start(f32[8,1152]{1,0:T(8,128)S(1)} %get-tuple-element.84.pair), channel_id=1, source_target_pairs={{0,2},{1,3},{2,0},{3,1},{4,6},{5,7},{6,4},{7,5},{8,10},{9,11},{10,... | collective-permute-start | bytes 110600 | tf_op jit(solution)/shard_map/ppermute | solution.py:408
  43.3 6.3 %collective-permute-start.12 = (f32[4,1024]{1,0:T(4,128)S(1)}, f32[4,1024]{1,0:T(4,128)S(1)}, u32[]{:S(2)}, u32[]{:S(2)}) collective-permute-start(f32[4,1024]{1,0:T(4,128)S(1)} %get-tuple-element.85._), channel_id=1, source_target_pairs={{0,6},{1,255},{2,4},{3,253},{4,10},{5,3},{6,8},{7,1},{8,14},{9,7},... | collective-permute-start | bytes 49160 | tf_op jit(solution)/shard_map/ppermute | solution.py:407
  47.2 2.9 %collective-permute-start.11 = (f32[4,1024]{1,0:T(4,128)S(1)}, f32[4,1024]{1,0:T(4,128)S(1)}, u32[]{:S(2)}, u32[]{:S(2)}) collective-permute-start(f32[4,1024]{1,0:T(4,128)S(1)} %get-tuple-element.85._), channel_id=1, source_target_pairs={{0,4},{1,253},{2,6},{3,255},{4,8},{5,1},{6,10},{7,3},{8,12},{9,5},... | collective-permute-start | bytes 49160 | tf_op jit(solution)/shard_map/ppermute | solution.py:406
  50.1 4.1 %collective-permute-start.13 = (f32[4,1024]{1,0:T(4,128)S(1)}, f32[4,1024]{1,0:T(4,128)S(1)}, u32[]{:S(2)}, u32[]{:S(2)}) collective-permute-start(f32[4,1024]{1,0:T(4,128)S(1)} %get-tuple-element.92.mine), channel_id=1, source_target_pairs={{0,1},{1,0},{2,3},{3,2},{4,5},{5,4},{6,7},{7,6},{8,9},{9,8},{10,11... | collective-permute-start | bytes 49160 | tf_op jit(solution)/shard_map/ppermute | solution.py:422

commit v4 on v3

--- a/solution.py
+++ b/solution.py
@@ -190,7 +190,10 @@
         copies[j].wait()
 
 
-def rows_kernel(proj, got_first, got_second, _0, _1, _2, _3, rows_out, gram_out):
+def back_kernel(proj, got_first, got_second, gain_grad, *refs):
+    *blocks, rows_out, out = refs
+    wide = blocks[0].shape[1]
+    width = 4 * wide
     n = proj.shape[0]
     rank = n // 2
     odd = odd_replica()
@@ -198,39 +201,38 @@
     got_left = jnp.where(odd, got_second[...], got_first[...])
     rows = jnp.concatenate([proj[:rank] - got_right, got_left - proj[rank:]], axis=0)
     rows_out[...] = rows
-    gram = lax.dot_general(rows, rows, NT, precision=lax.Precision.HIGHEST, preferred_element_type=F32)
-    gram_out[...] = jnp.concatenate([gram, jnp.zeros((n, 128 - n), F32)], axis=1)
-
-
-def back_kernel(rows, gram, gain_grad, *refs):
-    *blocks, out = refs
-    wide = blocks[0].shape[1]
-    width = 4 * wide
-    n = rows.shape[0]
-    r_hi, r_lo = split(rows[...])
+    r_hi, r_lo = split(rows)
     r = jnp.concatenate([r_hi, r_lo], axis=0)
     for j, (kept, i) in enumerate(((True, 0), (True, 1), (False, 0), (False, 1))):
         s_hi, s_lo = blocks[2 * j], blocks[2 * j + 1]
         both = dot(r, s_hi[...])
         out[:, chunk_at(kept, i, wide)] = both[:n] + both[n:] + dot(r_hi, s_lo[...])
-    out[:, width : width + 128] = gram[...]
+    square = dot(r, r, NT)
+    gram = (square[:n, :n] + square[n:, n:]) + (square[:n, n:] + square[n:, :n])
+    out[:, width : width + 128] = jnp.concatenate([gram, jnp.zeros((n, 128 - n), F32)], axis=1)
     out[:, width + 128 :] = jnp.broadcast_to(gain_grad[...], (n, 128))
 
 
-def pair_kernel(mine, other, pair, aside, gain_grad):
-    rank, width = aside.shape
+def pair_kernel(mine, other, keep, aside, gain_grad):
+    rank = keep.shape[0]
+    width = mine.shape[1] - 256
     both = mine[...] + other[...]
-    pair[...] = both[:, : width + 128]
-    aside[...] = jnp.where(core_index() == 0, both[:rank, :width], both[rank:, :width])
+    first = core_index() == 0
+    keep[:, :width] = jnp.where(first, both[rank:, :width], both[:rank, :width])
+    for e in range(2):
+        keep[:, width + 128 * e : width + 128 * (e + 1)] = both[e * rank : (e + 1) * rank, width : width + 128]
+    aside[:, :width] = jnp.where(first, both[:rank, :width], both[rank:, :width])
+    aside[:, width:] = jnp.zeros((rank, aside.shape[1] - width), F32)
     gain_grad[...] = both[0:1, width + 128 :]
 
 
-def edge_kernel(pair, other, near, far, _, out, gram):
+def edge_kernel(keep, other, near, far, _, out, gram):
     rank, width = out.shape
-    whole = pair[...] + other[...]
-    beyond = near[...] + far[...]
-    out[...] = jnp.where(core_index() == 0, beyond - whole[rank:, :width], whole[:rank, :width] - beyond)
-    gram[...] = whole[:, width:]
+    whole = keep[...] + other[...]
+    beyond = near[:, :width] + far[:, :width]
+    out[...] = jnp.where(core_index() == 0, beyond - whole[:, :width], whole[:, :width] - beyond)
+    for e in range(2):
+        gram[e * rank : (e + 1) * rank] = whole[:, width + 128 * e : width + 128 * (e + 1)]
 
 
 def inverse_factor(gram, rank):
@@ -386,26 +388,22 @@
     got_second = lax.ppermute(second, "loop", even_edges)
     s_s0, s_hi_s0, s_lo_s0 = step(0, kg_s0, w_s)
     s_s1, s_hi_s1, s_lo_s1 = step(1, kg_s1, w_s)
-    edge_rows, gram = call(
-        rows_kernel,
-        (proj, got_first, got_second, s_lo_k0, s_lo_k1, s_lo_s0, s_lo_s1),
-        [((n, depth), F32), ((n, 128), F32)],
-    )
-    (payload,) = call(
+    edge_rows, payload = call(
         back_kernel,
-        (edge_rows, gram, gain_part, s_hi_k0, s_lo_k0, s_hi_k1, s_lo_k1, s_hi_s0, s_lo_s0, s_hi_s1, s_lo_s1),
-        [((n, width + 256), F32)],
+        (proj, got_first, got_second, gain_part)
+        + (s_hi_k0, s_lo_k0, s_hi_k1, s_lo_k1, s_hi_s0, s_lo_s0, s_hi_s1, s_lo_s1),
+        [((n, depth), F32), ((n, width + 256), F32)],
     )
     other_core = lax.ppermute(payload, "tp", core)
-    pair, aside, gain_grad = call(
+    keep, aside, gain_grad = call(
         pair_kernel,
         (payload, other_core),
-        [((n, width + 128), F32), ((rank, width), F32), (gain.shape, F32)],
+        [((rank, width + 256), F32), ((rank, width + 384), F32), (gain.shape, F32)],
     )
     everyone = ("loop", "tp")
+    far = lax.ppermute(aside, everyone, along_far)
     near = lax.ppermute(aside, everyone, along)
-    far = lax.ppermute(aside, everyone, along_far)
-    other_chip = lax.ppermute(pair, "tp", chip)
+    other_chip = lax.ppermute(keep, "tp", chip)
     (input_grad,) = call(
         functools.partial(input_kernel, scale),
         (kg_k0, kg_k1, kg_s0, kg_s1, hi_k, hi_s, aside),
@@ -415,7 +413,7 @@
     )
     mine, gram = call(
         edge_kernel,
-        (pair, other_chip, near, far, input_grad),
+        (keep, other_chip, near, far, input_grad),
         [((rank, width), F32), ((n, 128), F32)],
         spaces=(True, True, True, True, False),
     )

time: 57.3 us -> 55.8 us (0.974)
  starting transfers between devices: 26.9 us -> 25.2 us
    ppermute x1, starting transfers between devices: 3.12 us -> 1.3 us  [shards(): other = lax.ppermute(mine, 'tp', core)]
    ppermute x1, starting transfers between devices: 3.88 us -> 5.29 us  [shards(): far = lax.ppermute(aside, everyone, along_far)]
    ppermute x1, starting transfers between devices: 2.54 us -> 1.27 us  [shards(): other_chip = lax.ppermute(keep, 'tp', chip)]
    ppermute x1, waiting for transfers between devices: 0.01 us -> 0.76 us  [shards(): other_chip = lax.ppermute(keep, 'tp', chip)]
    pallas_call x18 -> x17, Pallas kernels: 17.2 us -> 17.1 us  [call(): pl.pallas_call(body, out_shape=[pltpu.VMEM(shape, dtype) if inside else p...]
where the time goes in v4:
time: 55.8 us; the launch traced here: 55.7 us
  starting transfers between devices  25.2 us (45%)
  Pallas kernels  17.1 us (31%)
  waiting for transfers between devices  12.4 us (22%)
  between operations  0.95 us (2%)
    pallas_call x17, Pallas kernels, call(): pl.pallas_call(body, out_shape=[pltpu.VMEM(shape, dtype) if inside else p...  17.1 us
    ppermute x1, starting transfers between devices, shards(): got_first = lax.ppermute(first, 'loop', odd_edges)  7.65 us
    ppermute x1, waiting for transfers between devices, shards(): left_vec = lax.ppermute(vec, 'loop', right)  7.33 us
    ppermute x1, starting transfers between devices, shards(): far = lax.ppermute(aside, everyone, along_far)  5.29 us
    ppermute x1, starting transfers between devices, shards(): from_core = lax.ppermute(part, 'tp', core)  3.33 us
    ppermute x1, waiting for transfers between devices, shards(): from_chip1 = lax.ppermute(chip1, 'tp', chip)  2.53 us
    ppermute x1, starting transfers between devices, shards(): other_core = lax.ppermute(payload, 'tp', core)  1.94 us
    ppermute x1, starting transfers between devices, shards(): other = lax.ppermute(mine, 'tp', core)  1.3 us
  transfers between devices with their start and end apart: 14, of which 6 were waited for; matrix products, arithmetic and copies ran while one was open for 0% of the time, Pallas kernels for 18%

profile of v4, /device:TPU:1, one launch (start us, length us, event | category | flops | bytes accessed | tf_op | source)
XLA Modules:
  0.0 55.7 jit_solution(13141118011425212462)
XLA Ops:
  0.6 2.7 %shard_map.84 = (bf16[512,1280]{1,0:T(8,128)(2,1)S(1)}, f32[1280,512]{1,0:T(8,128)S(1)}, bf16[1280,512]{1,0:T(8,128)(2,1)S(1)}, bf16[512,512]{1,0:T(8,128)(2,1)S(1)}) custom-call(bf16[512,1280]{1,0:T(8,128)(2,1)} %tok.1, f32[1280,1024]{1,0:T(8,128)} %bitcast.8), custom_call_target="tpu_custom_call" | custom-call | flops 400 | bytes 1 | tf_op jit(solution)/shard_map/pallas_call | solution.py:29
  3.3 3.3 %collective-permute-start.1 = (bf16[512,512]{1,0:T(8,128)(2,1)S(1)}, bf16[512,512]{1,0:T(8,128)(2,1)S(1)}, u32[]{:S(2)}, u32[]{:S(2)}) collective-permute-start(bf16[512,512]{1,0:T(8,128)(2,1)S(1)} %get-tuple-element.54), channel_id=1, source_target_pairs={{0,1},{1,0},{2,3},{3,2},{4,5},{5,4},{6,7},{7,6},{8,9},{9,8},{10,11... | collective-permute-start | bytes 1572872 | tf_op jit(solution)/shard_map/ppermute | solution.py:338
  6.6 2.2 %shard_map.85 = (f32[1280,512]{1,0:T(8,128)S(1)}, bf16[1280,512]{1,0:T(8,128)(2,1)S(1)}, f32[512,512]{1,0:T(8,128)S(1)}) custom-call(bf16[512,1280]{1,0:T(8,128)(2,1)S(1)} %get-tuple-element.50.tok_v, f32[1280,1024]{1,0:T(8,128)} %bitcast.9), custom_call_target="tpu_custom_call" | custom-call | flops 400 | bytes 1 | tf_op jit(solution)/shard_map/pallas_call | solution.py:29
  8.9 0.0 copy-start.1
  8.9 0.0 collective-permute-done.1.got
  8.9 0.1 shard_map.86
  9.0 1.1 %collective-permute-start.3 = (bf16[512,256]{1,0:T(8,128)(2,1)S(1)}, bf16[512,256]{1,0:T(8,128)(2,1)S(1)}, u32[]{:S(2)}, u32[]{:S(2)}) collective-permute-start(bf16[512,256]{1,0:T(8,128)(2,1)S(1)} %get-tuple-element.57.own), channel_id=1, source_target_pairs={{0,2},{1,3},{2,0},{3,1},{4,6},{5,7},{6,4},{7,5},{8,10},{9,11},{10,... | collective-permute-start | bytes 786440 | tf_op jit(solution)/shard_map/ppermute | solution.py:347
  10.1 0.0 copy-done.1
  10.1 1.3 %collective-permute-start = (f32[4,1024]{1,0:T(4,128)S(1)}, f32[4,1024]{1,0:T(4,128)S(1)}, u32[]{:S(2)}, u32[]{:S(2)}) collective-permute-start(f32[4,1024]{1,0:T(4,128)S(1)} %bitcast.4), channel_id=1, source_target_pairs={{0,4},{4,8},{8,12},{12,16},{16,20},{20,24},{24,28},{28,32},{32,36}... | collective-permute-start | bytes 49160 | tf_op jit(solution)/shard_map/ppermute | solution.py:349
  11.4 0.7 %collective-permute-start.2 = (bf16[512,256]{1,0:T(8,128)(2,1)S(1)}, bf16[512,256]{1,0:T(8,128)(2,1)S(1)}, u32[]{:S(2)}, u32[]{:S(2)}) collective-permute-start(bf16[512,256]{1,0:T(8,128)(2,1)S(1)} %get-tuple-element.55._.own), channel_id=1, source_target_pairs={{0,2},{1,3},{2,0},{3,1},{4,6},{5,7},{6,4},{7,5},{8,10},{9,11},{10,... | collective-permute-start | bytes 786440 | tf_op jit(solution)/shard_map/ppermute | solution.py:348
  12.1 7.3 %collective-permute-done.left_vec = f32[4,1024]{1,0:T(4,128)S(1)} collective-permute-done((f32[4,1024]{1,0:T(4,128)S(1)}, f32[4,1024]{1,0:T(4,128)S(1)}, u32[]{:S(2)}, u32[]{:S(2)}) %collective-permute-start) | collective-permute-done | bytes 16416 | tf_op jit(solution)/shard_map/ppermute | solution.py:349
  19.4 0.0 copy-start
  19.4 1.6 %shard_map.87 = (f32[8,1280]{1,0:T(8,128)S(1)}, bf16[1280,512]{1,0:T(8,128)(2,1)S(1)}) custom-call(bf16[512,1280]{1,0:T(8,128)(2,1)S(1)} %get-tuple-element.50.tok_v, f32[1280,512]{1,0:T(8,128)S(1)} %get-tuple-element.51.w_k.w, f32[1280,512]{1,0:T(8,128)S(1)} %get-tuple-element.52.w_s.w, f32[4,1024]{1,0:T(4,128)S(1)} %bitcast.5, ...), custom_call_target="tpu_custom_call" | custom-call | flops 400 | bytes 1 | tf_op jit(solution)/shard_map/pallas_call | solution.py:29
  21.0 0.0 collective-permute-done.3.got
  21.0 0.0 copy-done
  21.0 0.0 copy-done.2
  21.0 0.6 %shard_map.88 = (bf16[512,256]{1,0:T(8,128)(2,1)S(1)}, f32[8,512]{1,0:T(8,128)S(1)}, f32[1,128]{1,0:T(1,128)S(1)}, f32[8,1280]{1,0:T(8,128)S(1)}) custom-call(bf16[512,256]{1,0:T(8,128)(2,1)S(1)} %get-tuple-element.57.own, bf16[512,256]{1,0:T(8,128)(2,1)S(1)} %collective-permute-done.3.got, ...), custom_call_target="tpu_custom_call", output_to_operand_aliasing={{3}: (8, {})} | custom-call | flops 16777216000 | bytes 41943040 | tf_op jit(solution)/shard_map/pallas_call | solution.py:29
  21.6 2.5 %collective-permute-done.2.got = bf16[512,256]{1,0:T(8,128)(2,1)S(1)} collective-permute-done((bf16[512,256]{1,0:T(8,128)(2,1)S(1)}, bf16[512,256]{1,0:T(8,128)(2,1)S(1)}, u32[]{:S(2)}, u32[]{:S(2)}) %collective-permute-start.2) | collective-permute-done | bytes 262176 | tf_op jit(solution)/shard_map/ppermute | solution.py:348
  24.1 0.6 %shard_map.89 = (bf16[512,256]{1,0:T(8,128)(2,1)S(1)}, f32[8,512]{1,0:T(8,128)S(1)}, f32[1,128]{1,0:T(1,128)S(1)}, bf16[512,256]{1,0:T(8,128)(2,1)S(1)}) custom-call(bf16[512,256]{1,0:T(8,128)(2,1)S(1)} %get-tuple-element.55._.own, bf16[512,256]{1,0:T(8,128)(2,1)S(1)} %collective-permute-done.2.got, ...), custom_call_target="tpu_custom_call", output_to_operand_aliasing={{3}: (8, {})} | custom-call | flops 400 | bytes 1 | tf_op jit(solution)/shard_map/pallas_call | solution.py:29
  24.7 0.8 %collective-permute-start.6 = (f32[8,512]{1,0:T(8,128)S(1)}, f32[8,512]{1,0:T(8,128)S(1)}, u32[]{:S(2)}, u32[]{:S(2)}) collective-permute-start(f32[8,512]{1,0:T(8,128)S(1)} %get-tuple-element.68.mine), channel_id=1, source_target_pairs={{0,1},{1,0},{2,3},{3,2},{4,5},{5,4},{6,7},{7,6},{8,9},{9,8},{10,11... | collective-permute-start | bytes 49160 | tf_op jit(solution)/shard_map/ppermute | solution.py:376
  25.5 0.1 collective-permute-start.4
  25.6 0.4 collective-permute-start.5
  26.0 0.3 collective-permute-done.6.other
  26.4 0.3 shard_map.94
  26.6 7.7 %collective-permute-start.7 = (f32[4,1280]{1,0:T(4,128)S(1)}, f32[4,1280]{1,0:T(4,128)S(1)}, u32[]{:S(2)}, u32[]{:S(2)}) collective-permute-start(f32[4,1280]{1,0:T(4,128)S(1)} %get-tuple-element.71), channel_id=1, source_target_pairs={{0,252},{4,8},{8,4},{12,16},{16,12},{20,24},{24,20},{28,32},{32,28... | collective-permute-start | bytes 61448 | tf_op jit(solution)/shard_map/ppermute | solution.py:387
  34.3 0.0 collective-permute-start.8
  34.3 0.5 shard_map.90
  34.8 0.5 shard_map.91
  35.3 0.0 collective-permute-done.5.kg.kg_s1
  35.3 0.5 shard_map.93
  35.8 0.0 collective-permute-done.4.kg.kg_s0
  35.9 0.5 shard_map.92
  36.4 0.0 collective-permute-done.7.got_first
  36.4 0.6 collective-permute-done.8.got_second
  36.9 0.9 %shard_map.95 = (f32[8,1280]{1,0:T(8,128)S(1)}, f32[8,1280]{1,0:T(8,128)S(1)}) custom-call(f32[8,1280]{1,0:T(8,128)S(1)} %get-tuple-element.70.proj, f32[4,1280]{1,0:T(4,128)S(1)} %collective-permute-done.7.got_first, f32[4,1280]{1,0:T(4,128)S(1)} %collective-permute-done.8.got_second, f32[1,128]{1,0:T(1,128)S(1)} %get-tuple-element.73.gain_grad, ...), custom_call_target="tpu_custom_call" | custom-call | flops 400 | bytes 1 | tf_op jit(solution)/shard_map/pallas_call | solution.py:29
  37.9 1.9 %collective-permute-start.9 = (f32[8,1280]{1,0:T(8,128)S(1)}, f32[8,1280]{1,0:T(8,128)S(1)}, u32[]{:S(2)}, u32[]{:S(2)}) collective-permute-start(f32[8,1280]{1,0:T(8,128)S(1)} %get-tuple-element.82.mine), channel_id=1, source_target_pairs={{0,1},{1,0},{2,3},{3,2},{4,5},{5,4},{6,7},{7,6},{8,9},{9,8},{10,11... | collective-permute-start | bytes 122888 | tf_op jit(solution)/shard_map/ppermute | solution.py:397
  39.8 0.9 %collective-permute-done.9.other = f32[8,1280]{1,0:T(8,128)S(1)} collective-permute-done((f32[8,1280]{1,0:T(8,128)S(1)}, f32[8,1280]{1,0:T(8,128)S(1)}, u32[]{:S(2)}, u32[]{:S(2)}) %collective-permute-start.9) | collective-permute-done | bytes 40992 | tf_op jit(solution)/shard_map/ppermute | solution.py:397
  40.7 5.3 %collective-permute-start.12 = (f32[4,1408]{1,0:T(4,128)S(1)}, f32[4,1408]{1,0:T(4,128)S(1)}, u32[]{:S(2)}, u32[]{:S(2)}) collective-permute-start(f32[4,1408]{1,0:T(4,128)S(1)} %get-tuple-element.84._), channel_id=1, source_target_pairs={{0,6},{1,255},{2,4},{3,253},{4,10},{5,3},{6,8},{7,1},{8,14},{9,7},... | collective-permute-start | bytes 67592 | tf_op jit(solution)/shard_map/ppermute | solution.py:404
  46.0 0.0 collective-permute-start.11
  46.0 1.3 %collective-permute-start.10 = (f32[4,1280]{1,0:T(4,128)S(1)}, f32[4,1280]{1,0:T(4,128)S(1)}, u32[]{:S(2)}, u32[]{:S(2)}) collective-permute-start(f32[4,1280]{1,0:T(4,128)S(1)} %get-tuple-element.83.keep), channel_id=1, source_target_pairs={{0,2},{1,3},{2,0},{3,1},{4,6},{5,7},{6,4},{7,5},{8,10},{9,11},{10,... | collective-permute-start | bytes 61448 | tf_op jit(solution)/shard_map/ppermute | solution.py:406
  47.3 2.4 %shard_map.97._ = bf16[512,1280]{1,0:T(8,128)(2,1)} custom-call(bf16[512,256]{1,0:T(8,128)(2,1)S(1)} %get-tuple-element.62.kg.kg_k0, bf16[512,256]{1,0:T(8,128)(2,1)S(1)} %get-tuple-element.64.kg.kg_k1, bf16[512,256]{1,0:T(8,128)(2,1)S(1)} %collective-permute-done.4.kg.kg_s0, bf16[512,256]{1,0:T(8,128)(2,1)S(1)} %collective-permute-done.5.kg.kg_s1, ...), custom_call_target="tpu_custom_call" | custom-call | flops 400 | bytes 1 | tf_op jit(solution)/shard_map/pallas_call | solution.py:29
  49.7 0.8 %collective-permute-done.10.other = f32[4,1280]{1,0:T(4,128)S(1)} collective-permute-done((f32[4,1280]{1,0:T(4,128)S(1)}, f32[4,1280]{1,0:T(4,128)S(1)}, u32[]{:S(2)}, u32[]{:S(2)}) %collective-permute-start.10) | collective-permute-done | bytes 20512 | tf_op jit(solution)/shard_map/ppermute | solution.py:406
  50.4 0.0 collective-permute-done.12.far
  50.4 0.0 collective-permute-done.11.near
  50.4 1.3 %collective-permute-start.13 = (f32[4,1024]{1,0:T(4,128)S(1)}, f32[4,1024]{1,0:T(4,128)S(1)}, u32[]{:S(2)}, u32[]{:S(2)}) collective-permute-start(f32[4,1024]{1,0:T(4,128)S(1)} %get-tuple-element.92.mine), channel_id=1, source_target_pairs={{0,1},{1,0},{2,3},{3,2},{4,5},{5,4},{6,7},{7,6},{8,9},{9,8},{10,11... | collective-permute-start | bytes 49160 | tf_op jit(solution)/shard_map/ppermute | solution.py:420
  51.7 1.0 %shard_map.99 = (f32[8,128]{1,0:T(8,128)S(1)}, bf16[1280,32]{1,0:T(8,128)(2,1)S(1)}, f32[1,128]{1,0:T(1,128)}) custom-call(f32[8,128]{1,0:T(8,128)S(1)} %get-tuple-element.87.gram, f32[8,1280]{1,0:T(8,128)S(1)} %get-tuple-element.88.rows, f32[1,128]{1,0:T(1,128)S(1)} %copy-done.2, f32[1,128]{1,0:T(1,128)S(1)} %get-tuple-element.89.gain_grad), custom_call_target="tpu_custom_call" | custom-call | flops 400 | bytes 1 | tf_op jit(solution)/shard_map/pallas_call | solution.py:29
  52.7 0.0 collective-permute-done.13.other
  52.7 2.7 %shard_map.100 = (f32[1280,1024]{1,0:T(8,128)}, f32[4,1024]{1,0:T(4,128)}) custom-call(f32[1280,256]{1,0:T(8,128)S(1)} %get-tuple-element.63.s_k0, f32[1280,256]{1,0:T(8,128)S(1)} %get-tuple-element.65.s_k1, f32[1280,256]{1,0:T(8,128)S(1)} %get-tuple-element.66.s_s0, f32[1280,256]{1,0:T(8,128)S(1)} %get-tuple-element.67.s_s1, ...), custom_call_target="tpu_custom_call" | custom-call | flops 400 | bytes 1 | tf_op jit(solution)/shard_map/pallas_call | solution.py:29
  (5 shorter events, 0.0 us)
Async XLA Ops:
  3.3 5.6 %collective-permute-start.1 = (bf16[512,512]{1,0:T(8,128)(2,1)S(1)}, bf16[512,512]{1,0:T(8,128)(2,1)S(1)}, u32[]{:S(2)}, u32[]{:S(2)}) collective-permute-start(bf16[512,512]{1,0:T(8,128)(2,1)S(1)} %get-tuple-element.54), channel_id=1, source_target_pairs={{0,1},{1,0},{2,3},{3,2},{4,5},{5,4},{6,7},{7,6},{8,9},{9,8},{10,11... | collective-permute-start | bytes 1572872 | tf_op jit(solution)/shard_map/ppermute | solution.py:338
  8.9 1.2 %copy-start.1 = (f32[1,4,1024]{2,1,0:T(4,128)S(1)}, f32[1,4,1024]{2,1,0:T(4,128)}, u32[]{:S(2)}) copy-start(f32[1,4,1024]{2,1,0:T(4,128)} %param.9) | copy-start | bytes 49156
  9.0 12.0 %collective-permute-start.3 = (bf16[512,256]{1,0:T(8,128)(2,1)S(1)}, bf16[512,256]{1,0:T(8,128)(2,1)S(1)}, u32[]{:S(2)}, u32[]{:S(2)}) collective-permute-start(bf16[512,256]{1,0:T(8,128)(2,1)S(1)} %get-tuple-element.57.own), channel_id=1, source_target_pairs={{0,2},{1,3},{2,0},{3,1},{4,6},{5,7},{6,4},{7,5},{8,10},{9,11},{10,... | collective-permute-start | bytes 786440 | tf_op jit(solution)/shard_map/ppermute | solution.py:347
  10.1 9.3 %collective-permute-start = (f32[4,1024]{1,0:T(4,128)S(1)}, f32[4,1024]{1,0:T(4,128)S(1)}, u32[]{:S(2)}, u32[]{:S(2)}) collective-permute-start(f32[4,1024]{1,0:T(4,128)S(1)} %bitcast.4), channel_id=1, source_target_pairs={{0,4},{4,8},{8,12},{12,16},{16,20},{20,24},{24,28},{28,32},{32,36}... | collective-permute-start | bytes 49160 | tf_op jit(solution)/shard_map/ppermute | solution.py:349
  11.4 12.7 %collective-permute-start.2 = (bf16[512,256]{1,0:T(8,128)(2,1)S(1)}, bf16[512,256]{1,0:T(8,128)(2,1)S(1)}, u32[]{:S(2)}, u32[]{:S(2)}) collective-permute-start(bf16[512,256]{1,0:T(8,128)(2,1)S(1)} %get-tuple-element.55._.own), channel_id=1, source_target_pairs={{0,2},{1,3},{2,0},{3,1},{4,6},{5,7},{6,4},{7,5},{8,10},{9,11},{10,... | collective-permute-start | bytes 786440 | tf_op jit(solution)/shard_map/ppermute | solution.py:348
  19.4 1.6 %copy-start = (bf16[512,1024]{1,0:T(8,128)(2,1)S(1)}, bf16[512,1024]{1,0:T(8,128)(2,1)}, u32[]{:S(2)}) copy-start(bf16[512,1024]{1,0:T(8,128)(2,1)} %cot.3) | copy-start | bytes 3145732
  19.4 1.6 %copy-start.2 = (f32[1,128]{1,0:T(1,128)S(1)}, f32[1,128]{1,0:T(1,128)}, u32[]{:S(2)}) copy-start(f32[1,128]{1,0:T(1,128)} %gain.5) | copy-start | bytes 1540
  24.7 1.6 %collective-permute-start.6 = (f32[8,512]{1,0:T(8,128)S(1)}, f32[8,512]{1,0:T(8,128)S(1)}, u32[]{:S(2)}, u32[]{:S(2)}) collective-permute-start(f32[8,512]{1,0:T(8,128)S(1)} %get-tuple-element.68.mine), channel_id=1, source_target_pairs={{0,1},{1,0},{2,3},{3,2},{4,5},{5,4},{6,7},{7,6},{8,9},{9,8},{10,11... | collective-permute-start | bytes 49160 | tf_op jit(solution)/shard_map/ppermute | solution.py:376
  25.5 10.3 %collective-permute-start.4 = (bf16[512,256]{1,0:T(8,128)(2,1)S(1)}, bf16[512,256]{1,0:T(8,128)(2,1)S(1)}, u32[]{:S(2)}, u32[]{:S(2)}) collective-permute-start(bf16[512,256]{1,0:T(8,128)(2,1)S(1)} %get-tuple-element.62.kg.kg_k0), channel_id=1, source_target_pairs={{0,1},{1,0},{2,3},{3,2},{4,5},{5,4},{6,7},{7,6},{8,9},{9,8},{10,11... | collective-permute-start | bytes 786440 | tf_op jit(solution)/shard_map/ppermute | solution.py:379
  25.6 9.7 %collective-permute-start.5 = (bf16[512,256]{1,0:T(8,128)(2,1)S(1)}, bf16[512,256]{1,0:T(8,128)(2,1)S(1)}, u32[]{:S(2)}, u32[]{:S(2)}) collective-permute-start(bf16[512,256]{1,0:T(8,128)(2,1)S(1)} %get-tuple-element.64.kg.kg_k1), channel_id=1, source_target_pairs={{0,1},{1,0},{2,3},{3,2},{4,5},{5,4},{6,7},{7,6},{8,9},{9,8},{10,11... | collective-permute-start | bytes 786440 | tf_op jit(solution)/shard_map/ppermute | solution.py:380
  26.6 9.7 %collective-permute-start.7 = (f32[4,1280]{1,0:T(4,128)S(1)}, f32[4,1280]{1,0:T(4,128)S(1)}, u32[]{:S(2)}, u32[]{:S(2)}) collective-permute-start(f32[4,1280]{1,0:T(4,128)S(1)} %get-tuple-element.71), channel_id=1, source_target_pairs={{0,252},{4,8},{8,4},{12,16},{16,12},{20,24},{24,20},{28,32},{32,28... | collective-permute-start | bytes 61448 | tf_op jit(solution)/shard_map/ppermute | solution.py:387
  34.3 2.6 %collective-permute-start.8 = (f32[4,1280]{1,0:T(4,128)S(1)}, f32[4,1280]{1,0:T(4,128)S(1)}, u32[]{:S(2)}, u32[]{:S(2)}) collective-permute-start(f32[4,1280]{1,0:T(4,128)S(1)} %get-tuple-element.72), channel_id=1, source_target_pairs={{0,4},{4,0},{8,12},{12,8},{16,20},{20,16},{24,28},{28,24},{32,36},... | collective-permute-start | bytes 61448 | tf_op jit(solution)/shard_map/ppermute | solution.py:388
  37.9 2.8 %collective-permute-start.9 = (f32[8,1280]{1,0:T(8,128)S(1)}, f32[8,1280]{1,0:T(8,128)S(1)}, u32[]{:S(2)}, u32[]{:S(2)}) collective-permute-start(f32[8,1280]{1,0:T(8,128)S(1)} %get-tuple-element.82.mine), channel_id=1, source_target_pairs={{0,1},{1,0},{2,3},{3,2},{4,5},{5,4},{6,7},{7,6},{8,9},{9,8},{10,11... | collective-permute-start | bytes 122888 | tf_op jit(solution)/shard_map/ppermute | solution.py:397
  40.7 9.7 %collective-permute-start.12 = (f32[4,1408]{1,0:T(4,128)S(1)}, f32[4,1408]{1,0:T(4,128)S(1)}, u32[]{:S(2)}, u32[]{:S(2)}) collective-permute-start(f32[4,1408]{1,0:T(4,128)S(1)} %get-tuple-element.84._), channel_id=1, source_target_pairs={{0,6},{1,255},{2,4},{3,253},{4,10},{5,3},{6,8},{7,1},{8,14},{9,7},... | collective-permute-start | bytes 67592 | tf_op jit(solution)/shard_map/ppermute | solution.py:404
  46.0 4.4 %collective-permute-start.11 = (f32[4,1408]{1,0:T(4,128)S(1)}, f32[4,1408]{1,0:T(4,128)S(1)}, u32[]{:S(2)}, u32[]{:S(2)}) collective-permute-start(f32[4,1408]{1,0:T(4,128)S(1)} %get-tuple-element.84._), channel_id=1, source_target_pairs={{0,4},{1,253},{2,6},{3,255},{4,8},{5,1},{6,10},{7,3},{8,12},{9,5},... | collective-permute-start | bytes 67592 | tf_op jit(solution)/shard_map/ppermute | solution.py:405
  46.0 4.4 %collective-permute-start.10 = (f32[4,1280]{1,0:T(4,128)S(1)}, f32[4,1280]{1,0:T(4,128)S(1)}, u32[]{:S(2)}, u32[]{:S(2)}) collective-permute-start(f32[4,1280]{1,0:T(4,128)S(1)} %get-tuple-element.83.keep), channel_id=1, source_target_pairs={{0,2},{1,3},{2,0},{3,1},{4,6},{5,7},{6,4},{7,5},{8,10},{9,11},{10,... | collective-permute-start | bytes 61448 | tf_op jit(solution)/shard_map/ppermute | solution.py:406
  50.4 2.3 %collective-permute-start.13 = (f32[4,1024]{1,0:T(4,128)S(1)}, f32[4,1024]{1,0:T(4,128)S(1)}, u32[]{:S(2)}, u32[]{:S(2)}) collective-permute-start(f32[4,1024]{1,0:T(4,128)S(1)} %get-tuple-element.92.mine), channel_id=1, source_target_pairs={{0,1},{1,0},{2,3},{3,2},{4,5},{5,4},{6,7},{7,6},{8,9},{9,8},{10,11... | collective-permute-start | bytes 49160 | tf_op jit(solution)/shard_map/ppermute | solution.py:420

commit v5 on v4

--- a/solution.py
+++ b/solution.py
@@ -148,7 +148,7 @@
 
 
 def odd_replica():
-    return lax.rem(lax.axis_index("loop"), 2) == 1
+    return lax.rem(lax.axis_index("loop"), 2) == 0
 
 
 def project_kernel(rate, mine, other, proj0, tok_v, first, second, out):
@@ -213,7 +213,7 @@
     out[:, width + 128 :] = jnp.broadcast_to(gain_grad[...], (n, 128))
 
 
-def pair_kernel(mine, other, keep, aside, gain_grad):
+def pair_kernel(mine, other, keep, near, far, gain_grad):
     rank = keep.shape[0]
     width = mine.shape[1] - 256
     both = mine[...] + other[...]
@@ -221,8 +221,9 @@
     keep[:, :width] = jnp.where(first, both[rank:, :width], both[:rank, :width])
     for e in range(2):
         keep[:, width + 128 * e : width + 128 * (e + 1)] = both[e * rank : (e + 1) * rank, width : width + 128]
-    aside[:, :width] = jnp.where(first, both[:rank, :width], both[rank:, :width])
-    aside[:, width:] = jnp.zeros((rank, aside.shape[1] - width), F32)
+    for aside in (near, far):
+        aside[:, :width] = jnp.where(first, both[:rank, :width], both[rank:, :width])
+        aside[:, width:] = jnp.zeros((rank, aside.shape[1] - width), F32)
     gain_grad[...] = both[0:1, width + 128 :]
 
 
@@ -372,9 +373,9 @@
     kg_k0, on_keys, gain_part, proj0 = norm(
         0, chip0, from_chip0, jnp.zeros((n, rows), F32), jnp.zeros(gain.shape, F32), proj0
     )
-    kg_k1, on_keys, gain_part, kg_k0 = norm(1, chip1, from_chip1, on_keys, gain_part, kg_k0)
+    s_k0, s_hi_k0, s_lo_k0 = step(0, kg_k0, w_k)
+    kg_k1, on_keys, gain_part, s_lo_k0 = norm(1, chip1, from_chip1, on_keys, gain_part, s_lo_k0)
     on_keys_s = lax.ppermute(on_keys, "tp", core)
-    s_k0, s_hi_k0, s_lo_k0 = step(0, kg_k0, w_k)
     s_k1, s_hi_k1, s_lo_k1 = step(1, kg_k1, w_k)
     kg_s0 = lax.ppermute(kg_k0, "tp", core)
     kg_s1 = lax.ppermute(kg_k1, "tp", core)
@@ -384,8 +385,8 @@
         [((rank, depth), F32), ((rank, depth), F32), ((n, depth), F32)],
         nbytes=40 * MIB,
     )
-    got_first = lax.ppermute(first, "loop", odd_edges)
-    got_second = lax.ppermute(second, "loop", even_edges)
+    got_first = lax.ppermute(first, "loop", even_edges)
+    got_second = lax.ppermute(second, "loop", odd_edges)
     s_s0, s_hi_s0, s_lo_s0 = step(0, kg_s0, w_s)
     s_s1, s_hi_s1, s_lo_s1 = step(1, kg_s1, w_s)
     edge_rows, payload = call(
@@ -395,18 +396,18 @@
         [((n, depth), F32), ((n, width + 256), F32)],
     )
     other_core = lax.ppermute(payload, "tp", core)
-    keep, aside, gain_grad = call(
+    keep, near, far, gain_grad = call(
         pair_kernel,
         (payload, other_core),
-        [((rank, width + 256), F32), ((rank, width + 384), F32), (gain.shape, F32)],
+        [((rank, width + 256), F32), ((rank, width + 384), F32), ((rank, width + 512), F32), (gain.shape, F32)],
     )
     everyone = ("loop", "tp")
-    far = lax.ppermute(aside, everyone, along_far)
-    near = lax.ppermute(aside, everyone, along)
+    far = lax.ppermute(far, everyone, along_far)
+    near = lax.ppermute(near, everyone, along)
     other_chip = lax.ppermute(keep, "tp", chip)
     (input_grad,) = call(
         functools.partial(input_kernel, scale),
-        (kg_k0, kg_k1, kg_s0, kg_s1, hi_k, hi_s, aside),
+        (kg_k0, kg_k1, kg_s0, kg_s1, hi_k, hi_s, keep),
         [((rows, depth), BF16)],
         [pltpu.VMEM((rows, depth), BF16), dma((steps,))],
         out_spaces=(False,),

time: 55.8 us -> 54.9 us (0.984)
  waiting for transfers between devices: 12.4 us -> 11.2 us
    ppermute x4, starting transfers between devices: 12.9 us -> 15.1 us  [the longest x1 7.67 us: shards(): got_second = lax.ppermute(second, 'loop', odd_edges)]
    ppermute x1, starting transfers between devices: 1.3 us -> 0.09 us  [shards(): other = lax.ppermute(mine, 'tp', core)]
    ppermute x1, starting transfers between devices: 1.94 us -> 1.25 us  [shards(): other_core = lax.ppermute(payload, 'tp', core)]
where the time goes in v5:
time: 54.9 us; the launch traced here: 54.7 us
  starting transfers between devices  25.4 us (46%)
  Pallas kernels  17.1 us (31%)
  waiting for transfers between devices  11.2 us (20%)
  between operations  0.97 us (2%)
    pallas_call x17, Pallas kernels, call(): pl.pallas_call(body, out_shape=[pltpu.VMEM(shape, dtype) if inside else p...  17.1 us
    ppermute x1, starting transfers between devices, shards(): got_second = lax.ppermute(second, 'loop', odd_edges)  7.67 us
    ppermute x1, waiting for transfers between devices, shards(): left_vec = lax.ppermute(vec, 'loop', right)  7.33 us
    ppermute x1, starting transfers between devices, shards(): far = lax.ppermute(far, everyone, along_far)  7.31 us
    ppermute x1, starting transfers between devices, shards(): from_core = lax.ppermute(part, 'tp', core)  3.33 us
    ppermute x1, waiting for transfers between devices, shards(): from_chip1 = lax.ppermute(chip1, 'tp', chip)  2.02 us
    ppermute x1, starting transfers between devices, shards(): left_vec = lax.ppermute(vec, 'loop', right)  1.3 us
    ppermute x1, starting transfers between devices, shards(): other_chip = lax.ppermute(keep, 'tp', chip)  1.27 us
  transfers between devices with their start and end apart: 14, of which 6 were waited for; matrix products, arithmetic and copies ran while one was open for 0% of the time, Pallas kernels for 18%

profile of v5, /device:TPU:1, one launch (start us, length us, event | category | flops | bytes accessed | tf_op | source)
XLA Modules:
  0.0 54.7 jit_solution(5394456468066058828)
XLA Ops:
  0.6 2.7 %shard_map.84 = (bf16[512,1280]{1,0:T(8,128)(2,1)S(1)}, f32[1280,512]{1,0:T(8,128)S(1)}, bf16[1280,512]{1,0:T(8,128)(2,1)S(1)}, bf16[512,512]{1,0:T(8,128)(2,1)S(1)}) custom-call(bf16[512,1280]{1,0:T(8,128)(2,1)} %tok.1, f32[1280,1024]{1,0:T(8,128)} %bitcast.8), custom_call_target="tpu_custom_call" | custom-call | flops 400 | bytes 1 | tf_op jit(solution)/shard_map/pallas_call | solution.py:29
  3.3 3.3 %collective-permute-start.1 = (bf16[512,512]{1,0:T(8,128)(2,1)S(1)}, bf16[512,512]{1,0:T(8,128)(2,1)S(1)}, u32[]{:S(2)}, u32[]{:S(2)}) collective-permute-start(bf16[512,512]{1,0:T(8,128)(2,1)S(1)} %get-tuple-element.55), channel_id=1, source_target_pairs={{0,1},{1,0},{2,3},{3,2},{4,5},{5,4},{6,7},{7,6},{8,9},{9,8},{10,11... | collective-permute-start | bytes 1572872 | tf_op jit(solution)/shard_map/ppermute | solution.py:339
  6.6 2.2 %shard_map.85 = (f32[1280,512]{1,0:T(8,128)S(1)}, bf16[1280,512]{1,0:T(8,128)(2,1)S(1)}, f32[512,512]{1,0:T(8,128)S(1)}) custom-call(bf16[512,1280]{1,0:T(8,128)(2,1)S(1)} %get-tuple-element.51.tok_v, f32[1280,1024]{1,0:T(8,128)} %bitcast.9), custom_call_target="tpu_custom_call" | custom-call | flops 400 | bytes 1 | tf_op jit(solution)/shard_map/pallas_call | solution.py:29
  8.9 0.0 copy-start.1
  8.9 0.0 collective-permute-done.1.got
  8.9 0.1 shard_map.86
  9.0 1.1 %collective-permute-start.2 = (bf16[512,256]{1,0:T(8,128)(2,1)S(1)}, bf16[512,256]{1,0:T(8,128)(2,1)S(1)}, u32[]{:S(2)}, u32[]{:S(2)}) collective-permute-start(bf16[512,256]{1,0:T(8,128)(2,1)S(1)} %get-tuple-element.58.own), channel_id=1, source_target_pairs={{0,2},{1,3},{2,0},{3,1},{4,6},{5,7},{6,4},{7,5},{8,10},{9,11},{10,... | collective-permute-start | bytes 786440 | tf_op jit(solution)/shard_map/ppermute | solution.py:348
  10.1 0.0 copy-done.1
  10.1 1.3 %collective-permute-start = (f32[4,1024]{1,0:T(4,128)S(1)}, f32[4,1024]{1,0:T(4,128)S(1)}, u32[]{:S(2)}, u32[]{:S(2)}) collective-permute-start(f32[4,1024]{1,0:T(4,128)S(1)} %bitcast.4), channel_id=1, source_target_pairs={{0,4},{4,8},{8,12},{12,16},{16,20},{20,24},{24,28},{28,32},{32,36}... | collective-permute-start | bytes 49160 | tf_op jit(solution)/shard_map/ppermute | solution.py:350
  11.4 0.7 %collective-permute-start.3 = (bf16[512,256]{1,0:T(8,128)(2,1)S(1)}, bf16[512,256]{1,0:T(8,128)(2,1)S(1)}, u32[]{:S(2)}, u32[]{:S(2)}) collective-permute-start(bf16[512,256]{1,0:T(8,128)(2,1)S(1)} %get-tuple-element.56._.own), channel_id=1, source_target_pairs={{0,2},{1,3},{2,0},{3,1},{4,6},{5,7},{6,4},{7,5},{8,10},{9,11},{10,... | collective-permute-start | bytes 786440 | tf_op jit(solution)/shard_map/ppermute | solution.py:349
  12.1 7.3 %collective-permute-done.left_vec = f32[4,1024]{1,0:T(4,128)S(1)} collective-permute-done((f32[4,1024]{1,0:T(4,128)S(1)}, f32[4,1024]{1,0:T(4,128)S(1)}, u32[]{:S(2)}, u32[]{:S(2)}) %collective-permute-start) | collective-permute-done | bytes 16416 | tf_op jit(solution)/shard_map/ppermute | solution.py:350
  19.4 0.0 copy-start
  19.4 1.6 %shard_map.87 = (f32[8,1280]{1,0:T(8,128)S(1)}, bf16[1280,512]{1,0:T(8,128)(2,1)S(1)}) custom-call(bf16[512,1280]{1,0:T(8,128)(2,1)S(1)} %get-tuple-element.51.tok_v, f32[1280,512]{1,0:T(8,128)S(1)} %get-tuple-element.52.w_k.w, f32[1280,512]{1,0:T(8,128)S(1)} %get-tuple-element.53.w_s.w, f32[4,1024]{1,0:T(4,128)S(1)} %bitcast.5, ...), custom_call_target="tpu_custom_call" | custom-call | flops 400 | bytes 1 | tf_op jit(solution)/shard_map/pallas_call | solution.py:29
  21.0 0.0 collective-permute-done.2.got
  21.0 0.0 copy-done
  21.0 0.0 copy-done.2
  21.0 0.6 %shard_map.88 = (bf16[512,256]{1,0:T(8,128)(2,1)S(1)}, f32[8,512]{1,0:T(8,128)S(1)}, f32[1,128]{1,0:T(1,128)S(1)}, f32[8,1280]{1,0:T(8,128)S(1)}) custom-call(bf16[512,256]{1,0:T(8,128)(2,1)S(1)} %get-tuple-element.58.own, bf16[512,256]{1,0:T(8,128)(2,1)S(1)} %collective-permute-done.2.got, ...), custom_call_target="tpu_custom_call", output_to_operand_aliasing={{3}: (8, {})} | custom-call | flops 16777216000 | bytes 41943040 | tf_op jit(solution)/shard_map/pallas_call | solution.py:29
  21.6 0.5 shard_map.89
  22.1 2.0 %collective-permute-done.3.got = bf16[512,256]{1,0:T(8,128)(2,1)S(1)} collective-permute-done((bf16[512,256]{1,0:T(8,128)(2,1)S(1)}, bf16[512,256]{1,0:T(8,128)(2,1)S(1)}, u32[]{:S(2)}, u32[]{:S(2)}) %collective-permute-start.3) | collective-permute-done | bytes 262176 | tf_op jit(solution)/shard_map/ppermute | solution.py:349
  24.1 0.6 %shard_map.90 = (bf16[512,256]{1,0:T(8,128)(2,1)S(1)}, f32[8,512]{1,0:T(8,128)S(1)}, f32[1,128]{1,0:T(1,128)S(1)}, bf16[1280,256]{1,0:T(8,128)(2,1)S(1)}) custom-call(bf16[512,256]{1,0:T(8,128)(2,1)S(1)} %get-tuple-element.56._.own, bf16[512,256]{1,0:T(8,128)(2,1)S(1)} %collective-permute-done.3.got, ...), custom_call_target="tpu_custom_call", output_to_operand_aliasing={{3}: (8, {})} | custom-call | flops 400 | bytes 1 | tf_op jit(solution)/shard_map/pallas_call | solution.py:29
  24.7 0.8 %collective-permute-start.6 = (f32[8,512]{1,0:T(8,128)S(1)}, f32[8,512]{1,0:T(8,128)S(1)}, u32[]{:S(2)}, u32[]{:S(2)}) collective-permute-start(f32[8,512]{1,0:T(8,128)S(1)} %get-tuple-element.69.mine), channel_id=1, source_target_pairs={{0,1},{1,0},{2,3},{3,2},{4,5},{5,4},{6,7},{7,6},{8,9},{9,8},{10,11... | collective-permute-start | bytes 49160 | tf_op jit(solution)/shard_map/ppermute | solution.py:378
  25.5 0.1 collective-permute-start.4
  25.6 0.4 collective-permute-start.5
  26.0 0.3 collective-permute-done.6.other
  26.4 0.3 shard_map.94
  26.7 0.1 collective-permute-start.7
  26.7 7.7 %collective-permute-start.8 = (f32[4,1280]{1,0:T(4,128)S(1)}, f32[4,1280]{1,0:T(4,128)S(1)}, u32[]{:S(2)}, u32[]{:S(2)}) collective-permute-start(f32[4,1280]{1,0:T(4,128)S(1)} %get-tuple-element.73), channel_id=1, source_target_pairs={{0,252},{4,8},{8,4},{12,16},{16,12},{20,24},{24,20},{28,32},{32,28... | collective-permute-start | bytes 61448 | tf_op jit(solution)/shard_map/ppermute | solution.py:389
  34.4 0.5 shard_map.91
  34.9 0.0 collective-permute-done.5.kg.kg_s1
  34.9 0.5 shard_map.93
  35.5 0.0 collective-permute-done.4.kg.kg_s0
  35.5 0.5 shard_map.92
  36.0 0.0 collective-permute-done.7.got_first
  36.0 0.0 collective-permute-done.8.got_second
  36.0 0.9 %shard_map.95 = (f32[8,1280]{1,0:T(8,128)S(1)}, f32[8,1280]{1,0:T(8,128)S(1)}) custom-call(f32[8,1280]{1,0:T(8,128)S(1)} %get-tuple-element.71.proj, f32[4,1280]{1,0:T(4,128)S(1)} %collective-permute-done.7.got_first, f32[4,1280]{1,0:T(4,128)S(1)} %collective-permute-done.8.got_second, f32[1,128]{1,0:T(1,128)S(1)} %get-tuple-element.74.gain_grad, ...), custom_call_target="tpu_custom_call" | custom-call | flops 400 | bytes 1 | tf_op jit(solution)/shard_map/pallas_call | solution.py:29
  36.9 1.2 %collective-permute-start.9 = (f32[8,1280]{1,0:T(8,128)S(1)}, f32[8,1280]{1,0:T(8,128)S(1)}, u32[]{:S(2)}, u32[]{:S(2)}) collective-permute-start(f32[8,1280]{1,0:T(8,128)S(1)} %get-tuple-element.83.mine), channel_id=1, source_target_pairs={{0,1},{1,0},{2,3},{3,2},{4,5},{5,4},{6,7},{7,6},{8,9},{9,8},{10,11... | collective-permute-start | bytes 122888 | tf_op jit(solution)/shard_map/ppermute | solution.py:398
  38.2 0.9 %collective-permute-done.9.other = f32[8,1280]{1,0:T(8,128)S(1)} collective-permute-done((f32[8,1280]{1,0:T(8,128)S(1)}, f32[8,1280]{1,0:T(8,128)S(1)}, u32[]{:S(2)}, u32[]{:S(2)}) %collective-permute-start.9) | collective-permute-done | bytes 40992 | tf_op jit(solution)/shard_map/ppermute | solution.py:398
  39.1 7.3 %collective-permute-start.12 = (f32[4,1536]{1,0:T(4,128)S(1)}, f32[4,1536]{1,0:T(4,128)S(1)}, u32[]{:S(2)}, u32[]{:S(2)}) collective-permute-start(f32[4,1536]{1,0:T(4,128)S(1)} %get-tuple-element.86), channel_id=1, source_target_pairs={{0,6},{1,255},{2,4},{3,253},{4,10},{5,3},{6,8},{7,1},{8,14},{9,7},... | collective-permute-start | bytes 73736 | tf_op jit(solution)/shard_map/ppermute | solution.py:405
  46.4 0.0 collective-permute-start.11
  46.4 1.3 %collective-permute-start.10 = (f32[4,1280]{1,0:T(4,128)S(1)}, f32[4,1280]{1,0:T(4,128)S(1)}, u32[]{:S(2)}, u32[]{:S(2)}) collective-permute-start(f32[4,1280]{1,0:T(4,128)S(1)} %get-tuple-element.84._.keep), channel_id=1, source_target_pairs={{0,2},{1,3},{2,0},{3,1},{4,6},{5,7},{6,4},{7,5},{8,10},{9,11},{10,... | collective-permute-start | bytes 61448 | tf_op jit(solution)/shard_map/ppermute | solution.py:407
  47.7 2.4 %shard_map.97._ = bf16[512,1280]{1,0:T(8,128)(2,1)} custom-call(bf16[512,256]{1,0:T(8,128)(2,1)S(1)} %get-tuple-element.60.kg.kg_k0, bf16[512,256]{1,0:T(8,128)(2,1)S(1)} %get-tuple-element.65.kg.kg_k1, bf16[512,256]{1,0:T(8,128)(2,1)S(1)} %collective-permute-done.4.kg.kg_s0, bf16[512,256]{1,0:T(8,128)(2,1)S(1)} %collective-permute-done.5.kg.kg_s1, ...), custom_call_target="tpu_custom_call" | custom-call | flops 400 | bytes 1 | tf_op jit(solution)/shard_map/pallas_call | solution.py:29
  50.1 0.5 collective-permute-done.10.other
  50.5 0.0 collective-permute-done.11.near
  50.5 0.0 collective-permute-done.12.far
  50.5 0.1 collective-permute-start.13
  50.6 1.0 %shard_map.99 = (f32[8,128]{1,0:T(8,128)S(1)}, bf16[1280,32]{1,0:T(8,128)(2,1)S(1)}, f32[1,128]{1,0:T(1,128)}) custom-call(f32[8,128]{1,0:T(8,128)S(1)} %get-tuple-element.89.gram, f32[8,1280]{1,0:T(8,128)S(1)} %get-tuple-element.90.rows, f32[1,128]{1,0:T(1,128)S(1)} %copy-done.2, f32[1,128]{1,0:T(1,128)S(1)} %get-tuple-element.91.gain_grad), custom_call_target="tpu_custom_call" | custom-call | flops 400 | bytes 1 | tf_op jit(solution)/shard_map/pallas_call | solution.py:29
  51.6 0.2 collective-permute-done.13.other
  51.8 2.7 %shard_map.100 = (f32[1280,1024]{1,0:T(8,128)}, f32[4,1024]{1,0:T(4,128)}) custom-call(f32[1280,256]{1,0:T(8,128)S(1)} %get-tuple-element.61.s_k0, f32[1280,256]{1,0:T(8,128)S(1)} %get-tuple-element.66.s_k1, f32[1280,256]{1,0:T(8,128)S(1)} %get-tuple-element.67.s_s0, f32[1280,256]{1,0:T(8,128)S(1)} %get-tuple-element.68.s_s1, ...), custom_call_target="tpu_custom_call" | custom-call | flops 400 | bytes 1 | tf_op jit(solution)/shard_map/pallas_call | solution.py:29
  (5 shorter events, 0.0 us)
Async XLA Ops:
  3.3 5.6 %collective-permute-start.1 = (bf16[512,512]{1,0:T(8,128)(2,1)S(1)}, bf16[512,512]{1,0:T(8,128)(2,1)S(1)}, u32[]{:S(2)}, u32[]{:S(2)}) collective-permute-start(bf16[512,512]{1,0:T(8,128)(2,1)S(1)} %get-tuple-element.55), channel_id=1, source_target_pairs={{0,1},{1,0},{2,3},{3,2},{4,5},{5,4},{6,7},{7,6},{8,9},{9,8},{10,11... | collective-permute-start | bytes 1572872 | tf_op jit(solution)/shard_map/ppermute | solution.py:339
  8.9 1.2 %copy-start.1 = (f32[1,4,1024]{2,1,0:T(4,128)S(1)}, f32[1,4,1024]{2,1,0:T(4,128)}, u32[]{:S(2)}) copy-start(f32[1,4,1024]{2,1,0:T(4,128)} %param.9) | copy-start | bytes 49156
  9.0 12.0 %collective-permute-start.2 = (bf16[512,256]{1,0:T(8,128)(2,1)S(1)}, bf16[512,256]{1,0:T(8,128)(2,1)S(1)}, u32[]{:S(2)}, u32[]{:S(2)}) collective-permute-start(bf16[512,256]{1,0:T(8,128)(2,1)S(1)} %get-tuple-element.58.own), channel_id=1, source_target_pairs={{0,2},{1,3},{2,0},{3,1},{4,6},{5,7},{6,4},{7,5},{8,10},{9,11},{10,... | collective-permute-start | bytes 786440 | tf_op jit(solution)/shard_map/ppermute | solution.py:348
  10.1 9.3 %collective-permute-start = (f32[4,1024]{1,0:T(4,128)S(1)}, f32[4,1024]{1,0:T(4,128)S(1)}, u32[]{:S(2)}, u32[]{:S(2)}) collective-permute-start(f32[4,1024]{1,0:T(4,128)S(1)} %bitcast.4), channel_id=1, source_target_pairs={{0,4},{4,8},{8,12},{12,16},{16,20},{20,24},{24,28},{28,32},{32,36}... | collective-permute-start | bytes 49160 | tf_op jit(solution)/shard_map/ppermute | solution.py:350
  11.4 12.7 %collective-permute-start.3 = (bf16[512,256]{1,0:T(8,128)(2,1)S(1)}, bf16[512,256]{1,0:T(8,128)(2,1)S(1)}, u32[]{:S(2)}, u32[]{:S(2)}) collective-permute-start(bf16[512,256]{1,0:T(8,128)(2,1)S(1)} %get-tuple-element.56._.own), channel_id=1, source_target_pairs={{0,2},{1,3},{2,0},{3,1},{4,6},{5,7},{6,4},{7,5},{8,10},{9,11},{10,... | collective-permute-start | bytes 786440 | tf_op jit(solution)/shard_map/ppermute | solution.py:349
  19.4 1.6 %copy-start = (bf16[512,1024]{1,0:T(8,128)(2,1)S(1)}, bf16[512,1024]{1,0:T(8,128)(2,1)}, u32[]{:S(2)}) copy-start(bf16[512,1024]{1,0:T(8,128)(2,1)} %cot.3) | copy-start | bytes 3145732
  19.4 1.6 %copy-start.2 = (f32[1,128]{1,0:T(1,128)S(1)}, f32[1,128]{1,0:T(1,128)}, u32[]{:S(2)}) copy-start(f32[1,128]{1,0:T(1,128)} %gain.5) | copy-start | bytes 1540
  24.7 1.6 %collective-permute-start.6 = (f32[8,512]{1,0:T(8,128)S(1)}, f32[8,512]{1,0:T(8,128)S(1)}, u32[]{:S(2)}, u32[]{:S(2)}) collective-permute-start(f32[8,512]{1,0:T(8,128)S(1)} %get-tuple-element.69.mine), channel_id=1, source_target_pairs={{0,1},{1,0},{2,3},{3,2},{4,5},{5,4},{6,7},{7,6},{8,9},{9,8},{10,11... | collective-permute-start | bytes 49160 | tf_op jit(solution)/shard_map/ppermute | solution.py:378
  25.5 9.9 %collective-permute-start.4 = (bf16[512,256]{1,0:T(8,128)(2,1)S(1)}, bf16[512,256]{1,0:T(8,128)(2,1)S(1)}, u32[]{:S(2)}, u32[]{:S(2)}) collective-permute-start(bf16[512,256]{1,0:T(8,128)(2,1)S(1)} %get-tuple-element.60.kg.kg_k0), channel_id=1, source_target_pairs={{0,1},{1,0},{2,3},{3,2},{4,5},{5,4},{6,7},{7,6},{8,9},{9,8},{10,11... | collective-permute-start | bytes 786440 | tf_op jit(solution)/shard_map/ppermute | solution.py:380
  25.6 9.3 %collective-permute-start.5 = (bf16[512,256]{1,0:T(8,128)(2,1)S(1)}, bf16[512,256]{1,0:T(8,128)(2,1)S(1)}, u32[]{:S(2)}, u32[]{:S(2)}) collective-permute-start(bf16[512,256]{1,0:T(8,128)(2,1)S(1)} %get-tuple-element.65.kg.kg_k1), channel_id=1, source_target_pairs={{0,1},{1,0},{2,3},{3,2},{4,5},{5,4},{6,7},{7,6},{8,9},{9,8},{10,11... | collective-permute-start | bytes 786440 | tf_op jit(solution)/shard_map/ppermute | solution.py:381
  26.7 9.3 %collective-permute-start.7 = (f32[4,1280]{1,0:T(4,128)S(1)}, f32[4,1280]{1,0:T(4,128)S(1)}, u32[]{:S(2)}, u32[]{:S(2)}) collective-permute-start(f32[4,1280]{1,0:T(4,128)S(1)} %get-tuple-element.72), channel_id=1, source_target_pairs={{0,4},{4,0},{8,12},{12,8},{16,20},{20,16},{24,28},{28,24},{32,36},... | collective-permute-start | bytes 61448 | tf_op jit(solution)/shard_map/ppermute | solution.py:388
  26.7 9.2 %collective-permute-start.8 = (f32[4,1280]{1,0:T(4,128)S(1)}, f32[4,1280]{1,0:T(4,128)S(1)}, u32[]{:S(2)}, u32[]{:S(2)}) collective-permute-start(f32[4,1280]{1,0:T(4,128)S(1)} %get-tuple-element.73), channel_id=1, source_target_pairs={{0,252},{4,8},{8,4},{12,16},{16,12},{20,24},{24,20},{28,32},{32,28... | collective-permute-start | bytes 61448 | tf_op jit(solution)/shard_map/ppermute | solution.py:389
  36.9 2.1 %collective-permute-start.9 = (f32[8,1280]{1,0:T(8,128)S(1)}, f32[8,1280]{1,0:T(8,128)S(1)}, u32[]{:S(2)}, u32[]{:S(2)}) collective-permute-start(f32[8,1280]{1,0:T(8,128)S(1)} %get-tuple-element.83.mine), channel_id=1, source_target_pairs={{0,1},{1,0},{2,3},{3,2},{4,5},{5,4},{6,7},{7,6},{8,9},{9,8},{10,11... | collective-permute-start | bytes 122888 | tf_op jit(solution)/shard_map/ppermute | solution.py:398
  39.1 11.5 %collective-permute-start.12 = (f32[4,1536]{1,0:T(4,128)S(1)}, f32[4,1536]{1,0:T(4,128)S(1)}, u32[]{:S(2)}, u32[]{:S(2)}) collective-permute-start(f32[4,1536]{1,0:T(4,128)S(1)} %get-tuple-element.86), channel_id=1, source_target_pairs={{0,6},{1,255},{2,4},{3,253},{4,10},{5,3},{6,8},{7,1},{8,14},{9,7},... | collective-permute-start | bytes 73736 | tf_op jit(solution)/shard_map/ppermute | solution.py:405
  46.4 4.1 %collective-permute-start.11 = (f32[4,1408]{1,0:T(4,128)S(1)}, f32[4,1408]{1,0:T(4,128)S(1)}, u32[]{:S(2)}, u32[]{:S(2)}) collective-permute-start(f32[4,1408]{1,0:T(4,128)S(1)} %get-tuple-element.85), channel_id=1, source_target_pairs={{0,4},{1,253},{2,6},{3,255},{4,8},{5,1},{6,10},{7,3},{8,12},{9,5},... | collective-permute-start | bytes 67592 | tf_op jit(solution)/shard_map/ppermute | solution.py:406
  46.4 4.1 %collective-permute-start.10 = (f32[4,1280]{1,0:T(4,128)S(1)}, f32[4,1280]{1,0:T(4,128)S(1)}, u32[]{:S(2)}, u32[]{:S(2)}) collective-permute-start(f32[4,1280]{1,0:T(4,128)S(1)} %get-tuple-element.84._.keep), channel_id=1, source_target_pairs={{0,2},{1,3},{2,0},{3,1},{4,6},{5,7},{6,4},{7,5},{8,10},{9,11},{10,... | collective-permute-start | bytes 61448 | tf_op jit(solution)/shard_map/ppermute | solution.py:407
  50.5 1.3 %collective-permute-start.13 = (f32[4,1024]{1,0:T(4,128)S(1)}, f32[4,1024]{1,0:T(4,128)S(1)}, u32[]{:S(2)}, u32[]{:S(2)}) collective-permute-start(f32[4,1024]{1,0:T(4,128)S(1)} %get-tuple-element.94.mine), channel_id=1, source_target_pairs={{0,1},{1,0},{2,3},{3,2},{4,5},{5,4},{6,7},{7,6},{8,9},{9,8},{10,11... | collective-permute-start | bytes 49160 | tf_op jit(solution)/shard_map/ppermute | solution.py:421

commit v6 on v5

--- a/solution.py
+++ b/solution.py
@@ -60,7 +60,7 @@
     return pl.ds(pl.multiple_of(which * (2 * wide) + i * wide, 128), wide)
 
 
-def half_in(w, to, kept, sems):
+def half_in(w, to, kept, sems, beside=()):
     half = to.shape[1]
     steps = sems.shape[0]
     k = to.shape[0] // steps
@@ -70,15 +70,19 @@
     for j in range(steps):
         at = pl.ds(j * k, k)
         copies.append(pltpu.make_async_copy(w.at[at, cols], to.at[at], sems.at[j]))
+        for copy in beside[j : j + 1]:
+            copy.start()
         copies[j].start()
     return copies
 
 
-def partial(tok_v, w_v, hi_v, copies):
+def partial(tok_v, w_v, hi_v, copies, beside=()):
     steps = len(copies)
     k = w_v.shape[0] // steps
     acc = None
     for j in range(steps):
+        for copy in beside[j : j + 1]:
+            copy.wait()
         copies[j].wait()
         at = slice(j * k, (j + 1) * k)
         hi = w_v[at].astype(BF16)
@@ -89,11 +93,14 @@
 
 
 def first_kernel(tok, w, tok_v, w_s, hi_s, part, tok_sem, w_sem):
-    tok_copy = pltpu.make_async_copy(tok, tok_v, tok_sem)
-    tok_copy.start()
-    copies = half_in(w, w_s, False, w_sem)
-    tok_copy.wait()
-    part[...] = partial(tok_v, w_s, hi_s, copies).astype(BF16)
+    steps = w_sem.shape[0]
+    k = tok.shape[1] // steps
+    tok_copies = []
+    for j in range(steps):
+        at = pl.ds(j * k, k)
+        tok_copies.append(pltpu.make_async_copy(tok.at[:, at], tok_v.at[:, at], tok_sem.at[j]))
+    copies = half_in(w, w_s, False, w_sem, tok_copies)
+    part[...] = partial(tok_v, w_s, hi_s, copies, tok_copies).astype(BF16)
 
 
 def own_kernel(tok_v, w, w_k, hi_k, own, w_sem):
@@ -274,6 +281,11 @@
     copy.wait()
 
 
+def last_blocks(depth):
+    short = depth // 20
+    return [0, short] + list(range(2 * short, depth, 4 * short)) + [depth]
+
+
 def mix_kernel(s_k0, s_k1, s_s0, s_s1, inverse, lhs, mine, other, out, new_vec, stage, vec_stage, right_side, sem, vec_sem):
     rank, width = vec_stage.shape
     depth, wide = s_k0.shape
@@ -288,15 +300,15 @@
     vec_stage[...] = nv[:rank]
     vec_copy = pltpu.make_async_copy(vec_stage, new_vec, vec_sem)
     vec_copy.start()
-    parts = sem.shape[0]
-    k = depth // parts
     copies = []
-    for p in range(parts):
-        at = slice(p * k, (p + 1) * k)
+    ends = last_blocks(depth)
+    for p, (lo, hi) in enumerate(zip(ends[:-1], ends[1:])):
+        at = slice(lo, hi)
         for s, kept, i in ((s_k0, True, 0), (s_k1, True, 1), (s_s0, False, 0), (s_s1, False, 1)):
             cols = chunk_at(kept, i, wide)
             stage[at, cols] = s[at] - dot(lhs[at], right_side[:, cols])
-        copies.append(pltpu.make_async_copy(stage.at[pl.ds(p * k, k)], out.at[pl.ds(p * k, k)], sem.at[p]))
+        rows_out = pl.ds(lo, hi - lo)
+        copies.append(pltpu.make_async_copy(stage.at[rows_out], out.at[rows_out], sem.at[p]))
         copies[p].start()
     for copy in copies:
         copy.wait()
@@ -333,7 +345,7 @@
         first_kernel,
         (tokens, weight),
         [((rows, depth), BF16), ((depth, half), F32), ((depth, half), BF16), ((rows, half), BF16)],
-        [dma, dma((steps,))],
+        [dma((steps,)), dma((steps,))],
         spaces=(False, False),
     )
     from_core = lax.ppermute(part, "tp", core)
@@ -426,7 +438,7 @@
         [pltpu.VMEM(gain.shape, F32), dma],
         out_spaces=(True, True, False),
     )
-    parts = 10
+    parts = len(last_blocks(depth)) - 1
     new_weights, new_vec = call(
         mix_kernel,
         (s_k0, s_k1, s_s0, s_s1, inverse, lhs, mine, other),

time: 54.9 us -> 54.7 us (level)
  no operation moved by 1% of the time
where the time goes in v6:
time: 54.7 us; the launch traced here: 54.6 us
  starting transfers between devices  25.4 us (46%)
  Pallas kernels  17 us (31%)
  waiting for transfers between devices  11.2 us (20%)
  between operations  0.97 us (2%)
    pallas_call x17, Pallas kernels, call(): pl.pallas_call(body, out_shape=[pltpu.VMEM(shape, dtype) if inside else p...  17 us
    ppermute x1, starting transfers between devices, shards(): got_second = lax.ppermute(second, 'loop', odd_edges)  7.67 us
    ppermute x1, waiting for transfers between devices, shards(): left_vec = lax.ppermute(vec, 'loop', right)  7.32 us
    ppermute x1, starting transfers between devices, shards(): far = lax.ppermute(far, everyone, along_far)  7.31 us
    ppermute x1, starting transfers between devices, shards(): from_core = lax.ppermute(part, 'tp', core)  3.33 us
    ppermute x1, waiting for transfers between devices, shards(): from_chip1 = lax.ppermute(chip1, 'tp', chip)  2.03 us
    ppermute x1, starting transfers between devices, shards(): left_vec = lax.ppermute(vec, 'loop', right)  1.3 us
    ppermute x1, starting transfers between devices, shards(): other_chip = lax.ppermute(keep, 'tp', chip)  1.27 us
  transfers between devices with their start and end apart: 14, of which 6 were waited for; matrix products, arithmetic and copies ran while one was open for 0% of the time, Pallas kernels for 18%

profile of v6, /device:TPU:1, one launch (start us, length us, event | category | flops | bytes accessed | tf_op | source)
XLA Modules:
  0.0 54.6 jit_solution(12418685860617804222)
XLA Ops:
  0.6 2.5 %shard_map.84 = (bf16[512,1280]{1,0:T(8,128)(2,1)S(1)}, f32[1280,512]{1,0:T(8,128)S(1)}, bf16[1280,512]{1,0:T(8,128)(2,1)S(1)}, bf16[512,512]{1,0:T(8,128)(2,1)S(1)}) custom-call(bf16[512,1280]{1,0:T(8,128)(2,1)} %tok.1, f32[1280,1024]{1,0:T(8,128)} %bitcast.8), custom_call_target="tpu_custom_call" | custom-call | flops 400 | bytes 1 | tf_op jit(solution)/shard_map/pallas_call | solution.py:29
  3.2 3.3 %collective-permute-start.1 = (bf16[512,512]{1,0:T(8,128)(2,1)S(1)}, bf16[512,512]{1,0:T(8,128)(2,1)S(1)}, u32[]{:S(2)}, u32[]{:S(2)}) collective-permute-start(bf16[512,512]{1,0:T(8,128)(2,1)S(1)} %get-tuple-element.55), channel_id=1, source_target_pairs={{0,1},{1,0},{2,3},{3,2},{4,5},{5,4},{6,7},{7,6},{8,9},{9,8},{10,11... | collective-permute-start | bytes 1572872 | tf_op jit(solution)/shard_map/ppermute | solution.py:351
  6.5 2.2 %shard_map.85 = (f32[1280,512]{1,0:T(8,128)S(1)}, bf16[1280,512]{1,0:T(8,128)(2,1)S(1)}, f32[512,512]{1,0:T(8,128)S(1)}) custom-call(bf16[512,1280]{1,0:T(8,128)(2,1)S(1)} %get-tuple-element.51.tok_v, f32[1280,1024]{1,0:T(8,128)} %bitcast.9), custom_call_target="tpu_custom_call" | custom-call | flops 400 | bytes 1 | tf_op jit(solution)/shard_map/pallas_call | solution.py:29
  8.8 0.0 copy-start.1
  8.8 0.0 collective-permute-done.1.got
  8.8 0.1 shard_map.86
  8.9 1.1 %collective-permute-start.2 = (bf16[512,256]{1,0:T(8,128)(2,1)S(1)}, bf16[512,256]{1,0:T(8,128)(2,1)S(1)}, u32[]{:S(2)}, u32[]{:S(2)}) collective-permute-start(bf16[512,256]{1,0:T(8,128)(2,1)S(1)} %get-tuple-element.58.own), channel_id=1, source_target_pairs={{0,2},{1,3},{2,0},{3,1},{4,6},{5,7},{6,4},{7,5},{8,10},{9,11},{10,... | collective-permute-start | bytes 786440 | tf_op jit(solution)/shard_map/ppermute | solution.py:360
  10.0 0.0 copy-done.1
  10.0 1.3 %collective-permute-start = (f32[4,1024]{1,0:T(4,128)S(1)}, f32[4,1024]{1,0:T(4,128)S(1)}, u32[]{:S(2)}, u32[]{:S(2)}) collective-permute-start(f32[4,1024]{1,0:T(4,128)S(1)} %bitcast.4), channel_id=1, source_target_pairs={{0,4},{4,8},{8,12},{12,16},{16,20},{20,24},{24,28},{28,32},{32,36}... | collective-permute-start | bytes 49160 | tf_op jit(solution)/shard_map/ppermute | solution.py:362
  11.3 0.7 %collective-permute-start.3 = (bf16[512,256]{1,0:T(8,128)(2,1)S(1)}, bf16[512,256]{1,0:T(8,128)(2,1)S(1)}, u32[]{:S(2)}, u32[]{:S(2)}) collective-permute-start(bf16[512,256]{1,0:T(8,128)(2,1)S(1)} %get-tuple-element.56._.own), channel_id=1, source_target_pairs={{0,2},{1,3},{2,0},{3,1},{4,6},{5,7},{6,4},{7,5},{8,10},{9,11},{10,... | collective-permute-start | bytes 786440 | tf_op jit(solution)/shard_map/ppermute | solution.py:361
  12.0 7.3 %collective-permute-done.left_vec = f32[4,1024]{1,0:T(4,128)S(1)} collective-permute-done((f32[4,1024]{1,0:T(4,128)S(1)}, f32[4,1024]{1,0:T(4,128)S(1)}, u32[]{:S(2)}, u32[]{:S(2)}) %collective-permute-start) | collective-permute-done | bytes 16416 | tf_op jit(solution)/shard_map/ppermute | solution.py:362
  19.3 0.0 copy-start
  19.3 1.6 %shard_map.87 = (f32[8,1280]{1,0:T(8,128)S(1)}, bf16[1280,512]{1,0:T(8,128)(2,1)S(1)}) custom-call(bf16[512,1280]{1,0:T(8,128)(2,1)S(1)} %get-tuple-element.51.tok_v, f32[1280,512]{1,0:T(8,128)S(1)} %get-tuple-element.52.w_k.w, f32[1280,512]{1,0:T(8,128)S(1)} %get-tuple-element.53.w_s.w, f32[4,1024]{1,0:T(4,128)S(1)} %bitcast.5, ...), custom_call_target="tpu_custom_call" | custom-call | flops 400 | bytes 1 | tf_op jit(solution)/shard_map/pallas_call | solution.py:29
  20.9 0.0 collective-permute-done.2.got
  20.9 0.0 copy-done
  20.9 0.0 copy-done.2
  20.9 0.6 %shard_map.88 = (bf16[512,256]{1,0:T(8,128)(2,1)S(1)}, f32[8,512]{1,0:T(8,128)S(1)}, f32[1,128]{1,0:T(1,128)S(1)}, f32[8,1280]{1,0:T(8,128)S(1)}) custom-call(bf16[512,256]{1,0:T(8,128)(2,1)S(1)} %get-tuple-element.58.own, bf16[512,256]{1,0:T(8,128)(2,1)S(1)} %collective-permute-done.2.got, ...), custom_call_target="tpu_custom_call", output_to_operand_aliasing={{3}: (8, {})} | custom-call | flops 16777216000 | bytes 41943040 | tf_op jit(solution)/shard_map/pallas_call | solution.py:29
  21.5 0.5 shard_map.89
  22.0 2.0 %collective-permute-done.3.got = bf16[512,256]{1,0:T(8,128)(2,1)S(1)} collective-permute-done((bf16[512,256]{1,0:T(8,128)(2,1)S(1)}, bf16[512,256]{1,0:T(8,128)(2,1)S(1)}, u32[]{:S(2)}, u32[]{:S(2)}) %collective-permute-start.3) | collective-permute-done | bytes 262176 | tf_op jit(solution)/shard_map/ppermute | solution.py:361
  24.0 0.6 %shard_map.90 = (bf16[512,256]{1,0:T(8,128)(2,1)S(1)}, f32[8,512]{1,0:T(8,128)S(1)}, f32[1,128]{1,0:T(1,128)S(1)}, bf16[1280,256]{1,0:T(8,128)(2,1)S(1)}) custom-call(bf16[512,256]{1,0:T(8,128)(2,1)S(1)} %get-tuple-element.56._.own, bf16[512,256]{1,0:T(8,128)(2,1)S(1)} %collective-permute-done.3.got, ...), custom_call_target="tpu_custom_call", output_to_operand_aliasing={{3}: (8, {})} | custom-call | flops 400 | bytes 1 | tf_op jit(solution)/shard_map/pallas_call | solution.py:29
  24.6 0.8 %collective-permute-start.6 = (f32[8,512]{1,0:T(8,128)S(1)}, f32[8,512]{1,0:T(8,128)S(1)}, u32[]{:S(2)}, u32[]{:S(2)}) collective-permute-start(f32[8,512]{1,0:T(8,128)S(1)} %get-tuple-element.69.mine), channel_id=1, source_target_pairs={{0,1},{1,0},{2,3},{3,2},{4,5},{5,4},{6,7},{7,6},{8,9},{9,8},{10,11... | collective-permute-start | bytes 49160 | tf_op jit(solution)/shard_map/ppermute | solution.py:390
  25.4 0.1 collective-permute-start.4
  25.5 0.4 collective-permute-start.5
  25.9 0.3 collective-permute-done.6.other
  26.3 0.3 shard_map.94
  26.6 0.1 collective-permute-start.7
  26.6 7.7 %collective-permute-start.8 = (f32[4,1280]{1,0:T(4,128)S(1)}, f32[4,1280]{1,0:T(4,128)S(1)}, u32[]{:S(2)}, u32[]{:S(2)}) collective-permute-start(f32[4,1280]{1,0:T(4,128)S(1)} %get-tuple-element.73), channel_id=1, source_target_pairs={{0,252},{4,8},{8,4},{12,16},{16,12},{20,24},{24,20},{28,32},{32,28... | collective-permute-start | bytes 61448 | tf_op jit(solution)/shard_map/ppermute | solution.py:401
  34.3 0.5 shard_map.91
  34.8 0.0 collective-permute-done.5.kg.kg_s1
  34.8 0.5 shard_map.93
  35.3 0.0 collective-permute-done.4.kg.kg_s0
  35.4 0.5 shard_map.92
  35.9 0.0 collective-permute-done.7.got_first
  35.9 0.0 collective-permute-done.8.got_second
  35.9 0.9 %shard_map.95 = (f32[8,1280]{1,0:T(8,128)S(1)}, f32[8,1280]{1,0:T(8,128)S(1)}) custom-call(f32[8,1280]{1,0:T(8,128)S(1)} %get-tuple-element.71.proj, f32[4,1280]{1,0:T(4,128)S(1)} %collective-permute-done.7.got_first, f32[4,1280]{1,0:T(4,128)S(1)} %collective-permute-done.8.got_second, f32[1,128]{1,0:T(1,128)S(1)} %get-tuple-element.74.gain_grad, ...), custom_call_target="tpu_custom_call" | custom-call | flops 400 | bytes 1 | tf_op jit(solution)/shard_map/pallas_call | solution.py:29
  36.8 1.2 %collective-permute-start.9 = (f32[8,1280]{1,0:T(8,128)S(1)}, f32[8,1280]{1,0:T(8,128)S(1)}, u32[]{:S(2)}, u32[]{:S(2)}) collective-permute-start(f32[8,1280]{1,0:T(8,128)S(1)} %get-tuple-element.83.mine), channel_id=1, source_target_pairs={{0,1},{1,0},{2,3},{3,2},{4,5},{5,4},{6,7},{7,6},{8,9},{9,8},{10,11... | collective-permute-start | bytes 122888 | tf_op jit(solution)/shard_map/ppermute | solution.py:410
  38.1 0.9 %collective-permute-done.9.other = f32[8,1280]{1,0:T(8,128)S(1)} collective-permute-done((f32[8,1280]{1,0:T(8,128)S(1)}, f32[8,1280]{1,0:T(8,128)S(1)}, u32[]{:S(2)}, u32[]{:S(2)}) %collective-permute-start.9) | collective-permute-done | bytes 40992 | tf_op jit(solution)/shard_map/ppermute | solution.py:410
  39.0 7.3 %collective-permute-start.12 = (f32[4,1536]{1,0:T(4,128)S(1)}, f32[4,1536]{1,0:T(4,128)S(1)}, u32[]{:S(2)}, u32[]{:S(2)}) collective-permute-start(f32[4,1536]{1,0:T(4,128)S(1)} %get-tuple-element.86), channel_id=1, source_target_pairs={{0,6},{1,255},{2,4},{3,253},{4,10},{5,3},{6,8},{7,1},{8,14},{9,7},... | collective-permute-start | bytes 73736 | tf_op jit(solution)/shard_map/ppermute | solution.py:417
  46.3 0.0 collective-permute-start.11
  46.3 1.3 %collective-permute-start.10 = (f32[4,1280]{1,0:T(4,128)S(1)}, f32[4,1280]{1,0:T(4,128)S(1)}, u32[]{:S(2)}, u32[]{:S(2)}) collective-permute-start(f32[4,1280]{1,0:T(4,128)S(1)} %get-tuple-element.84._.keep), channel_id=1, source_target_pairs={{0,2},{1,3},{2,0},{3,1},{4,6},{5,7},{6,4},{7,5},{8,10},{9,11},{10,... | collective-permute-start | bytes 61448 | tf_op jit(solution)/shard_map/ppermute | solution.py:419
  47.5 2.4 %shard_map.97._ = bf16[512,1280]{1,0:T(8,128)(2,1)} custom-call(bf16[512,256]{1,0:T(8,128)(2,1)S(1)} %get-tuple-element.60.kg.kg_k0, bf16[512,256]{1,0:T(8,128)(2,1)S(1)} %get-tuple-element.65.kg.kg_k1, bf16[512,256]{1,0:T(8,128)(2,1)S(1)} %collective-permute-done.4.kg.kg_s0, bf16[512,256]{1,0:T(8,128)(2,1)S(1)} %collective-permute-done.5.kg.kg_s1, ...), custom_call_target="tpu_custom_call" | custom-call | flops 400 | bytes 1 | tf_op jit(solution)/shard_map/pallas_call | solution.py:29
  49.9 0.5 collective-permute-done.10.other
  50.4 0.0 collective-permute-done.11.near
  50.4 0.0 collective-permute-done.12.far
  50.4 0.1 collective-permute-start.13
  50.5 1.0 %shard_map.99 = (f32[8,128]{1,0:T(8,128)S(1)}, bf16[1280,32]{1,0:T(8,128)(2,1)S(1)}, f32[1,128]{1,0:T(1,128)}) custom-call(f32[8,128]{1,0:T(8,128)S(1)} %get-tuple-element.89.gram, f32[8,1280]{1,0:T(8,128)S(1)} %get-tuple-element.90.rows, f32[1,128]{1,0:T(1,128)S(1)} %copy-done.2, f32[1,128]{1,0:T(1,128)S(1)} %get-tuple-element.91.gain_grad), custom_call_target="tpu_custom_call" | custom-call | flops 400 | bytes 1 | tf_op jit(solution)/shard_map/pallas_call | solution.py:29
  51.5 0.2 collective-permute-done.13.other
  51.7 2.7 %shard_map.100 = (f32[1280,1024]{1,0:T(8,128)}, f32[4,1024]{1,0:T(4,128)}) custom-call(f32[1280,256]{1,0:T(8,128)S(1)} %get-tuple-element.61.s_k0, f32[1280,256]{1,0:T(8,128)S(1)} %get-tuple-element.66.s_k1, f32[1280,256]{1,0:T(8,128)S(1)} %get-tuple-element.67.s_s0, f32[1280,256]{1,0:T(8,128)S(1)} %get-tuple-element.68.s_s1, ...), custom_call_target="tpu_custom_call" | custom-call | flops 400 | bytes 1 | tf_op jit(solution)/shard_map/pallas_call | solution.py:29
  (5 shorter events, 0.0 us)
Async XLA Ops:
  3.2 5.6 %collective-permute-start.1 = (bf16[512,512]{1,0:T(8,128)(2,1)S(1)}, bf16[512,512]{1,0:T(8,128)(2,1)S(1)}, u32[]{:S(2)}, u32[]{:S(2)}) collective-permute-start(bf16[512,512]{1,0:T(8,128)(2,1)S(1)} %get-tuple-element.55), channel_id=1, source_target_pairs={{0,1},{1,0},{2,3},{3,2},{4,5},{5,4},{6,7},{7,6},{8,9},{9,8},{10,11... | collective-permute-start | bytes 1572872 | tf_op jit(solution)/shard_map/ppermute | solution.py:351
  8.8 1.3 %copy-start.1 = (f32[1,4,1024]{2,1,0:T(4,128)S(1)}, f32[1,4,1024]{2,1,0:T(4,128)}, u32[]{:S(2)}) copy-start(f32[1,4,1024]{2,1,0:T(4,128)} %param.9) | copy-start | bytes 49156
  8.9 12.0 %collective-permute-start.2 = (bf16[512,256]{1,0:T(8,128)(2,1)S(1)}, bf16[512,256]{1,0:T(8,128)(2,1)S(1)}, u32[]{:S(2)}, u32[]{:S(2)}) collective-permute-start(bf16[512,256]{1,0:T(8,128)(2,1)S(1)} %get-tuple-element.58.own), channel_id=1, source_target_pairs={{0,2},{1,3},{2,0},{3,1},{4,6},{5,7},{6,4},{7,5},{8,10},{9,11},{10,... | collective-permute-start | bytes 786440 | tf_op jit(solution)/shard_map/ppermute | solution.py:360
  10.0 9.3 %collective-permute-start = (f32[4,1024]{1,0:T(4,128)S(1)}, f32[4,1024]{1,0:T(4,128)S(1)}, u32[]{:S(2)}, u32[]{:S(2)}) collective-permute-start(f32[4,1024]{1,0:T(4,128)S(1)} %bitcast.4), channel_id=1, source_target_pairs={{0,4},{4,8},{8,12},{12,16},{16,20},{20,24},{24,28},{28,32},{32,36}... | collective-permute-start | bytes 49160 | tf_op jit(solution)/shard_map/ppermute | solution.py:362
  11.3 12.7 %collective-permute-start.3 = (bf16[512,256]{1,0:T(8,128)(2,1)S(1)}, bf16[512,256]{1,0:T(8,128)(2,1)S(1)}, u32[]{:S(2)}, u32[]{:S(2)}) collective-permute-start(bf16[512,256]{1,0:T(8,128)(2,1)S(1)} %get-tuple-element.56._.own), channel_id=1, source_target_pairs={{0,2},{1,3},{2,0},{3,1},{4,6},{5,7},{6,4},{7,5},{8,10},{9,11},{10,... | collective-permute-start | bytes 786440 | tf_op jit(solution)/shard_map/ppermute | solution.py:361
  19.3 1.6 %copy-start = (bf16[512,1024]{1,0:T(8,128)(2,1)S(1)}, bf16[512,1024]{1,0:T(8,128)(2,1)}, u32[]{:S(2)}) copy-start(bf16[512,1024]{1,0:T(8,128)(2,1)} %cot.3) | copy-start | bytes 3145732
  19.3 1.6 %copy-start.2 = (f32[1,128]{1,0:T(1,128)S(1)}, f32[1,128]{1,0:T(1,128)}, u32[]{:S(2)}) copy-start(f32[1,128]{1,0:T(1,128)} %gain.5) | copy-start | bytes 1540
  24.6 1.6 %collective-permute-start.6 = (f32[8,512]{1,0:T(8,128)S(1)}, f32[8,512]{1,0:T(8,128)S(1)}, u32[]{:S(2)}, u32[]{:S(2)}) collective-permute-start(f32[8,512]{1,0:T(8,128)S(1)} %get-tuple-element.69.mine), channel_id=1, source_target_pairs={{0,1},{1,0},{2,3},{3,2},{4,5},{5,4},{6,7},{7,6},{8,9},{9,8},{10,11... | collective-permute-start | bytes 49160 | tf_op jit(solution)/shard_map/ppermute | solution.py:390
  25.4 9.9 %collective-permute-start.4 = (bf16[512,256]{1,0:T(8,128)(2,1)S(1)}, bf16[512,256]{1,0:T(8,128)(2,1)S(1)}, u32[]{:S(2)}, u32[]{:S(2)}) collective-permute-start(bf16[512,256]{1,0:T(8,128)(2,1)S(1)} %get-tuple-element.60.kg.kg_k0), channel_id=1, source_target_pairs={{0,1},{1,0},{2,3},{3,2},{4,5},{5,4},{6,7},{7,6},{8,9},{9,8},{10,11... | collective-permute-start | bytes 786440 | tf_op jit(solution)/shard_map/ppermute | solution.py:392
  25.5 9.3 %collective-permute-start.5 = (bf16[512,256]{1,0:T(8,128)(2,1)S(1)}, bf16[512,256]{1,0:T(8,128)(2,1)S(1)}, u32[]{:S(2)}, u32[]{:S(2)}) collective-permute-start(bf16[512,256]{1,0:T(8,128)(2,1)S(1)} %get-tuple-element.65.kg.kg_k1), channel_id=1, source_target_pairs={{0,1},{1,0},{2,3},{3,2},{4,5},{5,4},{6,7},{7,6},{8,9},{9,8},{10,11... | collective-permute-start | bytes 786440 | tf_op jit(solution)/shard_map/ppermute | solution.py:393
  26.6 9.3 %collective-permute-start.7 = (f32[4,1280]{1,0:T(4,128)S(1)}, f32[4,1280]{1,0:T(4,128)S(1)}, u32[]{:S(2)}, u32[]{:S(2)}) collective-permute-start(f32[4,1280]{1,0:T(4,128)S(1)} %get-tuple-element.72), channel_id=1, source_target_pairs={{0,4},{4,0},{8,12},{12,8},{16,20},{20,16},{24,28},{28,24},{32,36},... | collective-permute-start | bytes 61448 | tf_op jit(solution)/shard_map/ppermute | solution.py:400
  26.6 9.2 %collective-permute-start.8 = (f32[4,1280]{1,0:T(4,128)S(1)}, f32[4,1280]{1,0:T(4,128)S(1)}, u32[]{:S(2)}, u32[]{:S(2)}) collective-permute-start(f32[4,1280]{1,0:T(4,128)S(1)} %get-tuple-element.73), channel_id=1, source_target_pairs={{0,252},{4,8},{8,4},{12,16},{16,12},{20,24},{24,20},{28,32},{32,28... | collective-permute-start | bytes 61448 | tf_op jit(solution)/shard_map/ppermute | solution.py:401
  36.8 2.1 %collective-permute-start.9 = (f32[8,1280]{1,0:T(8,128)S(1)}, f32[8,1280]{1,0:T(8,128)S(1)}, u32[]{:S(2)}, u32[]{:S(2)}) collective-permute-start(f32[8,1280]{1,0:T(8,128)S(1)} %get-tuple-element.83.mine), channel_id=1, source_target_pairs={{0,1},{1,0},{2,3},{3,2},{4,5},{5,4},{6,7},{7,6},{8,9},{9,8},{10,11... | collective-permute-start | bytes 122888 | tf_op jit(solution)/shard_map/ppermute | solution.py:410
  39.0 11.5 %collective-permute-start.12 = (f32[4,1536]{1,0:T(4,128)S(1)}, f32[4,1536]{1,0:T(4,128)S(1)}, u32[]{:S(2)}, u32[]{:S(2)}) collective-permute-start(f32[4,1536]{1,0:T(4,128)S(1)} %get-tuple-element.86), channel_id=1, source_target_pairs={{0,6},{1,255},{2,4},{3,253},{4,10},{5,3},{6,8},{7,1},{8,14},{9,7},... | collective-permute-start | bytes 73736 | tf_op jit(solution)/shard_map/ppermute | solution.py:417
  46.3 4.1 %collective-permute-start.11 = (f32[4,1408]{1,0:T(4,128)S(1)}, f32[4,1408]{1,0:T(4,128)S(1)}, u32[]{:S(2)}, u32[]{:S(2)}) collective-permute-start(f32[4,1408]{1,0:T(4,128)S(1)} %get-tuple-element.85), channel_id=1, source_target_pairs={{0,4},{1,253},{2,6},{3,255},{4,8},{5,1},{6,10},{7,3},{8,12},{9,5},... | collective-permute-start | bytes 67592 | tf_op jit(solution)/shard_map/ppermute | solution.py:418
  46.3 4.1 %collective-permute-start.10 = (f32[4,1280]{1,0:T(4,128)S(1)}, f32[4,1280]{1,0:T(4,128)S(1)}, u32[]{:S(2)}, u32[]{:S(2)}) collective-permute-start(f32[4,1280]{1,0:T(4,128)S(1)} %get-tuple-element.84._.keep), channel_id=1, source_target_pairs={{0,2},{1,3},{2,0},{3,1},{4,6},{5,7},{6,4},{7,5},{8,10},{9,11},{10,... | collective-permute-start | bytes 61448 | tf_op jit(solution)/shard_map/ppermute | solution.py:419
  50.4 1.3 %collective-permute-start.13 = (f32[4,1024]{1,0:T(4,128)S(1)}, f32[4,1024]{1,0:T(4,128)S(1)}, u32[]{:S(2)}, u32[]{:S(2)}) collective-permute-start(f32[4,1024]{1,0:T(4,128)S(1)} %get-tuple-element.94.mine), channel_id=1, source_target_pairs={{0,1},{1,0},{2,3},{3,2},{4,5},{5,4},{6,7},{7,6},{8,9},{9,8},{10,11... | collective-permute-start | bytes 49160 | tf_op jit(solution)/shard_map/ppermute | solution.py:433
